TPU v7x, 32 devices: a whole 2x2x4 slice. The times are simulated.
32 devices in a mesh: section: 2 (over y), dp: 4 (over x, core), shard: 4 (over z).
Axes of the slice: x: 2, y: 2, z: 4, core: 2. Of those that a mesh axis runs over, the one named last changes fastest.
Arguments:
- features: bfloat16 [2, 512, 6144], P('section', ('dp', 'shard')), may hold values from -6 to 6
- delayed_error: bfloat16 [2, 512, 6144], P('section', ('dp', 'shard')), may hold values from -6 to 6
- ln_gain: float32 [2, 6144], P('section'), may hold values from 0.25 to 1.75
- w_in: bfloat16 [2, 6144, 12288], P('section', None, 'shard'), may hold values from -0.078125 to 0.078125
- w_out: bfloat16 [2, 12288, 6144], P('section', 'shard'), may hold values from -0.0546875 to 0.0546875
Outputs:
- passed_error: bfloat16 [2, 512, 6144], P('section', ('dp', 'shard'))
- gain_grad: float32 [2, 6144], P('section')
- w_in_grad: bfloat16 [2, 6144, 12288], P('section', 'dp', 'shard')
- w_out_grad: bfloat16 [2, 12288, 6144], P('section', 'shard', 'dp')
All inputs are finite; a program needn't handle non-finite values.
Results may differ from a plain program's by a relative error of at most 0.013.
Values may be sent and summed in bfloat16 or wider, within the bound.
No kernel may reach another device: no remote copies, remote signals or barrier semaphores. Data moves between devices by JAX's collectives and lax.ppermute only.
A program may use at most 256 MiB of HBM per device.

v0:
```python
import jax
import jax.numpy as jnp
from jax import lax
from jax.sharding import PartitionSpec as P

SQRT_HALF = 0.7071067811865476
INV_ROOT_TWO_PI = 0.3989422804014327
EPSILON = 1e-06


def shifted(block, axis, distance):
    devices = range(lax.axis_size(axis))
    route = [((i - distance) % len(devices), i) for i in devices]
    return lax.ppermute(block, axis, route)


def rounded(values):
    return lax.optimization_barrier(values.astype(jnp.bfloat16)).astype(jnp.float32)


def per_device(features, delayed_error, ln_gain, w_in, w_out):
    tokens_here = features[0]
    errors = delayed_error[0]
    scale = ln_gain[0]
    in_block = w_in[0]
    out_block = w_out[0]
    values = tokens_here.astype(jnp.float32)
    average = jnp.mean(values, -1, keepdims=True)
    centred = values - average
    variance = jnp.mean(centred * centred, -1, keepdims=True)
    inverse = lax.rsqrt(variance + EPSILON)
    centred = centred * inverse
    normed = (centred * scale).astype(jnp.bfloat16)
    normed_group, error_group = (
        lax.all_gather(normed, "shard", axis=0, tiled=True),
        lax.all_gather(errors, "shard", axis=0, tiled=True),
    )
    pre = jnp.dot(normed_group, in_block, preferred_element_type=jnp.float32)
    normal_cdf = 0.5 * (1.0 + jax.scipy.special.erf(pre * SQRT_HALF))
    density = INV_ROOT_TWO_PI * jnp.exp(-0.5 * pre * pre)
    active = (pre * normal_cdf).astype(jnp.bfloat16)
    back_act = jnp.einsum("td,fd->tf", error_group, out_block, preferred_element_type=jnp.float32)
    pre_error = (back_act * (normal_cdf + pre * density)).astype(jnp.bfloat16)
    norm_error = lax.psum_scatter(
        jnp.einsum("tf,df->td", pre_error, in_block, preferred_element_type=jnp.float32).astype(
            jnp.bfloat16
        ),
        "shard",
        scatter_dimension=0,
        tiled=True,
    ).astype(jnp.float32)
    scaled = norm_error * scale
    corrected = inverse * (
        scaled
        - jnp.mean(scaled, -1, keepdims=True)
        - centred * jnp.mean(scaled * centred, -1, keepdims=True)
    )
    own_error = (errors.astype(jnp.float32) + corrected).astype(jnp.bfloat16)
    gain_grad = lax.psum(jnp.sum(norm_error * centred, 0), ("dp", "shard"))
    passed = shifted(own_error, "section", -1)
    group_rows = normed_group.shape[0]
    column_width = normed_group.shape[1] // lax.axis_size("dp")
    column_first = lax.axis_index("dp") * column_width
    hidden_width = pre_error.shape[1]
    piece_normed = lax.all_gather(normed_group, "dp", axis=0, tiled=True)
    piece_pre = lax.all_gather(pre_error, "dp", axis=0, tiled=True)
    piece_active = lax.all_gather(active, "dp", axis=0, tiled=True)
    piece_error = lax.all_gather(error_group, "dp", axis=0, tiled=True)
    groups = piece_normed.shape[0] // group_rows
    piece_normed = lax.dynamic_slice_in_dim(piece_normed, column_first, column_width, 1)
    piece_error = lax.dynamic_slice_in_dim(piece_error, column_first, column_width, 1)
    piece_normed = piece_normed.reshape(groups, group_rows, column_width)
    piece_pre = piece_pre.reshape(groups, group_rows, hidden_width)
    piece_active = piece_active.reshape(groups, group_rows, hidden_width)
    piece_error = piece_error.reshape(groups, group_rows, column_width)
    in_terms = jnp.einsum(
        "kta,ktf->kaf", piece_normed, piece_pre, preferred_element_type=jnp.float32
    )
    out_terms = jnp.einsum(
        "ktf,kta->kfa", piece_active, piece_error, preferred_element_type=jnp.float32
    )
    in_total = jnp.sum(rounded(in_terms), 0)
    out_total = jnp.sum(rounded(out_terms), 0)
    return (
        passed[None],
        gain_grad[None],
        in_total.astype(jnp.bfloat16)[None],
        out_total.astype(jnp.bfloat16)[None],
    )


def solution(mesh):
    return jax.shard_map(
        per_device,
        mesh=mesh,
        in_specs=(
            P("section", ("dp", "shard"), None),
            P("section", ("dp", "shard"), None),
            P("section", None),
            P("section", None, "shard"),
            P("section", "shard", None),
        ),
        out_specs=(
            P("section", ("dp", "shard"), None),
            P("section", None),
            P("section", "dp", "shard"),
            P("section", "shard", "dp"),
        ),
        check_vma=False,
    )
```

profile of v0, /device:TPU:0, one launch (start us, length us, event | category | flops | bytes accessed | tf_op | source)
XLA Modules:
  0.0 378.9 jit_solution(8763108392371671483)
XLA Ops:
  7.2 0.0 all-gather.9.cloned.1.call-start
  7.2 1.2 convert_reduce_fusion
  8.4 1.3 fusion.33
  9.7 1.9 fusion.28
  11.6 0.0 all-gather.17.cloned.1.call-start
  11.7 0.7 all-gather.17.cloned.1.call-update
  12.4 0.0 reduce-scatter.2.cloned.1.call-start
  12.4 39.1 %all-gather.9.cloned.1.call-done = bf16[128,6144]{1,0:T(8,128)(2,1)} async-done(((bf16[32,6144]{1,0:T(8,128)(2,1)}), bf16[128,6144]{1,0:T(8,128)(2,1)}) %all-gather.9.cloned.1.call-update) | async-done | bytes 1572880 | tf_op jit(solution)/shard_map/all_gather | solution.py:35
  51.6 16.2 %multiply_convert_fusion = (bf16[128,3072]{1,0:T(8,128)(2,1)}, f32[128,3072]{1,0:T(8,128)S(1)}) fusion(bf16[128,6144]{1,0:T(8,128)(2,1)} %all-gather.9.cloned.1.call-done, bf16[1,6144,3072]{2,1,0:T(8,128)(2,1)} %param.8), kind=kOutput, calls=%fused_computation.17 | convolution fusion | flops 4833804288 | bytes 41680896 | tf_op jit(solution)/shard_map/dot_general | solution.py:38
  67.8 21.3 %all-gather.17.cloned.1.call-done = bf16[1,128,6144]{2,1,0:T(8,128)(2,1)} async-done(((bf16[1,32,6144]{2,1,0:T(8,128)(2,1)}), bf16[1,128,6144]{2,1,0:T(8,128)(2,1)}) %all-gather.17.cloned.1.call-update) | async-done | bytes 1572880 | tf_op jit(solution)/shard_map/all_gather | solution.py:36
  89.1 18.2 %fusion.12 = bf16[128,3072]{1,0:T(8,128)(2,1)S(1)} fusion(bf16[1,3072,6144]{2,1,0:T(8,128)(2,1)} %param.9, f32[128,3072]{1,0:T(8,128)S(1)} %get-tuple-element.8, bf16[1,128,6144]{2,1,0:T(8,128)(2,1)} %all-gather.17.cloned.1.call-done), kind=kOutput, calls=%fused_computation.10 | convolution fusion | flops 4835770368 | bytes 41680896 | tf_op jit(solution)/shard_map/td,fd->tf/dot_general | solution.py:42
  107.3 19.3 %fusion.6 = bf16[128,6144]{1,0:T(8,128)(2,1)} fusion(bf16[128,3072]{1,0:T(8,128)(2,1)S(1)} %fusion.12, bf16[1,6144,3072]{2,1,0:T(8,128)(2,1)} %param.8), kind=kOutput, calls=%fused_computation.8 | convolution fusion | flops 4832624640 | bytes 40108032 | tf_op jit(solution)/shard_map/tf,df->td/dot_general | solution.py:45
  126.6 0.0 all-gather.11.cloned.1.call-start
  126.6 0.5 all-gather.11.cloned.1.call-update
  127.2 0.5 all-gather.13.cloned.1.call-update
  127.8 0.5 all-gather.19.cloned.1.call-update
  128.4 0.7 all-gather.15.cloned.1.call-update
  129.1 31.8 %reduce-scatter.2.cloned.1.call-done = bf16[32,6144]{1,0:T(8,128)(2,1)} async-done(((bf16[128,6144]{1,0:T(8,128)(2,1)}), bf16[32,6144]{1,0:T(8,128)(2,1)}) %reduce-scatter.2.cloned.1.call-update) | async-done | bytes 393232 | tf_op jit(solution)/shard_map/reduce_scatter | solution.py:44
  160.9 1.5 fusion.35
  162.4 1.3 fusion.32
  163.7 1.6 collective-permute-start
  165.3 60.3 %psum.7 = f32[1,6144]{1,0:T(1,128)} all-reduce(f32[1,6144]{1,0:T(1,128)S(1)} %bitcast.79), channel_id=1, replica_groups=mesh['section'=2,'dp'=4,'shard'=4] {'dp','shard'}, use_global_device_ids=true, to_apply=%region_6.0 | all-reduce | flops 6144 | bytes 49152 | tf_op jit(solution)/shard_map/psum | solution.py:59
  225.6 1.5 constant_dynamic-slice_fusion.1
  227.1 11.0 %all-gather.13.cloned.1.call-done = bf16[512,3072]{1,0:T(8,128)(2,1)} async-done(((bf16[128,3072]{1,0:T(8,128)(2,1)}), bf16[512,3072]{1,0:T(8,128)(2,1)}) %all-gather.13.cloned.1.call-update) | async-done | bytes 3145744 | tf_op jit(solution)/shard_map/all_gather | solution.py:66
  238.1 19.6 %convolution_convert_fusion.1 = bf16[4,1536,3072]{2,1,0:T(8,128)(2,1)} fusion(bf16[4,128,1536]{2,1,0:T(8,128)(2,1)S(1)} %bitcast.72, bf16[4,128,3072]{2,1,0:T(8,128)(2,1)} %bitcast.73), kind=kOutput, calls=%fused_computation.1 | convolution fusion | flops 4850712576 | bytes 42467328 | tf_op jit(solution)/shard_map/kta,ktf->kaf/dot_general | solution.py:76
  257.7 28.2 %all-gather.19.cloned.1.call-done = bf16[1,512,6144]{2,1,0:T(8,128)(2,1)} async-done(((bf16[1,128,6144]{2,1,0:T(8,128)(2,1)}), bf16[1,512,6144]{2,1,0:T(8,128)(2,1)}) %all-gather.19.cloned.1.call-update) | async-done | bytes 6291472 | tf_op jit(solution)/shard_map/all_gather | solution.py:68
  285.9 1.5 constant_dynamic-slice_fusion
  287.4 29.2 %all-gather.15.cloned.1.call-done = bf16[512,3072]{1,0:T(8,128)(2,1)} async-done(((bf16[128,3072]{1,0:T(8,128)(2,1)}), bf16[512,3072]{1,0:T(8,128)(2,1)}) %all-gather.15.cloned.1.call-update) | async-done | bytes 3145744 | tf_op jit(solution)/shard_map/all_gather | solution.py:67
  316.6 17.6 %convolution_convert_fusion = bf16[4,3072,1536]{2,1,0:T(8,128)(2,1)} fusion(bf16[4,128,3072]{2,1,0:T(8,128)(2,1)} %bitcast.74, bf16[4,128,1536]{2,1,0:T(8,128)(2,1)S(1)} %bitcast.71), kind=kOutput, calls=%fused_computation | convolution fusion | flops 4850712576 | bytes 42467328 | tf_op jit(solution)/shard_map/ktf,kta->kfa/dot_general | solution.py:79
  334.2 18.5 %reduce_sum.74 = bf16[1536,3072]{1,0:T(8,128)(2,1)} reduce(bf16[4,1536,3072]{2,1,0:T(8,128)(2,1)} %convolution_convert_fusion.1, bf16[]{:T(256)} %constant.33.clone.1), dimensions={0}, to_apply=%region_7.0 | reduce | flops 14155776 | bytes 47185920 | tf_op jit(solution)/shard_map/reduce_sum | solution.py:82
  352.7 18.6 %reduce_sum.75 = bf16[3072,1536]{1,0:T(8,128)(2,1)} reduce(bf16[4,3072,1536]{2,1,0:T(8,128)(2,1)} %convolution_convert_fusion, bf16[]{:T(256)} %constant.33.clone.1), dimensions={0}, to_apply=%region_8.0 | reduce | flops 14155776 | bytes 47185920 | tf_op jit(solution)/shard_map/reduce_sum | solution.py:83
  371.3 0.7 copy.15
  (18 shorter events, 0.2 us)
Async XLA Ops:
  7.2 44.4 %all-gather.9.cloned.1.call-start = ((), (), s32[]{:S(2)}) async-start(), calls=%async_computation.1 | async-start | bytes 1966080 | tf_op jit(solution)/shard_map/all_gather | solution.py:35
  11.6 77.5 %all-gather.17.cloned.1.call-start = ((), (), s32[]{:S(2)}) async-start(), calls=%async_computation.6 | async-start | bytes 1966080 | tf_op jit(solution)/shard_map/all_gather | solution.py:36
  12.4 148.5 %reduce-scatter.2.cloned.1.call-start = ((), (), s32[]{:S(2)}) async-start(), calls=%async_computation.2 | async-start | bytes 1966080 | tf_op jit(solution)/shard_map/reduce_scatter | solution.py:44
  107.3 19.3 %copy-start.1 = (bf16[128,3072]{1,0:T(8,128)(2,1)}, bf16[128,3072]{1,0:T(8,128)(2,1)S(1)}, u32[]{:S(2)}) copy-start(bf16[128,3072]{1,0:T(8,128)(2,1)S(1)} %fusion.12) | copy-start | bytes 2359300
  126.6 99.0 %all-gather.11.cloned.1.call-start = ((), (), s32[]{:S(2)}) async-start(), calls=%async_computation.3 | async-start | bytes 7864320 | tf_op jit(solution)/shard_map/all_gather | solution.py:65
  127.2 33.7 %copy-start = (bf16[1,32,6144]{2,1,0:T(8,128)(2,1)S(1)}, bf16[1,32,6144]{2,1,0:T(8,128)(2,1)}, u32[]{:S(2)}) copy-start(bf16[1,32,6144]{2,1,0:T(8,128)(2,1)} %param.5) | copy-start | bytes 1179652
  127.2 33.7 %copy-start.3 = (f32[1,6144]{1,0:T(1,128)S(1)}, f32[1,6144]{1,0:T(1,128)}, u32[]{:S(2)}) copy-start(f32[1,6144]{1,0:T(1,128)} %param.7) | copy-start | bytes 73732
  127.2 111.0 %all-gather.13.cloned.1.call-start = ((), (), s32[]{:S(2)}) async-start(), calls=%async_computation.4 | async-start | bytes 3932160 | tf_op jit(solution)/shard_map/all_gather | solution.py:66
  127.8 34.6 %copy-start.2 = (bf16[1,32,6144]{2,1,0:T(8,128)(2,1)S(1)}, bf16[1,32,6144]{2,1,0:T(8,128)(2,1)}, u32[]{:S(2)}) copy-start(bf16[1,32,6144]{2,1,0:T(8,128)(2,1)} %param.6) | copy-start | bytes 1179652
  127.8 158.1 %all-gather.19.cloned.1.call-start = ((), (), s32[]{:S(2)}) async-start(), calls=%async_computation.7 | async-start | bytes 7864320 | tf_op jit(solution)/shard_map/all_gather | solution.py:68
  128.4 188.3 %all-gather.15.cloned.1.call-start = ((), (), s32[]{:S(2)}) async-start(), calls=%async_computation.5 | async-start | bytes 3932160 | tf_op jit(solution)/shard_map/all_gather | solution.py:67
  163.7 61.9 %collective-permute-start = (bf16[32,6144]{1,0:T(8,128)(2,1)S(1)}, bf16[32,6144]{1,0:T(8,128)(2,1)S(1)}, u32[]{:S(2)}, u32[]{:S(2)}) collective-permute-start(bf16[32,6144]{1,0:T(8,128)(2,1)S(1)} %fusion.32), channel_id=1, source_target_pairs={{16,0},{0,16},{17,1},{1,17},{18,2},{2,18},{19,3},{3,19},{20,4},{4,... | collective-permute-start | bytes 1179656 | tf_op jit(solution)/shard_map/ppermute | solution.py:14
Sparse Core Ops, SparseCore 0:
  11.7 39.7 all-gather.8
  53.1 35.9 all-gather.16
  126.7 34.1 reduce-scatter.1
  162.3 45.7 all-gather.10
  209.5 28.6 all-gather.12
  239.6 46.3 all-gather.18
  288.1 28.5 all-gather.14
where the time goes:
time: 379 us
  waiting for transfers between devices  164 us (43%)
  matrix products  90.8 us (24%)
  blocking collectives  60.3 us (16%)
  other arithmetic  44.3 us (12%)
  between operations  14.2 us (4%)
  local copies, waits for them, and re-layouts  3.79 us (1%)
    psum x1, blocking collectives, per_device(): gain_grad = lax.psum(jnp.sum(norm_error * centred, 0), ('dp', 'shard'))  60.3 us
    all_gather x1, waiting for transfers between devices, per_device(): lax.all_gather(normed, 'shard', axis=0, tiled=True)  39.1 us
    reduce_scatter x1, waiting for transfers between devices, per_device(): lax.psum_scatter(jnp.einsum('tf,df->td', pre_error, in_block, preferred_e...  31.8 us
    all_gather x1, waiting for transfers between devices, per_device(): piece_active = lax.all_gather(active, 'dp', axis=0, tiled=True)  29.2 us
    all_gather x1, waiting for transfers between devices, per_device(): piece_error = lax.all_gather(error_group, 'dp', axis=0, tiled=True)  28.2 us
    all_gather x1, waiting for transfers between devices, per_device(): lax.all_gather(errors, 'shard', axis=0, tiled=True)  21.3 us
    dot_general x1, matrix products, per_device(): jnp.einsum('kta,ktf->kaf', piece_normed, piece_pre, preferred_element_typ...  19.6 us
    dot_general x1, matrix products, per_device(): jnp.einsum('tf,df->td', pre_error, in_block, preferred_element_type=jnp.f...  19.3 us
  transfers between devices with their start and end apart: 8, of which 6 were waited for; matrix products, arithmetic and copies ran while one was open for 11% of the time, Pallas kernels for 0%

commit v1 on v0

v1 whole, which is shorter than its diff:
```python
import functools

import jax
import jax.numpy as jnp
from jax import lax
from jax.experimental import pallas as pl
from jax.experimental.pallas import tpu as pltpu
from jax.sharding import PartitionSpec as P

SQRT_HALF = 0.7071067811865476
INV_ROOT_TWO_PI = 0.3989422804014327
EPSILON = 1e-06
VMEM_BYTES = 40 * 1024 * 1024


def tile_of(extent, largest=512):
    for size in (512, 384, 256, 128):
        if size <= largest and extent % size == 0:
            return size
    return extent


def params(grid=1):
    return pltpu.CompilerParams(
        vmem_limit_bytes=VMEM_BYTES, dimension_semantics=("arbitrary",) * grid
    )


def cost(flops, moved):
    return pl.CostEstimate(flops=int(flops), bytes_accessed=int(moved), transcendentals=0)


def dot(a, b, a_dim, b_dim):
    return lax.dot_general(
        a, b, (((a_dim,), (b_dim,)), ((), ())), preferred_element_type=jnp.float32
    )


def whole(shape):
    return pl.BlockSpec(shape, lambda *_: (0,) * len(shape))


def norm_kernel(hi_ref, x_ref, e_ref, g_ref, n_far, n_near, e_far, e_near, full):
    half = n_far.shape[1]
    values = x_ref[...].astype(jnp.float32)
    centred = values - jnp.mean(values, -1, keepdims=True)
    variance = jnp.mean(centred * centred, -1, keepdims=True)
    full[...] = centred * lax.rsqrt(variance + EPSILON) * g_ref[...]
    near = pl.ds(pl.multiple_of(hi_ref[0] * half, half), half)
    far = pl.ds(pl.multiple_of((1 - hi_ref[0]) * half, half), half)
    n_far[...] = full[:, far].astype(n_far.dtype)
    n_near[...] = full[:, near].astype(n_near.dtype)
    e_far[...] = e_ref[:, far]
    e_near[...] = e_ref[:, near]


def norm_halves(hi, x, e, gain):
    rows, width = x.shape
    half = jax.ShapeDtypeStruct((rows, width // 2), x.dtype)
    return pl.pallas_call(
        norm_kernel,
        out_shape=[half] * 4,
        grid_spec=pltpu.PrefetchScalarGridSpec(
            num_scalar_prefetch=1,
            grid=(1,),
            in_specs=[whole(x.shape), whole(e.shape), whole(gain.shape)],
            out_specs=[whole(half.shape)] * 4,
            scratch_shapes=[pltpu.VMEM(x.shape, jnp.float32)],
        ),
        compiler_params=params(),
        cost_estimate=cost(10 * x.size, 8 * x.size),
    )(hi, x, e, gain)


def part_kernel(count, dim, stage, _, *refs):
    blocks, refs = refs[:count], refs[count:]
    w_ref, refs = refs[0], refs[1:]
    group = refs[-1]

    @pl.when(pl.program_id(0) == 0)
    def _():
        rows = blocks[0].shape[0]
        for k, block in enumerate(blocks):
            group[k * rows:(k + 1) * rows, :] = block[...]

    total = dot(group[...], w_ref[...], 1, dim)
    if stage == "first":
        refs[0][...] = total
    elif stage == "active":
        prior, active, slope = refs[:3]
        pre = prior[...] + total
        normal_cdf = 0.5 * (1.0 + lax.erf(pre * SQRT_HALF))
        density = INV_ROOT_TWO_PI * jnp.exp(-0.5 * pre * pre)
        active[...] = (pre * normal_cdf).astype(active.dtype)
        slope[...] = normal_cdf + pre * density
    else:
        prior, slope, pre_error = refs[:3]
        pre_error[...] = ((prior[...] + total) * slope[...]).astype(pre_error.dtype)


def part(which, blocks, weight, dim, stage, extra=()):
    rows, half = blocks[0].shape
    tokens = rows * len(blocks)
    hidden = weight.shape[1 - dim]
    tile = tile_of(hidden)
    kind = blocks[0].dtype
    if dim == 0:
        w_spec = pl.BlockSpec((half, tile), lambda j, s: (s[0], j))
    else:
        w_spec = pl.BlockSpec((tile, half), lambda j, s: (j, s[0]))
    column = pl.BlockSpec((tokens, tile), lambda j, s: (0, j))
    wide = jax.ShapeDtypeStruct((tokens, hidden), jnp.float32)
    narrow = jax.ShapeDtypeStruct((tokens, hidden), kind)
    outs = {"first": [wide], "active": [narrow, wide], "error": [narrow]}[stage]
    return pl.pallas_call(
        functools.partial(part_kernel, len(blocks), dim, stage),
        out_shape=outs + [jax.ShapeDtypeStruct((tokens, half), kind)],
        grid_spec=pltpu.PrefetchScalarGridSpec(
            num_scalar_prefetch=1,
            grid=(hidden // tile,),
            in_specs=[whole((rows, half))] * len(blocks) + [w_spec] + [column] * len(extra),
            out_specs=[column] * len(outs) + [whole((tokens, half))],
        ),
        compiler_params=params(),
        cost_estimate=cost(2 * tokens * half * hidden, 2 * half * hidden),
    )(which, *blocks, weight, *extra)


def back_kernel(count, _, p_ref, w_ref, n_ref, g_ref, *outs):
    rows = outs[0].shape[0]
    term = dot(p_ref[...], w_ref[...], 1, 1).astype(outs[0].dtype)
    for k in range(count):
        outs[k][...] = term[k * rows:(k + 1) * rows, :]
    product = term.astype(jnp.float32) * n_ref[...].astype(jnp.float32)
    outs[count][...] = jnp.sum(product, 0, keepdims=True) / g_ref[...]


def back(which, count, pre_error, w_in, normed, gain):
    tokens, hidden = pre_error.shape
    half = normed.shape[1]
    tile = tile_of(half)
    steps = half // tile
    column = lambda j, s: (0, j)
    return pl.pallas_call(
        functools.partial(back_kernel, count),
        out_shape=[jax.ShapeDtypeStruct((tokens // count, half), normed.dtype)] * count
        + [jax.ShapeDtypeStruct((1, half), jnp.float32)],
        grid_spec=pltpu.PrefetchScalarGridSpec(
            num_scalar_prefetch=1,
            grid=(steps,),
            in_specs=[
                whole(pre_error.shape),
                pl.BlockSpec((tile, hidden), lambda j, s: (s[0] * steps + j, 0)),
                pl.BlockSpec((tokens, tile), column),
                pl.BlockSpec((1, tile), lambda j, s: (0, s[0] * steps + j)),
            ],
            out_specs=[pl.BlockSpec((tokens // count, tile), column)] * count
            + [pl.BlockSpec((1, tile), column)],
        ),
        compiler_params=params(),
        cost_estimate=cost(2 * tokens * half * hidden, 2 * half * hidden),
    )(which, pre_error, w_in, normed, gain)


def grad_kernel(count, cut_rows, _, *refs):
    cut, full, (out, a_all, b_all) = refs[:count], refs[count:2 * count], refs[2 * count:]
    rows = cut[0].shape[0]

    @pl.when(pl.program_id(0) == 0)
    def _():
        for k in range(count):
            a_all[k * rows:(k + 1) * rows, :] = cut[k][...]
            b_all[k * rows:(k + 1) * rows, :] = full[k][...]

    size = out.shape[0]
    window = pl.ds(pl.multiple_of(pl.program_id(0) * size, size), size)
    if cut_rows:
        out[...] = dot(a_all[:, window], b_all[...], 0, 0).astype(out.dtype)
    else:
        out[...] = dot(b_all[:, window], a_all[...], 0, 0).astype(out.dtype)


def grad(lo, cut, full, cut_rows):
    rows, hidden = full[0].shape
    width = cut[0].shape[1] // 2
    count = len(full)
    shape = (width, hidden) if cut_rows else (hidden, width)
    tile = tile_of(shape[0], 256 if cut_rows else 512)
    return pl.pallas_call(
        functools.partial(grad_kernel, count, cut_rows),
        out_shape=jax.ShapeDtypeStruct(shape, full[0].dtype),
        grid_spec=pltpu.PrefetchScalarGridSpec(
            num_scalar_prefetch=1,
            grid=(shape[0] // tile,),
            in_specs=[pl.BlockSpec((rows, width), lambda j, s: (0, s[0]))] * count
            + [whole((rows, hidden))] * count,
            out_specs=pl.BlockSpec((tile, shape[1]), lambda j, s: (j, 0)),
            scratch_shapes=[
                pltpu.VMEM((count * rows, width), full[0].dtype),
                pltpu.VMEM((count * rows, hidden), full[0].dtype),
            ],
        ),
        compiler_params=params(),
        cost_estimate=cost(2 * count * rows * width * hidden, 2 * width * hidden),
    )(lo, *cut, *full)


def own_kernel(count, flag_ref, x_ref, e_ref, g_ref, *refs):
    out, scaled_ref = refs[2 * count:]
    half = refs[0].shape[1]
    hi, last = flag_ref[0], flag_ref[1]
    for k, place in enumerate((1 - hi, hi)):
        terms = refs[k * count:(k + 1) * count]
        total = terms[0][...].astype(jnp.float32)
        for term in terms[1:3]:
            total = total + term[...].astype(jnp.float32)
        for term in terms[3:]:
            total = total + jnp.where(last == 1, term[...].astype(jnp.float32), 0.0)
        window = pl.ds(pl.multiple_of(place * half, half), half)
        scaled_ref[:, window] = total * g_ref[:, window]
    values = x_ref[...].astype(jnp.float32)
    centred = values - jnp.mean(values, -1, keepdims=True)
    variance = jnp.mean(centred * centred, -1, keepdims=True)
    inverse = lax.rsqrt(variance + EPSILON)
    centred = centred * inverse
    scaled = scaled_ref[...]
    corrected = inverse * (
        scaled
        - jnp.mean(scaled, -1, keepdims=True)
        - centred * jnp.mean(scaled * centred, -1, keepdims=True)
    )
    out[...] = (e_ref[...].astype(jnp.float32) + corrected).astype(out.dtype)


def own_error_of(flags, x, e, gain, far, near):
    return pl.pallas_call(
        functools.partial(own_kernel, len(far)),
        out_shape=jax.ShapeDtypeStruct(x.shape, x.dtype),
        grid_spec=pltpu.PrefetchScalarGridSpec(
            num_scalar_prefetch=1,
            grid=(1,),
            in_specs=[whole(x.shape), whole(e.shape), whole(gain.shape)]
            + [whole(t.shape) for t in (*far, *near)],
            out_specs=whole(x.shape),
            scratch_shapes=[pltpu.VMEM(x.shape, jnp.float32)],
        ),
        compiler_params=params(),
        cost_estimate=cost(20 * x.size, 16 * x.size),
    )(flags, x, e, gain, *far, *near)


def swapped(block, axis, mask):
    return lax.ppermute(block, axis, [(i, i ^ mask) for i in range(lax.axis_size(axis))])


def on_line(axis):
    return lax.axis_size(axis) == 4


def gathered(own, axis, last):
    if not on_line(axis):
        return [lax.all_gather(own, axis, axis=0, tiled=True)]
    third = swapped(own, axis, 3)
    first = swapped(own, axis, 1)
    second = lax.ppermute(
        jnp.where(last, own, third), axis, [(0, 2), (3, 1), (2, 3), (1, 0)]
    )
    return [own, first, second, third]


def returned(terms, axis, last):
    if not on_line(axis):
        return [lax.psum_scatter(terms[0], axis, scatter_dimension=0, tiled=True)]
    own, first, second, third = terms
    second = lax.ppermute(second, axis, [(2, 0), (1, 3), (3, 2), (0, 1)])
    first = swapped(first, axis, 1)
    third = swapped(
        third + jnp.where(last, jnp.zeros_like(second), second), axis, 3
    )
    return [own, first, third, second]


def summed(value, axis):
    size = lax.axis_size(axis)
    if size & (size - 1):
        return lax.psum(value, axis)
    mask = 1
    while mask < size:
        value = value + swapped(value, axis, mask)
        mask *= 2
    return value


def per_device(features, delayed_error, ln_gain, w_in, w_out):
    x, e, w_in, w_out = features[0], delayed_error[0], w_in[0], w_out[0]
    dp = lax.axis_index("dp")
    shard = lax.axis_index("shard")
    last = (shard == 0) | (shard == lax.axis_size("shard") - 1)
    hi, lo = dp // 2, dp % 2
    near = jnp.full((1,), hi, jnp.int32)
    far = 1 - near
    lo = jnp.full((1,), lo, jnp.int32)
    flags = jnp.stack([hi, last.astype(jnp.int32)])

    n_far, n_near, e_far, e_near = norm_halves(near, x, e, ln_gain)
    n_far = gathered(n_far, "shard", last)
    n_near = gathered(n_near, "shard", last)
    e_far = gathered(e_far, "shard", last)
    e_near = gathered(e_near, "shard", last)
    count = len(n_far)

    def spread(mine, for_other):
        across = swapped(for_other, "dp", 2)
        return [mine, swapped(mine, "dp", 1), across, swapped(across, "dp", 1)]

    pre, n_far = part(far, n_far, w_in, 0, "first")
    active, slope, n_near = part(near, n_near, w_in, 0, "active", (pre,))
    n_all = spread(n_near, n_far)
    active_all = spread(active, active)
    back_act, e_far = part(far, e_far, w_out, 1, "first")
    pre_error, e_near = part(near, e_near, w_out, 1, "error", (back_act, slope))
    e_all = spread(e_near, e_far)
    pre_error_all = spread(pre_error, pre_error)

    *far_terms, gain_far = back(far, count, pre_error, w_in, n_far, ln_gain)
    far_terms = returned(far_terms, "shard", last)
    *near_terms, gain_near = back(near, count, pre_error, w_in, n_near, ln_gain)
    near_terms = returned(near_terms, "shard", last)
    gain_grad = jnp.where(
        hi == 1,
        jnp.concatenate([gain_far, gain_near], 1),
        jnp.concatenate([gain_near, gain_far], 1),
    )
    gain_grad = summed(summed(gain_grad, "dp"), "shard")

    w_out_grad = grad(lo, e_all, active_all, False)
    own_error = own_error_of(flags, x, e, ln_gain, far_terms, near_terms)
    n_section = lax.axis_size("section")
    passed = lax.ppermute(
        own_error, "section", [((i + 1) % n_section, i) for i in range(n_section)]
    )
    w_in_grad = grad(lo, n_all, pre_error_all, True)
    return passed[None], gain_grad, w_in_grad[None], w_out_grad[None]


def solution(mesh):
    return jax.shard_map(
        per_device,
        mesh=mesh,
        in_specs=(
            P("section", ("dp", "shard"), None),
            P("section", ("dp", "shard"), None),
            P("section", None),
            P("section", None, "shard"),
            P("section", "shard", None),
        ),
        out_specs=(
            P("section", ("dp", "shard"), None),
            P("section", None),
            P("section", "dp", "shard"),
            P("section", "shard", "dp"),
        ),
        check_vma=False,
    )
```

time: 379 us -> 238 us (0.63)
  matrix products: 90.8 us -> 0 us
  Pallas kernels: 0 us -> 85.6 us
  waiting for transfers between devices: 164 us -> 88 us
  blocking collectives: 60.3 us -> 0 us
  starting transfers between devices: 1.83 us -> 50.7 us
  other arithmetic: 44.3 us -> 1.7 us
  between operations: 14.2 us -> 0.89 us
  local copies, waits for them, and re-layouts: 3.79 us -> 9.7 us
    all_gather x6 -> x0, waiting for transfers between devices: 129 us -> none  [the longest x1 39.1 us: per_device(): lax.all_gather(normed, 'shard', axis=0, tiled=True)]
    dot_general x5 -> x0, matrix products: 90.8 us -> none  [the longest x1 19.6 us: per_device(): jnp.einsum('kta,ktf->kaf', piece_normed, piece_pre, preferred_element_typ...]
    ppermute x1 -> x35, waiting for transfers between devices: 0.01 us -> 88 us  [the longest x28 86.8 us: swapped(): lax.ppermute(block, axis, [(i, i ^ mask) for i in range(lax.axis_size(axi...]
    pallas_call x0 -> x10, Pallas kernels: none -> 85.6 us  [the longest x4 41.7 us: part(): pl.pallas_call(functools.partial(part_kernel, len(blocks), dim, stage), o...]
    psum x1 -> x0, blocking collectives: 60.3 us -> none  [per_device(): gain_grad = lax.psum(jnp.sum(norm_error * centred, 0), ('dp', 'shard'))]
    ppermute x1 -> x35, starting transfers between devices: 1.56 us -> 50.7 us  [the longest x28 39 us: swapped(): lax.ppermute(block, axis, [(i, i ^ mask) for i in range(lax.axis_size(axi...]
    reduce_sum x5 -> x0, other arithmetic: 41 us -> none  [the longest x1 18.6 us: per_device(): out_total = jnp.sum(rounded(out_terms), 0)]
    reduce_scatter x1 -> x0, waiting for transfers between devices: 31.8 us -> none  [per_device(): lax.psum_scatter(jnp.einsum('tf,df->td', pre_error, in_block, preferred_e...]
  transfers between devices with their start and end apart: 8 -> 35, of which waited for: 6 -> 14; matrix products, arithmetic and copies ran while one was open for 11% -> 1% of each run, Pallas kernels for 0% -> 22%
where the time goes in v1:
time: 238 us; the launch traced here: 237 us
  waiting for transfers between devices  88 us (37%)
  Pallas kernels  85.6 us (36%)
  starting transfers between devices  50.7 us (21%)
  local copies, waits for them, and re-layouts  9.7 us (4%)
    ppermute x28, waiting for transfers between devices, swapped(): lax.ppermute(block, axis, [(i, i ^ mask) for i in range(lax.axis_size(axi...  86.8 us
    pallas_call x4, Pallas kernels, part(): pl.pallas_call(functools.partial(part_kernel, len(blocks), dim, stage), o...  41.7 us
    ppermute x28, starting transfers between devices, swapped(): lax.ppermute(block, axis, [(i, i ^ mask) for i in range(lax.axis_size(axi...  39 us
    pallas_call x2, Pallas kernels, back(): pl.pallas_call(functools.partial(back_kernel, count), out_shape=[jax.Shap...  22.2 us
    pallas_call x2, Pallas kernels, grad(): pl.pallas_call(functools.partial(grad_kernel, count, cut_rows), out_shape...  19.6 us
    unnamed x37, local copies, waits for them, and re-layouts  9.7 us
    ppermute x4, starting transfers between devices, gathered(): lax.ppermute(jnp.where(last, own, third), axis, [(0, 2), (3, 1), (2, 3),...  7.19 us
  transfers between devices with their start and end apart: 35, of which 14 were waited for; matrix products, arithmetic and copies ran while one was open for 1% of the time, Pallas kernels for 22%

profile of v1, /device:TPU:0, one launch (start us, length us, event | category | flops | bytes accessed | tf_op | source)
XLA Modules:
  0.0 236.6 jit_solution(11591695602812329648)
XLA Ops:
  3.8 5.1 %collective-permute-start.1 = (bf16[32,3072]{1,0:T(8,128)(2,1)S(1)}, bf16[32,3072]{1,0:T(8,128)(2,1)S(1)}, u32[]{:S(2)}, u32[]{:S(2)}) collective-permute-start(bf16[32,3072]{1,0:T(8,128)(2,1)S(1)} %get-tuple-element.27.refs_0_), channel_id=1, source_target_pairs={{0,3},{1,2},{2,1},{3,0},{4,7},{5,6},{6,5},{7,4},{8,11},{9,10},{10,... | collective-permute-start | bytes 589832 | tf_op jit(solution)/shard_map/ppermute | solution.py:253
  11.0 2.9 %collective-permute-start.7 = (bf16[32,3072]{1,0:T(8,128)(2,1)S(1)}, bf16[32,3072]{1,0:T(8,128)(2,1)S(1)}, u32[]{:S(2)}, u32[]{:S(2)}) collective-permute-start(bf16[32,3072]{1,0:T(8,128)(2,1)S(1)} %get-tuple-element.30.refs_0_), channel_id=1, source_target_pairs={{0,3},{1,2},{2,1},{3,0},{4,7},{5,6},{6,5},{7,4},{8,11},{9,10},{10,... | collective-permute-start | bytes 589832 | tf_op jit(solution)/shard_map/ppermute | solution.py:253
  14.7 4.9 %collective-permute-start.6 = (bf16[32,3072]{1,0:T(8,128)(2,1)S(1)}, bf16[32,3072]{1,0:T(8,128)(2,1)S(1)}, u32[]{:S(2)}, u32[]{:S(2)}) collective-permute-start(bf16[32,3072]{1,0:T(8,128)(2,1)S(1)} %get-tuple-element.30.refs_0_), channel_id=1, source_target_pairs={{0,1},{1,0},{2,3},{3,2},{4,5},{5,4},{6,7},{7,6},{8,9},{9,8},{10,11... | collective-permute-start | bytes 589832 | tf_op jit(solution)/shard_map/ppermute | solution.py:253
  19.6 3.6 %collective-permute-done.4.refs_3_ = bf16[32,3072]{1,0:T(8,128)(2,1)S(1)} collective-permute-done((bf16[32,3072]{1,0:T(8,128)(2,1)S(1)}, bf16[32,3072]{1,0:T(8,128)(2,1)S(1)}, u32[]{:S(2)}, u32[]{:S(2)}) %collective-permute-start.4) | collective-permute-done | bytes 196640 | tf_op jit(solution)/shard_map/ppermute | solution.py:253
  23.2 3.8 %collective-permute-start.10 = (bf16[32,3072]{1,0:T(8,128)(2,1)S(1)}, bf16[32,3072]{1,0:T(8,128)(2,1)S(1)}, u32[]{:S(2)}, u32[]{:S(2)}) collective-permute-start(bf16[32,3072]{1,0:T(8,128)(2,1)S(1)} %get-tuple-element.31.refs_0_), channel_id=1, source_target_pairs={{0,3},{1,2},{2,1},{3,0},{4,7},{5,6},{6,5},{7,4},{8,11},{9,10},{10,... | collective-permute-start | bytes 589832 | tf_op jit(solution)/shard_map/ppermute | solution.py:253
  27.0 12.3 %collective-permute-done.10.refs_3_ = bf16[32,3072]{1,0:T(8,128)(2,1)S(1)} collective-permute-done((bf16[32,3072]{1,0:T(8,128)(2,1)S(1)}, bf16[32,3072]{1,0:T(8,128)(2,1)S(1)}, u32[]{:S(2)}, u32[]{:S(2)}) %collective-permute-start.10) | collective-permute-done | bytes 196640 | tf_op jit(solution)/shard_map/ppermute | solution.py:253
  39.4 3.7 %collective-permute-start.9 = (bf16[32,3072]{1,0:T(8,128)(2,1)S(1)}, bf16[32,3072]{1,0:T(8,128)(2,1)S(1)}, u32[]{:S(2)}, u32[]{:S(2)}) collective-permute-start(bf16[32,3072]{1,0:T(8,128)(2,1)S(1)} %get-tuple-element.31.refs_0_), channel_id=1, source_target_pairs={{0,1},{1,0},{2,3},{3,2},{4,5},{5,4},{6,7},{7,6},{8,9},{9,8},{10,11... | collective-permute-start | bytes 589832 | tf_op jit(solution)/shard_map/ppermute | solution.py:253
  44.2 4.7 %collective-permute-done.9.refs_1_ = bf16[32,3072]{1,0:T(8,128)(2,1)S(1)} collective-permute-done((bf16[32,3072]{1,0:T(8,128)(2,1)S(1)}, bf16[32,3072]{1,0:T(8,128)(2,1)S(1)}, u32[]{:S(2)}, u32[]{:S(2)}) %collective-permute-start.9) | collective-permute-done | bytes 196640 | tf_op jit(solution)/shard_map/ppermute | solution.py:253
  48.9 3.0 %collective-permute-start.2 = (bf16[32,3072]{1,0:T(8,128)(2,1)S(1)}, bf16[32,3072]{1,0:T(8,128)(2,1)S(1)}, u32[]{:S(2)}, u32[]{:S(2)}) collective-permute-start(bf16[32,3072]{1,0:T(8,128)(2,1)S(1)} %broadcast_select_fusion.3), channel_id=1, source_target_pairs={{0,2},{3,1},{2,3},{1,0},{4,6},{7,5},{6,7},{5,4},{8,10},{11,9},{10,... | collective-permute-start | bytes 589832 | tf_op jit(solution)/shard_map/ppermute | solution.py:265
  53.1 2.9 %collective-permute-start.8 = (bf16[32,3072]{1,0:T(8,128)(2,1)S(1)}, bf16[32,3072]{1,0:T(8,128)(2,1)S(1)}, u32[]{:S(2)}, u32[]{:S(2)}) collective-permute-start(bf16[32,3072]{1,0:T(8,128)(2,1)S(1)} %broadcast_select_fusion.1), channel_id=1, source_target_pairs={{0,2},{3,1},{2,3},{1,0},{4,6},{7,5},{6,7},{5,4},{8,10},{11,9},{10,... | collective-permute-start | bytes 589832 | tf_op jit(solution)/shard_map/ppermute | solution.py:265
  56.0 9.1 %shard_map.86 = (f32[128,3072]{1,0:T(8,128)S(1)}, bf16[128,3072]{1,0:T(8,128)(2,1)S(1)}) custom-call(s32[1]{0:T(128)S(6)} %sub.8._, bf16[32,3072]{1,0:T(8,128)(2,1)S(1)} %get-tuple-element.31.refs_0_, bf16[32,3072]{1,0:T(8,128)(2,1)S(1)} %collective-permute-done.9.refs_1_, bf16[32,3072]{1,0:T(8,128)(2,1)S(1)} %collective-permute-done.11.refs_2_, ...), custom_call_target="tpu_custom_call" | custom-call | flops 2415919104 | bytes 18874368 | tf_op jit(solution)/shard_map/pallas_call | solution.py:115
  65.3 9.9 %shard_map.87 = (bf16[128,3072]{1,0:T(8,128)(2,1)}, f32[128,3072]{1,0:T(8,128)S(1)}, bf16[128,3072]{1,0:T(8,128)(2,1)S(1)}) custom-call(s32[1]{0:T(128)} %bitcast.hi_ref._, bf16[32,3072]{1,0:T(8,128)(2,1)S(1)} %get-tuple-element.30.refs_0_, bf16[32,3072]{1,0:T(8,128)(2,1)S(1)} %collective-permute-done.6.refs_1_, ...), custom_call_target="tpu_custom_call" | custom-call | flops 2415919104 | bytes 18874368 | tf_op jit(solution)/shard_map/pallas_call | solution.py:115
  75.2 11.7 %shard_map.85 = (f32[128,3072]{1,0:T(8,128)S(1)}, bf16[128,3072]{1,0:T(8,128)(2,1)}) custom-call(s32[1]{0:T(128)S(6)} %sub.8._, bf16[32,3072]{1,0:T(8,128)(2,1)S(1)} %get-tuple-element.28.refs_0_, bf16[32,3072]{1,0:T(8,128)(2,1)S(1)} %collective-permute-done.3.refs_1_, bf16[32,3072]{1,0:T(8,128)(2,1)S(1)} %collective-permute-done.5.refs_2_, ...), custom_call_target="tpu_custom_call" | custom-call | flops 2415919104 | bytes 18874368 | tf_op jit(solution)/shard_map/pallas_call | solution.py:115
  86.9 11.0 %shard_map.88 = (bf16[128,3072]{1,0:T(8,128)(2,1)S(1)}, bf16[128,3072]{1,0:T(8,128)(2,1)S(1)}) custom-call(s32[1]{0:T(128)} %bitcast.hi_ref._, bf16[32,3072]{1,0:T(8,128)(2,1)S(1)} %get-tuple-element.27.refs_0_, bf16[32,3072]{1,0:T(8,128)(2,1)S(1)} %collective-permute-done.refs_1_, bf16[32,3072]{1,0:T(8,128)(2,1)S(1)} %collective-permute-done.2.refs_2_, ...), custom_call_target="tpu_custom_call" | custom-call | flops 2415919104 | bytes 18874368 | tf_op jit(solution)/shard_map/pallas_call | solution.py:115
  97.9 11.2 %shard_map.89 = (bf16[32,3072]{1,0:T(8,128)(2,1)S(1)}, bf16[32,3072]{1,0:T(8,128)(2,1)S(1)}, bf16[32,3072]{1,0:T(8,128)(2,1)S(1)}, bf16[32,3072]{1,0:T(8,128)(2,1)S(1)}, f32[1,3072]{1,0:T(1,128)S(1)}) custom-call(s32[1]{0:T(128)S(6)} %sub.8._, bf16[128,3072]{1,0:T(8,128)(2,1)S(1)} %get-tuple-element.34.p_ref.refs_4_, bf16[6144,3072]{1,0:T(8,128)(2,1)} %bitcast.16, ...), custom_call_target="tpu_custom_call" | custom-call | flops 2415919104 | bytes 18874368 | tf_op jit(solution)/shard_map/pallas_call | solution.py:144
  109.2 2.0 collective-permute-start.13
  111.1 11.0 %shard_map.90 = (bf16[32,3072]{1,0:T(8,128)(2,1)S(1)}, bf16[32,3072]{1,0:T(8,128)(2,1)S(1)}, bf16[32,3072]{1,0:T(8,128)(2,1)S(1)}, bf16[32,3072]{1,0:T(8,128)(2,1)S(1)}, f32[1,3072]{1,0:T(1,128)S(1)}) custom-call(s32[1]{0:T(128)} %bitcast.hi_ref._, bf16[128,3072]{1,0:T(8,128)(2,1)S(1)} %get-tuple-element.34.p_ref.refs_4_, bf16[6144,3072]{1,0:T(8,128)(2,1)} %bitcast.17, ...), custom_call_target="tpu_custom_call" | custom-call | flops 2415919104 | bytes 18874368 | tf_op jit(solution)/shard_map/pallas_call | solution.py:144
  123.5 1.6 collective-permute-start.20
  125.0 2.3 collective-permute-done.20
  132.4 1.9 collective-permute-start.22
  134.3 8.9 %collective-permute-done.22 = f32[1,6144]{1,0:T(1,128)S(1)} collective-permute-done((f32[1,6144]{1,0:T(1,128)S(1)}, f32[1,6144]{1,0:T(1,128)S(1)}, u32[]{:S(2)}, u32[]{:S(2)}) %collective-permute-start.22) | collective-permute-done | bytes 24608 | tf_op jit(solution)/shard_map/ppermute | solution.py:253
  146.8 2.5 %collective-permute-start.14 = (bf16[32,3072]{1,0:T(8,128)(2,1)S(1)}, bf16[32,3072]{1,0:T(8,128)(2,1)S(1)}, u32[]{:S(2)}, u32[]{:S(2)}) collective-permute-start(bf16[32,3072]{1,0:T(8,128)(2,1)S(1)} %select_add_fusion.1), channel_id=1, source_target_pairs={{0,3},{1,2},{2,1},{3,0},{4,7},{5,6},{6,5},{7,4},{8,11},{9,10},{10,... | collective-permute-start | bytes 589832 | tf_op jit(solution)/shard_map/ppermute | solution.py:253
  149.3 5.1 %collective-permute-done.14.refs_2_ = bf16[32,3072]{1,0:T(8,128)(2,1)S(1)} collective-permute-done((bf16[32,3072]{1,0:T(8,128)(2,1)S(1)}, bf16[32,3072]{1,0:T(8,128)(2,1)S(1)}, u32[]{:S(2)}, u32[]{:S(2)}) %collective-permute-start.14) | collective-permute-done | bytes 196640 | tf_op jit(solution)/shard_map/ppermute | solution.py:253
  155.1 2.4 %collective-permute-start.17 = (bf16[32,3072]{1,0:T(8,128)(2,1)S(1)}, bf16[32,3072]{1,0:T(8,128)(2,1)S(1)}, u32[]{:S(2)}, u32[]{:S(2)}) collective-permute-start(bf16[32,3072]{1,0:T(8,128)(2,1)S(1)} %select_add_fusion), channel_id=1, source_target_pairs={{0,3},{1,2},{2,1},{3,0},{4,7},{5,6},{6,5},{7,4},{8,11},{9,10},{10,... | collective-permute-start | bytes 589832 | tf_op jit(solution)/shard_map/ppermute | solution.py:253
  157.5 5.1 %collective-permute-done.17.refs_6_ = bf16[32,3072]{1,0:T(8,128)(2,1)S(1)} collective-permute-done((bf16[32,3072]{1,0:T(8,128)(2,1)S(1)}, bf16[32,3072]{1,0:T(8,128)(2,1)S(1)}, u32[]{:S(2)}, u32[]{:S(2)}) %collective-permute-start.17) | collective-permute-done | bytes 196640 | tf_op jit(solution)/shard_map/ppermute | solution.py:253
  165.2 15.5 %collective-permute-done.27.refs_6_ = bf16[128,3072]{1,0:T(8,128)(2,1)} collective-permute-done((bf16[128,3072]{1,0:T(8,128)(2,1)S(1)}, bf16[128,3072]{1,0:T(8,128)(2,1)}, u32[]{:S(2)}, u32[]{:S(2)}) %collective-permute-start.27) | collective-permute-done | bytes 786464 | tf_op jit(solution)/shard_map/ppermute | solution.py:253
  183.5 1.6 shard_map.91
  185.2 12.4 %collective-permute-done.33.refs_6_ = bf16[128,3072]{1,0:T(8,128)(2,1)} collective-permute-done((bf16[128,3072]{1,0:T(8,128)(2,1)}, bf16[128,3072]{1,0:T(8,128)(2,1)}, u32[]{:S(2)}, u32[]{:S(2)}) %collective-permute-start.33) | collective-permute-done | bytes 786464 | tf_op jit(solution)/shard_map/ppermute | solution.py:253
  197.5 1.5 collective-permute-start.18
  199.0 14.1 %collective-permute-done.30.refs_2_ = bf16[128,3072]{1,0:T(8,128)(2,1)} collective-permute-done((bf16[128,3072]{1,0:T(8,128)(2,1)}, bf16[128,3072]{1,0:T(8,128)(2,1)}, u32[]{:S(2)}, u32[]{:S(2)}) %collective-permute-start.30) | collective-permute-done | bytes 786464 | tf_op jit(solution)/shard_map/ppermute | solution.py:253
  216.2 9.7 %shard_map.92 = bf16[1536,3072]{1,0:T(8,128)(2,1)} custom-call(s32[1]{0:T(128)} %bitcast.7._, bf16[128,3072]{1,0:T(8,128)(2,1)S(1)} %get-tuple-element.40.n_ref.refs_0_, bf16[128,3072]{1,0:T(8,128)(2,1)S(1)} %copy-done.15, bf16[128,3072]{1,0:T(8,128)(2,1)} %collective-permute-done.24.refs_2_, bf16[128,3072]{1,0:T(8,128)(2,1)} %collective-permute-done.25.refs_3_, ...), custom_call_target="tpu_custom_call" | custom-call | flops 4831838208 | bytes 9437184 | tf_op jit(solution)/shard_map/pallas_call | solution.py:189
  226.0 9.9 %shard_map.93 = bf16[3072,1536]{1,0:T(8,128)(2,1)} custom-call(s32[1]{0:T(128)} %bitcast.7._, bf16[128,3072]{1,0:T(8,128)(2,1)S(1)} %copy-done.13, bf16[128,3072]{1,0:T(8,128)(2,1)} %collective-permute-done.29.refs_1_, bf16[128,3072]{1,0:T(8,128)(2,1)} %collective-permute-done.30.refs_2_, bf16[128,3072]{1,0:T(8,128)(2,1)} %collective-permute-done.31.refs_3_, ...), custom_call_target="tpu_custom_call" | custom-call | flops 4831838208 | bytes 9437184 | tf_op jit(solution)/shard_map/pallas_call | solution.py:189
  (97 shorter events, 28.3 us)
Async XLA Ops:
  3.8 10.9 %collective-permute-start.1 = (bf16[32,3072]{1,0:T(8,128)(2,1)S(1)}, bf16[32,3072]{1,0:T(8,128)(2,1)S(1)}, u32[]{:S(2)}, u32[]{:S(2)}) collective-permute-start(bf16[32,3072]{1,0:T(8,128)(2,1)S(1)} %get-tuple-element.27.refs_0_), channel_id=1, source_target_pairs={{0,3},{1,2},{2,1},{3,0},{4,7},{5,6},{6,5},{7,4},{8,11},{9,10},{10,... | collective-permute-start | bytes 589832 | tf_op jit(solution)/shard_map/ppermute | solution.py:253
  9.0 78.0 %collective-permute-start = (bf16[32,3072]{1,0:T(8,128)(2,1)S(1)}, bf16[32,3072]{1,0:T(8,128)(2,1)S(1)}, u32[]{:S(2)}, u32[]{:S(2)}) collective-permute-start(bf16[32,3072]{1,0:T(8,128)(2,1)S(1)} %get-tuple-element.27.refs_0_), channel_id=1, source_target_pairs={{0,1},{1,0},{2,3},{3,2},{4,5},{5,4},{6,7},{7,6},{8,9},{9,8},{10,11... | collective-permute-start | bytes 589832 | tf_op jit(solution)/shard_map/ppermute | solution.py:253
  9.0 14.2 %collective-permute-start.4 = (bf16[32,3072]{1,0:T(8,128)(2,1)S(1)}, bf16[32,3072]{1,0:T(8,128)(2,1)S(1)}, u32[]{:S(2)}, u32[]{:S(2)}) collective-permute-start(bf16[32,3072]{1,0:T(8,128)(2,1)S(1)} %get-tuple-element.28.refs_0_), channel_id=1, source_target_pairs={{0,3},{1,2},{2,1},{3,0},{4,7},{5,6},{6,5},{7,4},{8,11},{9,10},{10,... | collective-permute-start | bytes 589832 | tf_op jit(solution)/shard_map/ppermute | solution.py:253
  9.9 65.4 %collective-permute-start.3 = (bf16[32,3072]{1,0:T(8,128)(2,1)S(1)}, bf16[32,3072]{1,0:T(8,128)(2,1)S(1)}, u32[]{:S(2)}, u32[]{:S(2)}) collective-permute-start(bf16[32,3072]{1,0:T(8,128)(2,1)S(1)} %get-tuple-element.28.refs_0_), channel_id=1, source_target_pairs={{0,1},{1,0},{2,3},{3,2},{4,5},{5,4},{6,7},{7,6},{8,9},{9,8},{10,11... | collective-permute-start | bytes 589832 | tf_op jit(solution)/shard_map/ppermute | solution.py:253
  11.0 32.1 %collective-permute-start.7 = (bf16[32,3072]{1,0:T(8,128)(2,1)S(1)}, bf16[32,3072]{1,0:T(8,128)(2,1)S(1)}, u32[]{:S(2)}, u32[]{:S(2)}) collective-permute-start(bf16[32,3072]{1,0:T(8,128)(2,1)S(1)} %get-tuple-element.30.refs_0_), channel_id=1, source_target_pairs={{0,3},{1,2},{2,1},{3,0},{4,7},{5,6},{6,5},{7,4},{8,11},{9,10},{10,... | collective-permute-start | bytes 589832 | tf_op jit(solution)/shard_map/ppermute | solution.py:253
  14.7 50.4 %collective-permute-start.6 = (bf16[32,3072]{1,0:T(8,128)(2,1)S(1)}, bf16[32,3072]{1,0:T(8,128)(2,1)S(1)}, u32[]{:S(2)}, u32[]{:S(2)}) collective-permute-start(bf16[32,3072]{1,0:T(8,128)(2,1)S(1)} %get-tuple-element.30.refs_0_), channel_id=1, source_target_pairs={{0,1},{1,0},{2,3},{3,2},{4,5},{5,4},{6,7},{7,6},{8,9},{9,8},{10,11... | collective-permute-start | bytes 589832 | tf_op jit(solution)/shard_map/ppermute | solution.py:253
  23.2 16.2 %collective-permute-start.10 = (bf16[32,3072]{1,0:T(8,128)(2,1)S(1)}, bf16[32,3072]{1,0:T(8,128)(2,1)S(1)}, u32[]{:S(2)}, u32[]{:S(2)}) collective-permute-start(bf16[32,3072]{1,0:T(8,128)(2,1)S(1)} %get-tuple-element.31.refs_0_), channel_id=1, source_target_pairs={{0,3},{1,2},{2,1},{3,0},{4,7},{5,6},{6,5},{7,4},{8,11},{9,10},{10,... | collective-permute-start | bytes 589832 | tf_op jit(solution)/shard_map/ppermute | solution.py:253
  39.4 9.5 %collective-permute-start.9 = (bf16[32,3072]{1,0:T(8,128)(2,1)S(1)}, bf16[32,3072]{1,0:T(8,128)(2,1)S(1)}, u32[]{:S(2)}, u32[]{:S(2)}) collective-permute-start(bf16[32,3072]{1,0:T(8,128)(2,1)S(1)} %get-tuple-element.31.refs_0_), channel_id=1, source_target_pairs={{0,1},{1,0},{2,3},{3,2},{4,5},{5,4},{6,7},{7,6},{8,9},{9,8},{10,11... | collective-permute-start | bytes 589832 | tf_op jit(solution)/shard_map/ppermute | solution.py:253
  43.1 10.0 %collective-permute-start.11 = (bf16[32,3072]{1,0:T(8,128)(2,1)S(1)}, bf16[32,3072]{1,0:T(8,128)(2,1)S(1)}, u32[]{:S(2)}, u32[]{:S(2)}) collective-permute-start(bf16[32,3072]{1,0:T(8,128)(2,1)S(1)} %broadcast_select_fusion), channel_id=1, source_target_pairs={{0,2},{3,1},{2,3},{1,0},{4,6},{7,5},{6,7},{5,4},{8,10},{11,9},{10,... | collective-permute-start | bytes 589832 | tf_op jit(solution)/shard_map/ppermute | solution.py:265
  48.9 38.1 %collective-permute-start.2 = (bf16[32,3072]{1,0:T(8,128)(2,1)S(1)}, bf16[32,3072]{1,0:T(8,128)(2,1)S(1)}, u32[]{:S(2)}, u32[]{:S(2)}) collective-permute-start(bf16[32,3072]{1,0:T(8,128)(2,1)S(1)} %broadcast_select_fusion.3), channel_id=1, source_target_pairs={{0,2},{3,1},{2,3},{1,0},{4,6},{7,5},{6,7},{5,4},{8,10},{11,9},{10,... | collective-permute-start | bytes 589832 | tf_op jit(solution)/shard_map/ppermute | solution.py:265
  53.1 12.2 %collective-permute-start.8 = (bf16[32,3072]{1,0:T(8,128)(2,1)S(1)}, bf16[32,3072]{1,0:T(8,128)(2,1)S(1)}, u32[]{:S(2)}, u32[]{:S(2)}) collective-permute-start(bf16[32,3072]{1,0:T(8,128)(2,1)S(1)} %broadcast_select_fusion.1), channel_id=1, source_target_pairs={{0,2},{3,1},{2,3},{1,0},{4,6},{7,5},{6,7},{5,4},{8,10},{11,9},{10,... | collective-permute-start | bytes 589832 | tf_op jit(solution)/shard_map/ppermute | solution.py:265
  65.1 10.1 %collective-permute-start.5 = (bf16[32,3072]{1,0:T(8,128)(2,1)S(1)}, bf16[32,3072]{1,0:T(8,128)(2,1)S(1)}, u32[]{:S(2)}, u32[]{:S(2)}) collective-permute-start(bf16[32,3072]{1,0:T(8,128)(2,1)S(1)} %broadcast_select_fusion.2), channel_id=1, source_target_pairs={{0,2},{3,1},{2,3},{1,0},{4,6},{7,5},{6,7},{5,4},{8,10},{11,9},{10,... | collective-permute-start | bytes 589832 | tf_op jit(solution)/shard_map/ppermute | solution.py:265
  109.2 23.2 %collective-permute-start.13 = (bf16[32,3072]{1,0:T(8,128)(2,1)S(1)}, bf16[32,3072]{1,0:T(8,128)(2,1)S(1)}, u32[]{:S(2)}, u32[]{:S(2)}) collective-permute-start(bf16[32,3072]{1,0:T(8,128)(2,1)S(1)} %get-tuple-element.39), channel_id=1, source_target_pairs={{2,0},{1,3},{3,2},{0,1},{6,4},{5,7},{7,6},{4,5},{10,8},{9,11},{11,... | collective-permute-start | bytes 589832 | tf_op jit(solution)/shard_map/ppermute | solution.py:275
  128.5 34.9 %collective-permute-start.23 = (bf16[128,3072]{1,0:T(8,128)(2,1)S(1)}, bf16[128,3072]{1,0:T(8,128)(2,1)S(1)}, u32[]{:S(2)}, u32[]{:S(2)}) collective-permute-start(bf16[128,3072]{1,0:T(8,128)(2,1)S(1)} %get-tuple-element.40.n_ref.refs_0_), channel_id=1, source_target_pairs={{0,4},{4,0},{8,12},{12,8},{1,5},{5,1},{9,13},{13,9},{2,6},{6,2},{1... | collective-permute-start | bytes 2359304 | tf_op jit(solution)/shard_map/ppermute | solution.py:253
  128.5 16.2 %collective-permute-start.12 = (bf16[32,3072]{1,0:T(8,128)(2,1)S(1)}, bf16[32,3072]{1,0:T(8,128)(2,1)S(1)}, u32[]{:S(2)}, u32[]{:S(2)}) collective-permute-start(bf16[32,3072]{1,0:T(8,128)(2,1)S(1)} %get-tuple-element.37), channel_id=1, source_target_pairs={{0,1},{1,0},{2,3},{3,2},{4,5},{5,4},{6,7},{7,6},{8,9},{9,8},{10,11... | collective-permute-start | bytes 589832 | tf_op jit(solution)/shard_map/ppermute | solution.py:253
  129.5 15.8 %collective-permute-start.15 = (bf16[32,3072]{1,0:T(8,128)(2,1)S(1)}, bf16[32,3072]{1,0:T(8,128)(2,1)S(1)}, u32[]{:S(2)}, u32[]{:S(2)}) collective-permute-start(bf16[32,3072]{1,0:T(8,128)(2,1)S(1)} %get-tuple-element.42), channel_id=1, source_target_pairs={{0,1},{1,0},{2,3},{3,2},{4,5},{5,4},{6,7},{7,6},{8,9},{9,8},{10,11... | collective-permute-start | bytes 589832 | tf_op jit(solution)/shard_map/ppermute | solution.py:253
  131.3 15.5 %collective-permute-start.16 = (bf16[32,3072]{1,0:T(8,128)(2,1)S(1)}, bf16[32,3072]{1,0:T(8,128)(2,1)S(1)}, u32[]{:S(2)}, u32[]{:S(2)}) collective-permute-start(bf16[32,3072]{1,0:T(8,128)(2,1)S(1)} %get-tuple-element.44), channel_id=1, source_target_pairs={{2,0},{1,3},{3,2},{0,1},{6,4},{5,7},{7,6},{4,5},{10,8},{9,11},{11,... | collective-permute-start | bytes 589832 | tf_op jit(solution)/shard_map/ppermute | solution.py:275
  132.4 10.9 %collective-permute-start.22 = (f32[1,6144]{1,0:T(1,128)S(1)}, f32[1,6144]{1,0:T(1,128)S(1)}, u32[]{:S(2)}, u32[]{:S(2)}) collective-permute-start(f32[1,6144]{1,0:T(1,128)S(1)} %add.27), channel_id=1, source_target_pairs={{0,2},{1,3},{2,0},{3,1},{4,6},{5,7},{6,4},{7,5},{8,10},{9,11},{10,... | collective-permute-start | bytes 73736 | tf_op jit(solution)/shard_map/ppermute | solution.py:253
  143.3 21.6 %collective-permute-start.24 = (bf16[128,3072]{1,0:T(8,128)(2,1)S(1)}, bf16[128,3072]{1,0:T(8,128)(2,1)}, u32[]{:S(2)}, u32[]{:S(2)}) collective-permute-start(bf16[128,3072]{1,0:T(8,128)(2,1)S(1)} %get-tuple-element.35.n_ref), channel_id=1, source_target_pairs={{0,8},{4,12},{8,0},{12,4},{1,9},{5,13},{9,1},{13,5},{2,10},{6,14},... | collective-permute-start | bytes 2359304 | tf_op jit(solution)/shard_map/ppermute | solution.py:253
  144.8 35.9 %collective-permute-start.27 = (bf16[128,3072]{1,0:T(8,128)(2,1)S(1)}, bf16[128,3072]{1,0:T(8,128)(2,1)}, u32[]{:S(2)}, u32[]{:S(2)}) collective-permute-start(bf16[128,3072]{1,0:T(8,128)(2,1)S(1)} %get-tuple-element.34.p_ref.refs_4_), channel_id=1, source_target_pairs={{0,8},{4,12},{8,0},{12,4},{1,9},{5,13},{9,1},{13,5},{2,10},{6,14},... | collective-permute-start | bytes 2359304 | tf_op jit(solution)/shard_map/ppermute | solution.py:253
  145.3 52.2 %collective-permute-start.33 = (bf16[128,3072]{1,0:T(8,128)(2,1)}, bf16[128,3072]{1,0:T(8,128)(2,1)}, u32[]{:S(2)}, u32[]{:S(2)}) collective-permute-start(bf16[128,3072]{1,0:T(8,128)(2,1)} %get-tuple-element.49.refs_4_), channel_id=1, source_target_pairs={{0,8},{4,12},{8,0},{12,4},{1,9},{5,13},{9,1},{13,5},{2,10},{6,14},... | collective-permute-start | bytes 2359304 | tf_op jit(solution)/shard_map/ppermute | solution.py:253
  146.8 7.6 %collective-permute-start.14 = (bf16[32,3072]{1,0:T(8,128)(2,1)S(1)}, bf16[32,3072]{1,0:T(8,128)(2,1)S(1)}, u32[]{:S(2)}, u32[]{:S(2)}) collective-permute-start(bf16[32,3072]{1,0:T(8,128)(2,1)S(1)} %select_add_fusion.1), channel_id=1, source_target_pairs={{0,3},{1,2},{2,1},{3,0},{4,7},{5,6},{6,5},{7,4},{8,11},{9,10},{10,... | collective-permute-start | bytes 589832 | tf_op jit(solution)/shard_map/ppermute | solution.py:253
  155.1 7.6 %collective-permute-start.17 = (bf16[32,3072]{1,0:T(8,128)(2,1)S(1)}, bf16[32,3072]{1,0:T(8,128)(2,1)S(1)}, u32[]{:S(2)}, u32[]{:S(2)}) collective-permute-start(bf16[32,3072]{1,0:T(8,128)(2,1)S(1)} %select_add_fusion), channel_id=1, source_target_pairs={{0,3},{1,2},{2,1},{3,0},{4,7},{5,6},{6,5},{7,4},{8,11},{9,10},{10,... | collective-permute-start | bytes 589832 | tf_op jit(solution)/shard_map/ppermute | solution.py:253
  163.4 35.6 %collective-permute-start.26 = (bf16[128,3072]{1,0:T(8,128)(2,1)S(1)}, bf16[128,3072]{1,0:T(8,128)(2,1)}, u32[]{:S(2)}, u32[]{:S(2)}) collective-permute-start(bf16[128,3072]{1,0:T(8,128)(2,1)S(1)} %get-tuple-element.34.p_ref.refs_4_), channel_id=1, source_target_pairs={{0,4},{4,0},{8,12},{12,8},{1,5},{5,1},{9,13},{13,9},{2,6},{6,2},{1... | collective-permute-start | bytes 2359304 | tf_op jit(solution)/shard_map/ppermute | solution.py:253
  164.3 48.8 %collective-permute-start.30 = (bf16[128,3072]{1,0:T(8,128)(2,1)}, bf16[128,3072]{1,0:T(8,128)(2,1)}, u32[]{:S(2)}, u32[]{:S(2)}) collective-permute-start(bf16[128,3072]{1,0:T(8,128)(2,1)} %get-tuple-element.48), channel_id=1, source_target_pairs={{0,8},{4,12},{8,0},{12,4},{1,9},{5,13},{9,1},{13,5},{2,10},{6,14},... | collective-permute-start | bytes 2359304 | tf_op jit(solution)/shard_map/ppermute | solution.py:253
  164.9 48.8 %collective-permute-start.25 = (bf16[128,3072]{1,0:T(8,128)(2,1)}, bf16[128,3072]{1,0:T(8,128)(2,1)}, u32[]{:S(2)}, u32[]{:S(2)}) collective-permute-start(bf16[128,3072]{1,0:T(8,128)(2,1)} %collective-permute-done.24.refs_2_), channel_id=1, source_target_pairs={{0,4},{4,0},{8,12},{12,8},{1,5},{5,1},{9,13},{13,9},{2,6},{6,2},{1... | collective-permute-start | bytes 2359304 | tf_op jit(solution)/shard_map/ppermute | solution.py:253
  180.7 34.4 %collective-permute-start.28 = (bf16[128,3072]{1,0:T(8,128)(2,1)}, bf16[128,3072]{1,0:T(8,128)(2,1)}, u32[]{:S(2)}, u32[]{:S(2)}) collective-permute-start(bf16[128,3072]{1,0:T(8,128)(2,1)} %collective-permute-done.27.refs_6_), channel_id=1, source_target_pairs={{0,4},{4,0},{8,12},{12,8},{1,5},{5,1},{9,13},{13,9},{2,6},{6,2},{1... | collective-permute-start | bytes 2359304 | tf_op jit(solution)/shard_map/ppermute | solution.py:253
  197.5 15.6 %collective-permute-start.18 = (bf16[32,6144]{1,0:T(8,128)(2,1)S(1)}, bf16[32,6144]{1,0:T(8,128)(2,1)S(1)}, u32[]{:S(2)}, u32[]{:S(2)}) collective-permute-start(bf16[32,6144]{1,0:T(8,128)(2,1)S(1)} %shard_map.91), channel_id=1, source_target_pairs={{16,0},{0,16},{17,1},{1,17},{18,2},{2,18},{19,3},{3,19},{20,4},{4,... | collective-permute-start | bytes 1179656 | tf_op jit(solution)/shard_map/ppermute | solution.py:339
  199.0 26.9 %collective-permute-start.32 = (bf16[128,3072]{1,0:T(8,128)(2,1)}, bf16[128,3072]{1,0:T(8,128)(2,1)S(1)}, u32[]{:S(2)}, u32[]{:S(2)}) collective-permute-start(bf16[128,3072]{1,0:T(8,128)(2,1)} %get-tuple-element.49.refs_4_), channel_id=1, source_target_pairs={{0,4},{4,0},{8,12},{12,8},{1,5},{5,1},{9,13},{13,9},{2,6},{6,2},{1... | collective-permute-start | bytes 2359304 | tf_op jit(solution)/shard_map/ppermute | solution.py:253
  213.1 12.9 %collective-permute-start.29 = (bf16[128,3072]{1,0:T(8,128)(2,1)}, bf16[128,3072]{1,0:T(8,128)(2,1)}, u32[]{:S(2)}, u32[]{:S(2)}) collective-permute-start(bf16[128,3072]{1,0:T(8,128)(2,1)} %copy-done.12), channel_id=1, source_target_pairs={{0,4},{4,0},{8,12},{12,8},{1,5},{5,1},{9,13},{13,9},{2,6},{6,2},{1... | collective-permute-start | bytes 2359304 | tf_op jit(solution)/shard_map/ppermute | solution.py:253
  213.1 12.9 %collective-permute-start.34 = (bf16[128,3072]{1,0:T(8,128)(2,1)}, bf16[128,3072]{1,0:T(8,128)(2,1)}, u32[]{:S(2)}, u32[]{:S(2)}) collective-permute-start(bf16[128,3072]{1,0:T(8,128)(2,1)} %collective-permute-done.33.refs_6_), channel_id=1, source_target_pairs={{0,4},{4,0},{8,12},{12,8},{1,5},{5,1},{9,13},{13,9},{2,6},{6,2},{1... | collective-permute-start | bytes 2359304 | tf_op jit(solution)/shard_map/ppermute | solution.py:253
  213.6 12.4 %collective-permute-start.31 = (bf16[128,3072]{1,0:T(8,128)(2,1)}, bf16[128,3072]{1,0:T(8,128)(2,1)}, u32[]{:S(2)}, u32[]{:S(2)}) collective-permute-start(bf16[128,3072]{1,0:T(8,128)(2,1)} %collective-permute-done.30.refs_2_), channel_id=1, source_target_pairs={{0,4},{4,0},{8,12},{12,8},{1,5},{5,1},{9,13},{13,9},{2,6},{6,2},{1... | collective-permute-start | bytes 2359304 | tf_op jit(solution)/shard_map/ppermute | solution.py:253
  (21 other events, 295.9 us)

commit v2 on v0

v2 whole, which is shorter than its diff:
```python
import functools

import jax
import jax.numpy as jnp
from jax import lax
from jax.experimental import pallas as pl
from jax.experimental.pallas import tpu as pltpu
from jax.sharding import PartitionSpec as P

SQRT_HALF = 0.7071067811865476
INV_ROOT_TWO_PI = 0.3989422804014327
EPSILON = 1e-06
MIB = 1024 * 1024
PIECES = 4


def tile_of(extent, largest=512):
    for size in (512, 384, 256, 128):
        if size <= largest and extent % size == 0:
            return size
    return extent


def dot(a, b, a_dim, b_dim):
    return lax.dot_general(
        a, b, (((a_dim,), (b_dim,)), ((), ())), preferred_element_type=jnp.float32
    )


def array(shape, kind):
    return jax.ShapeDtypeStruct(shape, kind)


def window(size, place):
    return pl.ds(pl.multiple_of(place * size, size), size)


def pair_place():
    return lax.axis_index("dp") % 2


def on_end():
    shard = lax.axis_index("shard")
    return (shard == 0) | (shard == lax.axis_size("shard") - 1)


def run(body, arrays, outputs, scratch=(), apart=(), out_apart=(), after=(), limit=None):
    n_in, n_out = len(arrays) + len(apart), len(outputs) + len(out_apart)
    anywhere, near = pl.BlockSpec(memory_space=pl.ANY), pl.BlockSpec(memory_space=pltpu.VMEM)

    def kernel(*refs):
        first = n_in + len(after)
        body(refs[:n_in], refs[first:first + n_out], refs[first + n_out:])

    return pl.pallas_call(
        kernel,
        out_shape=[*outputs, *out_apart],
        in_specs=[near] * len(arrays) + [anywhere] * (len(apart) + len(after)),
        out_specs=[near] * len(outputs) + [anywhere] * len(out_apart),
        scratch_shapes=list(scratch),
        compiler_params=pltpu.CompilerParams(
            vmem_limit_bytes=((limit or 8) if lax.axis_size("shard") == 4 else 58) * MIB
        ),
        cost_estimate=pl.CostEstimate(flops=1000, bytes_accessed=1000, transcendentals=0),
    )(*arrays, *apart, *after)


def normalised(x_ref):
    values = x_ref[...].astype(jnp.float32)
    centred = values - jnp.mean(values, -1, keepdims=True)
    variance = jnp.mean(centred * centred, -1, keepdims=True)
    inverse = lax.rsqrt(variance + EPSILON)
    return centred * inverse, inverse


def far_place():
    return 1 - lax.axis_index("dp") // 2


def near_place():
    return lax.axis_index("dp") // 2


def tokens_of(x, e, gain):
    rows, width = x.shape
    half = width // 2

    def body(ins, outs, scratch):
        x_near, e_near, g_near, sems = scratch
        copies = [
            pltpu.make_async_copy(ins[k], place, sems.at[k])
            for k, place in enumerate((x_near, e_near, g_near))
        ]
        for copy in copies:
            copy.start()
        for copy in copies:
            copy.wait()
        outs[0][:rows, :] = (normalised(x_near)[0] * g_near[...]).astype(x.dtype)
        outs[0][rows:, :] = e_near[...]
        outs[1][...] = outs[0][:, window(half, far_place())]

    return run(
        body, (), [array((2 * rows, width), x.dtype), array((2 * rows, half), x.dtype)],
        apart=(x, e, gain),
        scratch=[
            pltpu.VMEM(x.shape, x.dtype),
            pltpu.VMEM(e.shape, e.dtype),
            pltpu.VMEM(gain.shape, gain.dtype),
            pltpu.SemaphoreType.DMA((3,)),
        ],
        limit=58,
    )


def passed_on(own, came, after=()):
    rows, width = own.shape
    half = width // 2

    def body(ins, outs, scratch):
        for out, place in zip(outs, (far_place(), near_place())):
            columns = window(half, place)
            out[...] = jnp.where(on_end(), ins[0][:, columns], ins[1][:, columns])

    return run(body, (own, came), [array((rows, half), own.dtype)] * 2, after=after)


def far_of(block, after=()):
    rows, width = block.shape
    half = width // 2

    def body(ins, outs, scratch):
        outs[0][...] = ins[0][:, window(half, far_place())]

    return run(body, (block,), [array((rows, half), block.dtype)], after=after)[0]


def grouped(blocks, near, apart=(), pieces=0, after=()):
    half = blocks[0].shape[1] // 2
    rows, kind = blocks[0].shape[0] // 2, blocks[0].dtype
    below = rows * len(blocks)

    def body(ins, outs, scratch):
        columns = window(half, near_place() if near else far_place())
        for k, block in enumerate(ins):
            part = block[...] if block.shape[1] == half else block[:, columns]
            outs[0][k * rows:(k + 1) * rows, :] = part[:rows]
            outs[0][below + k * rows:below + (k + 1) * rows, :] = part[rows:]
            if k in apart:
                at = apart.index(k) * 2 * rows
                outs[1][at:at + 2 * rows, :] = part
        for k in range(pieces):
            at = k * (2 * below // pieces)
            outs[1 + k][...] = outs[0][at:at + 2 * below // pieces, :]

    outs = [array((2 * below, half), kind)]
    if apart:
        outs.append(array((2 * rows * len(apart), half), kind))
    outs += [array((2 * below // pieces, half), kind)] * pieces if pieces else []
    return run(body, blocks, outs, after=after)


def regrouped(parts, after=()):
    half = parts[0].shape[1]
    rows = parts[0].shape[0] // 2
    count = sum(part.shape[0] for part in parts) // (2 * rows)

    def body(ins, outs, scratch):
        blocks = [
            part[at:at + 2 * rows, :] for part in ins for at in range(0, part.shape[0], 2 * rows)
        ]
        for k, block in enumerate(blocks):
            outs[0][k * rows:(k + 1) * rows, :] = block[:rows]
            outs[0][(count + k) * rows:(count + k + 1) * rows, :] = block[rows:]

    outs = [array((2 * count * rows, half), parts[0].dtype)]
    return run(body, parts, outs, after=after)[0]


def held(block, after):
    def body(ins, outs, scratch):
        outs[0][...] = ins[0][...]

    return run(body, (block,), [array(block.shape, block.dtype)], after=after)[0]


def forth_and_back(groups, w_in, w_out, after=()):
    tokens, half = groups[0].shape
    rows, hidden, kind = tokens // 2, w_in.shape[1] // 2, groups[0].dtype
    tile = tile_of(hidden)
    steps = hidden // tile

    def body(ins, outs, scratch):
        w_in_ref, w_out_ref = ins[-2:]
        rows_all, in_weight, out_weight, sems = scratch

        def coming(j, forth, near=False):
            units = window(tile, pair_place() * steps + j)
            place = window(tile, j)
            depth = window(half, near_place() if near else far_place())
            if forth:
                source = w_in_ref.at[depth, units]
                target = (outs[2] if near else in_weight).at[:, place]
            else:
                source = w_out_ref.at[units, depth]
                target = (outs[3] if near else out_weight).at[place, :]
            return pltpu.make_async_copy(
                source, target, sems.at[2 * int(near) + 1 - int(forth), j]
            )

        every = [(j, forth, near) for near in (False, True) for forth in (True, False) for j in range(steps)]
        for which in every:
            coming(*which).start()
        for k in range(2):
            rows_all[k * rows:(k + 1) * rows, :] = ins[k][:rows, :]

        @pl.loop(0, steps)
        def _(j):
            coming(j, True).wait()
            place = window(tile, j)
            outs[0][:, place] = dot(rows_all[...], in_weight[:, place], 1, 0)

        for k in range(2):
            rows_all[k * rows:(k + 1) * rows, :] = ins[k][rows:, :]

        @pl.loop(0, steps)
        def _(j):
            coming(j, False).wait()
            place = window(tile, j)
            outs[1][:, place] = dot(rows_all[...], out_weight[place, :], 1, 1)

        for which in every[2 * steps:]:
            coming(*which).wait()

    wide = array((tokens, hidden), jnp.float32)
    return run(
        body, groups,
        [wide, wide, array((half, hidden), kind), array((hidden, half), kind)],
        apart=(w_in, w_out),
        scratch=[
            pltpu.VMEM((tokens, half), kind),
            pltpu.VMEM((half, hidden), kind),
            pltpu.VMEM((hidden, half), kind),
            pltpu.SemaphoreType.DMA((4, steps)),
        ],
        after=after, limit=24,
    )


def finished(group, pairs, prior, after=()):
    tokens, half = group.shape
    rows, hidden, kind = tokens // 2, prior[0].shape[1], group.dtype
    tile = tile_of(hidden)
    piece = pairs[0].shape[0]
    each = rows // piece

    def body(ins, outs, scratch):
        pre_ref, back_act_ref, in_weight, out_weight = ins[1 + 2 * each:]
        rows_all, slope_ref = scratch

        def stack(below):
            rows_all[:rows, :] = ins[0][below * rows:(below + 1) * rows, :]
            for k in range(each):
                at = rows + k * piece
                rows_all[at:at + piece, :] = ins[1 + below * each + k][...]

        stack(0)

        @pl.loop(0, hidden // tile)
        def _(j):
            place = window(tile, j)
            pre = pre_ref[:, place] + dot(rows_all[...], in_weight[:, place], 1, 0)
            normal_cdf = 0.5 * (1.0 + lax.erf(pre * SQRT_HALF))
            density = INV_ROOT_TWO_PI * jnp.exp(-0.5 * pre * pre)
            outs[0][:tokens, place] = (pre * normal_cdf).astype(kind)
            slope_ref[:, place] = normal_cdf + pre * density

        stack(1)

        @pl.loop(0, hidden // tile)
        def _(j):
            place = window(tile, j)
            back_act = back_act_ref[:, place] + dot(rows_all[...], out_weight[place, :], 1, 1)
            outs[0][tokens:, place] = (back_act * slope_ref[:, place]).astype(kind)

    return run(
        body, (group, *pairs, *prior), [array((2 * tokens, hidden), kind)],
        [pltpu.VMEM((tokens, half), kind), pltpu.VMEM((tokens, hidden), jnp.float32)],
        after=after, limit=8,
    )[0]


def sums(both, near_weight, w_in, after=()):
    tokens, hidden = both.shape[0] // 2, both.shape[1]
    half, rows, kind = near_weight.shape[0], tokens // 2, both.dtype
    tile = tile_of(half)
    piece = rows // PIECES

    def body(ins, outs, scratch):
        far_weight, sem = scratch
        coming = pltpu.make_async_copy(
            ins[2].at[window(half, far_place()), window(hidden, pair_place())], far_weight, sem
        )
        coming.start()
        for weight, place in ((ins[1], near_place()), (far_weight, far_place())):
            first = place * (half // tile)
            if weight is far_weight:
                coming.wait()

            @pl.loop(0, half // tile)
            def _(j):
                columns = window(tile, first + j)
                term = dot(ins[0][tokens:, :], weight[window(tile, j), :], 1, 1)
                outs[0][:, columns] = term[:rows]
                for k in range(PIECES):
                    at = rows + k * piece
                    outs[1 + k][:, columns] = term[at:at + piece].astype(kind)

    return run(
        body, (both, near_weight),
        [array((rows, 2 * half), jnp.float32)] + [array((piece, 2 * half), kind)] * PIECES,
        [pltpu.VMEM((half, hidden), kind), pltpu.SemaphoreType.DMA],
        apart=(w_in,), after=after, limit=16,
    )


def joined(mine, others, far, near, gain, count, after=()):
    rows, width = mine.shape
    half = width // 2
    block = rows // count
    kind = others[0].dtype
    piece = rows // PIECES

    def body(ins, outs, scratch):
        mine_ref, others_ref, g_ref = ins[0], ins[1:1 + PIECES], ins[-1]
        for group_ref, place in ((ins[-3], far_place()), (ins[-2], near_place())):
            columns = window(half, place)
            total = jnp.zeros((1, half), jnp.float32)
            for k in range(PIECES):
                here = slice(k * piece, (k + 1) * piece)
                term = mine_ref[here, columns] + others_ref[k][:, columns].astype(jnp.float32)
                term = term.astype(kind)
                if count == PIECES:
                    outs[k][:, columns] = term
                else:
                    outs[0][here, columns] = term
                weighed = term.astype(jnp.float32) * group_ref[here, :].astype(jnp.float32)
                total = total + jnp.sum(weighed, 0, keepdims=True)
            outs[count][:, columns] = total / g_ref[:, columns]

    return run(
        body, (mine, *others, far, near, gain),
        [array((block, width), kind)] * count + [array((1, width), jnp.float32)],
        after=after,
    )


def added(mine, came, after=()):
    def body(ins, outs, scratch):
        came_here = jnp.where(on_end(), 0.0, ins[1][...].astype(jnp.float32))
        outs[0][...] = (ins[0][...].astype(jnp.float32) + came_here).astype(mine.dtype)

    return run(body, (mine, came), [array(mine.shape, mine.dtype)], after=after)[0]


def gradients(cut, full, after=()):
    tokens, part = full[0].shape[0] // 2, full[0].shape[1]
    rows, width, kind = tokens // 2, cut[0][0].shape[1] // 2, full[0].dtype
    tile = tile_of(2 * part)
    steps = 2 * part // tile
    names = [entry[0] for entry in cut]

    def body(ins, outs, scratch):
        a_all, b_all, wide, tall, in_sems, sems = scratch
        lo = pair_place()
        moves = [[], []]
        for which in range(2):
            at = 0
            for k, (_, first, count) in enumerate(cut):
                if first[which] is None:
                    continue
                source = ins[k].at[pl.ds(first[which], count), window(width, lo)]
                moves[which].append((source, a_all.at[which, pl.ds(at, count), :]))
                at += count
            for k in range(4):
                for half in range(2):
                    at = (k // 2 * 2 + (half if k % 2 == 0 else 1 - half)) * rows
                    place = window(part, lo if k % 2 == 0 else 1 - lo)
                    source = ins[len(cut) + k].at[pl.ds(which * tokens + half * rows, rows), :]
                    moves[which].append((source, b_all.at[which, pl.ds(at, rows), place]))
        copies = [
            [
                pltpu.make_async_copy(a, b, in_sems.at[which, k])
                for k, (a, b) in enumerate(moves[which])
            ]
            for which in range(2)
        ]
        for copy in [*copies[0], *copies[1]]:
            copy.start()

        for which in range(2):
            for copy in copies[which]:
                copy.wait()
            buffer = (tall, wide)[which]

            def leaving(j):
                place = window(tile, j)
                target = outs[1 + which].at[place, :] if which == 0 else outs[1 + which].at[:, place]
                return pltpu.make_async_copy(buffer.at[j % 2], target, sems.at[which, j % 2])

            @pl.loop(0, steps)
            def _(j):
                place = window(tile, j)
                if which == 0:
                    result = dot(b_all[0, :, place], a_all[0], 0, 0)
                else:
                    result = dot(a_all[1], b_all[1, :, place], 0, 0)

                @pl.when(j >= 2)
                def _():
                    leaving(j - 2).wait()

                buffer[j % 2] = result.astype(kind)
                leaving(j).start()

            if which == 1:
                for k in range(2):
                    buffer = (tall, wide)[k]
                    for j in range(max(steps - 2, 0), steps):
                        place = window(tile, j)
                        target = outs[1 + k].at[place, :] if k == 0 else outs[1 + k].at[:, place]
                        pltpu.make_async_copy(
                            buffer.at[j % 2], target, sems.at[k, j % 2]
                        ).wait()
        outs[0][...] = jnp.zeros_like(outs[0])

    return run(
        body, (), [array((8, 128), jnp.float32)],
        out_apart=[array((2 * part, width), kind), array((width, 2 * part), kind)],
        apart=[*names, *full],
        scratch=[
            pltpu.VMEM((2, 4 * rows, width), kind),
            pltpu.VMEM((2, 4 * rows, 2 * part), kind),
            pltpu.VMEM((2, width, tile), kind),
            pltpu.VMEM((2, tile, width), kind),
            pltpu.SemaphoreType.DMA((2, len(cut) + 8)),
            pltpu.SemaphoreType.DMA((2, 2)),
        ],
        after=after, limit=24,
    )


def total(parts, after=()):
    def body(ins, outs, scratch):
        sums = [part[...] for part in ins]
        while len(sums) > 1:
            sums = [sums[k] + sums[k + 1] for k in range(0, len(sums), 2)]
        outs[0][...] = sums[0]

    return run(body, parts, [array(parts[0].shape, parts[0].dtype)], after=after)[0]


def own_error_of(x, e, gain, terms, after=()):
    def body(ins, outs, scratch):
        x_ref, e_ref, g_ref = ins[:3]
        total = ins[3][...].astype(jnp.float32)
        for term in ins[4:6]:
            total = total + term[...].astype(jnp.float32)
        for term in ins[6:]:
            total = total + jnp.where(on_end(), term[...].astype(jnp.float32), 0.0)
        scaled = total * g_ref[...]
        centred, inverse = normalised(x_ref)
        corrected = inverse * (
            scaled
            - jnp.mean(scaled, -1, keepdims=True)
            - centred * jnp.mean(scaled * centred, -1, keepdims=True)
        )
        outs[0][...] = (e_ref[...].astype(jnp.float32) + corrected).astype(x.dtype)

    return run(body, (x, e, gain, *terms), [array(x.shape, x.dtype)], after=after)[0]


def swapped(block, axis, mask):
    return lax.ppermute(block, axis, [(i, i ^ mask) for i in range(lax.axis_size(axis))])


def pair(block):
    return swapped(block, "dp", 1)


def across(block):
    return swapped(block, "dp", 2)


def summed(value, axis):
    size = lax.axis_size(axis)
    if size & (size - 1):
        return lax.psum(value, axis)
    mask = 1
    while mask < size:
        value = value + swapped(value, axis, mask)
        mask *= 2
    return value


RELAY = [(0, 2), (3, 1), (2, 3), (1, 0)]
RELAY_BACK = [(b, a) for a, b in RELAY]


def gathered(chunk):
    return [
        lax.all_gather(chunk, "shard", axis=0)[k] for k in range(lax.axis_size("shard"))
    ]


def per_device(features, delayed_error, ln_gain, w_in, w_out):
    x, e, w_in, w_out = features[0], delayed_error[0], w_in[0], w_out[0]
    line = lax.axis_size("shard") == 4

    own, own_far = tokens_of(x, e, ln_gain)
    if line:
        first, third = swapped(own, "shard", 1), swapped(own, "shard", 3)
        own_across = across(own_far)
        passing_far, passing_near = passed_on(own, third, after=(own_across,))
        second_far = lax.ppermute(passing_far, "shard", RELAY)
        second_near = lax.ppermute(passing_near, "shard", RELAY)
        first_across = across(far_of(first))
        blocks = [own, first, second_far, third]
        far, rest_far = grouped(blocks, False, apart=(2, 3), after=(first_across,))
        rest_across = across(rest_far)
        blocks = [own, first, second_near, third]
        tie = (rest_across,)
    else:
        blocks = gathered(own)
        (far,) = grouped(blocks, False)
        far_across = across(far)
        tie = ()
    far_pair = pair(far)
    prior = forth_and_back((far, far_pair), w_in, w_out)
    near, *pieces = grouped(blocks, True, pieces=PIECES, after=(prior[0],))
    pairs = [pair(piece) for piece in pieces]
    both = finished(near, pairs, prior, after=tie)
    both_across = across(both)
    both_pair = pair(both)
    mine, *others = sums(both, prior[2], w_in)
    if line:
        far_across = regrouped((own_across, first_across, rest_across), after=(others[0],))
    count = PIECES if line else 1
    *terms, gain_grad = joined(
        mine, [pair(other) for other in others], far, near, ln_gain, count
    )
    if line:
        own_terms, first_terms, second_terms, third_terms = terms
        second_terms = lax.ppermute(second_terms, "shard", RELAY_BACK)
        first_terms = swapped(first_terms, "shard", 1)
        passing = added(third_terms, second_terms, after=(both_pair,))
        tie = (passing,)
        terms = [own_terms, first_terms, swapped(passing, "shard", 3), second_terms]
        tie = (terms[1], terms[2])
        far_across = held(far_across, (passing,))
        gain_grad = held(gain_grad, (passing,))
    else:
        terms = [lax.psum_scatter(terms[0], "shard", scatter_dimension=0, tiled=True)]
    far_across_pair = pair(far_across)
    both_across = held(both_across, tie)
    both_across_pair = pair(both_across)
    own_error = own_error_of(x, e, ln_gain, terms, after=(both_across,))
    n_section = lax.axis_size("section")
    passed = lax.ppermute(
        own_error, "section", [((i + 1) % n_section, i) for i in range(n_section)]
    )
    gain_grad = held(summed(gain_grad, "dp"), (own_error,))
    if line:
        gain_parts = [gain_grad] + [swapped(gain_grad, "shard", mask) for mask in (1, 2, 3)]
    else:
        gain_parts = [summed(gain_grad, "shard")]

    tokens = both.shape[0] // 2
    rows = tokens // 2
    piece = pairs[0].shape[0]
    each = rows // piece
    cut = [(near, (rows, 0), rows)]
    cut += [(pairs[k], (None, 0) if k < each else (0, None), piece) for k in range(PIECES)]
    cut += [(far_across, (rows, 0), rows), (far_across_pair, (rows, 0), rows)]
    token, w_out_grad, w_in_grad = gradients(
        cut, (both, both_pair, both_across, both_across_pair), after=(own_error,)
    )
    gain_grad = total(gain_parts, after=(token,))
    return passed[None], gain_grad, w_in_grad[None], w_out_grad[None]


def solution(mesh):
    return jax.shard_map(
        per_device,
        mesh=mesh,
        in_specs=(
            P("section", ("dp", "shard"), None),
            P("section", ("dp", "shard"), None),
            P("section", None),
            P("section", None, "shard"),
            P("section", "shard", None),
        ),
        out_specs=(
            P("section", ("dp", "shard"), None),
            P("section", None),
            P("section", "dp", "shard"),
            P("section", "shard", "dp"),
        ),
        check_vma=False,
    )
```

time: 379 us -> 165 us (0.44)
  waiting for transfers between devices: 164 us -> 63.8 us
  matrix products: 90.8 us -> 0 us
  blocking collectives: 60.3 us -> 0 us
  Pallas kernels: 0 us -> 48.9 us
  other arithmetic: 44.3 us -> 0.05 us
  starting transfers between devices: 1.83 us -> 42.3 us
  between operations: 14.2 us -> 0.85 us
  local copies, waits for them, and re-layouts: 3.79 us -> 9.32 us
    all_gather x6 -> x0, waiting for transfers between devices: 129 us -> none  [the longest x1 39.1 us: per_device(): lax.all_gather(normed, 'shard', axis=0, tiled=True)]
    dot_general x5 -> x0, matrix products: 90.8 us -> none  [the longest x1 19.6 us: per_device(): jnp.einsum('kta,ktf->kaf', piece_normed, piece_pre, preferred_element_typ...]
    ppermute x1 -> x29, waiting for transfers between devices: 0.01 us -> 63.8 us  [the longest x25 45.1 us: swapped(): lax.ppermute(block, axis, [(i, i ^ mask) for i in range(lax.axis_size(axi...]
    psum x1 -> x0, blocking collectives: 60.3 us -> none  [per_device(): gain_grad = lax.psum(jnp.sum(norm_error * centred, 0), ('dp', 'shard'))]
    pallas_call x0 -> x18, Pallas kernels: none -> 48.9 us  [run(): pl.pallas_call(kernel, out_shape=[*outputs, *out_apart], in_specs=[near]...]
    reduce_sum x5 -> x0, other arithmetic: 41 us -> none  [the longest x1 18.6 us: per_device(): out_total = jnp.sum(rounded(out_terms), 0)]
    ppermute x1 -> x29, starting transfers between devices: 1.56 us -> 42.3 us  [the longest x25 22.3 us: swapped(): lax.ppermute(block, axis, [(i, i ^ mask) for i in range(lax.axis_size(axi...]
    reduce_scatter x1 -> x0, waiting for transfers between devices: 31.8 us -> none  [per_device(): lax.psum_scatter(jnp.einsum('tf,df->td', pre_error, in_block, preferred_e...]
  transfers between devices with their start and end apart: 8 -> 29, of which waited for: 6 -> 18; matrix products, arithmetic and copies ran while one was open for 11% -> 0% of each run, Pallas kernels for 0% -> 24%
where the time goes in v2:
time: 165 us
  waiting for transfers between devices  63.8 us (39%)
  Pallas kernels  48.9 us (30%)
  starting transfers between devices  42.3 us (26%)
  local copies, waits for them, and re-layouts  9.32 us (6%)
    pallas_call x18, Pallas kernels, run(): pl.pallas_call(kernel, out_shape=[*outputs, *out_apart], in_specs=[near]...  48.9 us
    ppermute x25, waiting for transfers between devices, swapped(): lax.ppermute(block, axis, [(i, i ^ mask) for i in range(lax.axis_size(axi...  45.1 us
    ppermute x25, starting transfers between devices, swapped(): lax.ppermute(block, axis, [(i, i ^ mask) for i in range(lax.axis_size(axi...  22.3 us
    ppermute x1, starting transfers between devices, per_device(): second_far = lax.ppermute(passing_far, 'shard', RELAY)  16.7 us
    ppermute x1, waiting for transfers between devices, per_device(): second_terms = lax.ppermute(second_terms, 'shard', RELAY_BACK)  10.1 us
    unnamed x15, local copies, waits for them, and re-layouts  9.32 us
    ppermute x1, waiting for transfers between devices, per_device(): second_far = lax.ppermute(passing_far, 'shard', RELAY)  5.91 us
  transfers between devices with their start and end apart: 29, of which 18 were waited for; matrix products, arithmetic and copies ran while one was open for 0% of the time, Pallas kernels for 24%

profile of v2, /device:TPU:0, one launch (start us, length us, event | category | flops | bytes accessed | tf_op | source)
XLA Modules:
  0.0 165.1 jit_solution(15874021125940866770)
XLA Ops:
  0.6 2.6 %shard_map.84 = (bf16[64,6144]{1,0:T(8,128)(2,1)}, bf16[64,3072]{1,0:T(8,128)(2,1)}) custom-call(bf16[32,6144]{1,0:T(8,128)(2,1)} %bitcast.7, bf16[32,6144]{1,0:T(8,128)(2,1)} %bitcast.9, f32[1,6144]{1,0:T(1,128)} %refs_2_.3), custom_call_target="tpu_custom_call" | custom-call | flops 1000 | bytes 1000 | tf_op jit(solution)/shard_map/pallas_call | solution.py:55
  3.2 5.1 %collective-permute-start.1 = (bf16[64,6144]{1,0:T(8,128)(2,1)}, bf16[64,6144]{1,0:T(8,128)(2,1)S(1)}, u32[]{:S(2)}, u32[]{:S(2)}) collective-permute-start(bf16[64,6144]{1,0:T(8,128)(2,1)} %get-tuple-element.32.refs_0_), channel_id=1, source_target_pairs={{0,3},{1,2},{2,1},{3,0},{4,7},{5,6},{6,5},{7,4},{8,11},{9,10},{10,... | collective-permute-start | bytes 2359304 | tf_op jit(solution)/shard_map/ppermute | solution.py:483
  8.3 1.5 collective-permute-start.2
  9.8 9.3 %collective-permute-done.2.refs_2_.refs_0_ = bf16[64,3072]{1,0:T(8,128)(2,1)S(1)} collective-permute-done((bf16[64,3072]{1,0:T(8,128)(2,1)}, bf16[64,3072]{1,0:T(8,128)(2,1)S(1)}, u32[]{:S(2)}, u32[]{:S(2)}) %collective-permute-start.2) | collective-permute-done | bytes 393248 | tf_op jit(solution)/shard_map/ppermute | solution.py:483
  19.1 7.9 %collective-permute-done.1.refs_1_.refs_3_ = bf16[64,6144]{1,0:T(8,128)(2,1)S(1)} collective-permute-done((bf16[64,6144]{1,0:T(8,128)(2,1)}, bf16[64,6144]{1,0:T(8,128)(2,1)S(1)}, u32[]{:S(2)}, u32[]{:S(2)}) %collective-permute-start.1) | collective-permute-done | bytes 786464 | tf_op jit(solution)/shard_map/ppermute | solution.py:483
  27.0 1.1 copy-done.2
  28.2 16.7 %collective-permute-start.4 = (bf16[64,3072]{1,0:T(8,128)(2,1)S(1)}, bf16[64,3072]{1,0:T(8,128)(2,1)S(1)}, u32[]{:S(2)}, u32[]{:S(2)}) collective-permute-start(bf16[64,3072]{1,0:T(8,128)(2,1)S(1)} %get-tuple-element.35), channel_id=1, source_target_pairs={{0,2},{3,1},{2,3},{1,0},{4,6},{7,5},{6,7},{5,4},{8,10},{11,9},{10,... | collective-permute-start | bytes 1179656 | tf_op jit(solution)/shard_map/ppermute | solution.py:524
  45.0 1.6 collective-permute-start.5
  46.5 5.9 %collective-permute-done.4.refs_2_ = bf16[64,3072]{1,0:T(8,128)(2,1)S(1)} collective-permute-done((bf16[64,3072]{1,0:T(8,128)(2,1)S(1)}, bf16[64,3072]{1,0:T(8,128)(2,1)S(1)}, u32[]{:S(2)}, u32[]{:S(2)}) %collective-permute-start.4) | collective-permute-done | bytes 393248 | tf_op jit(solution)/shard_map/ppermute | solution.py:524
  52.4 2.3 %collective-permute-done.5.refs_4_.refs_1_ = bf16[64,3072]{1,0:T(8,128)(2,1)S(1)} collective-permute-done((bf16[64,3072]{1,0:T(8,128)(2,1)S(1)}, bf16[64,3072]{1,0:T(8,128)(2,1)S(1)}, u32[]{:S(2)}, u32[]{:S(2)}) %collective-permute-start.5) | collective-permute-done | bytes 393248 | tf_op jit(solution)/shard_map/ppermute | solution.py:483
  55.0 1.1 collective-permute-start.3
  56.1 1.5 collective-permute-start.11
  58.4 12.3 %shard_map.88 = (f32[256,1536]{1,0:T(8,128)S(1)}, f32[256,1536]{1,0:T(8,128)S(1)}, bf16[3072,1536]{1,0:T(8,128)(2,1)S(1)}, bf16[1536,3072]{1,0:T(8,128)(2,1)S(1)}) custom-call(bf16[256,3072]{1,0:T(8,128)(2,1)S(1)} %get-tuple-element.36.refs_0_.refs_5_, bf16[256,3072]{1,0:T(8,128)(2,1)S(1)} %collective-permute-done.6.refs_1_, bf16[6144,3072]{1,0:T(8,128)(2,1)} %bitcast.11, ...), custom_call_target="tpu_custom_call" | custom-call | flops 1000 | bytes 1000 | tf_op jit(solution)/shard_map/pallas_call | solution.py:55
  70.7 3.7 %copy-done = bf16[1536,3072]{1,0:T(8,128)(2,1)} copy-done((bf16[1536,3072]{1,0:T(8,128)(2,1)}, bf16[1536,3072]{1,0:T(8,128)(2,1)S(1)}, u32[]{:S(2)}) %copy-start) | copy-done | bytes 9437208
  78.2 3.7 %copy-done.1 = bf16[1536,3072]{1,0:T(8,128)(2,1)S(1)} copy-done((bf16[1536,3072]{1,0:T(8,128)(2,1)S(1)}, bf16[1536,3072]{1,0:T(8,128)(2,1)}, u32[]{:S(2)}) %copy-start.1) | copy-done | bytes 9437208
  81.8 6.7 %shard_map.90.refs_0_.refs_7_ = bf16[512,1536]{1,0:T(8,128)(2,1)S(1)} custom-call(bf16[256,3072]{1,0:T(8,128)(2,1)S(1)} %get-tuple-element.38.refs_0_.refs_6_, bf16[64,3072]{1,0:T(8,128)(2,1)S(1)} %collective-permute-done.7.refs_1_, bf16[64,3072]{1,0:T(8,128)(2,1)S(1)} %collective-permute-done.8.refs_2_, ...), custom_call_target="tpu_custom_call" | custom-call | flops 1000 | bytes 1000 | tf_op jit(solution)/shard_map/pallas_call | solution.py:55
  88.7 7.4 %shard_map.91 = (f32[128,6144]{1,0:T(8,128)S(1)}, bf16[32,6144]{1,0:T(8,128)(2,1)S(1)}, bf16[32,6144]{1,0:T(8,128)(2,1)S(1)}, bf16[32,6144]{1,0:T(8,128)(2,1)S(1)}, bf16[32,6144]{1,0:T(8,128)(2,1)S(1)}) custom-call(bf16[512,1536]{1,0:T(8,128)(2,1)S(1)} %shard_map.90.refs_0_.refs_7_, bf16[3072,1536]{1,0:T(8,128)(2,1)S(1)} %get-tuple-element.44.refs_7_.refs_1_, ...), custom_call_target="tpu_custom_call" | custom-call | flops 1000 | bytes 1000 | tf_op jit(solution)/shard_map/pallas_call | solution.py:55
  96.5 1.5 collective-permute-start.20
  98.5 1.2 collective-permute-done.13.refs_2_
  100.9 1.0 shard_map.92
  102.3 1.8 %collective-permute-start.16 = (bf16[32,6144]{1,0:T(8,128)(2,1)S(1)}, bf16[32,6144]{1,0:T(8,128)(2,1)S(1)}, u32[]{:S(2)}, u32[]{:S(2)}) collective-permute-start(bf16[32,6144]{1,0:T(8,128)(2,1)S(1)} %get-tuple-element.53), channel_id=1, source_target_pairs={{0,1},{1,0},{2,3},{3,2},{4,5},{5,4},{6,7},{7,6},{8,9},{9,8},{10,11... | collective-permute-start | bytes 1179656 | tf_op jit(solution)/shard_map/ppermute | solution.py:483
  104.2 10.1 %collective-permute-done.17.refs_1_.refs_6_ = bf16[32,6144]{1,0:T(8,128)(2,1)S(1)} collective-permute-done((bf16[32,6144]{1,0:T(8,128)(2,1)S(1)}, bf16[32,6144]{1,0:T(8,128)(2,1)S(1)}, u32[]{:S(2)}, u32[]{:S(2)}) %collective-permute-start.17) | collective-permute-done | bytes 393248 | tf_op jit(solution)/shard_map/ppermute | solution.py:553
  114.4 1.6 collective-permute-start.19
  116.3 5.8 %collective-permute-done.16.refs_1_.refs_4_ = bf16[32,6144]{1,0:T(8,128)(2,1)S(1)} collective-permute-done((bf16[32,6144]{1,0:T(8,128)(2,1)S(1)}, bf16[32,6144]{1,0:T(8,128)(2,1)S(1)}, u32[]{:S(2)}, u32[]{:S(2)}) %collective-permute-start.16) | collective-permute-done | bytes 393248 | tf_op jit(solution)/shard_map/ppermute | solution.py:483
  122.1 10.9 %collective-permute-done.20.refs_0_ = bf16[512,1536]{1,0:T(8,128)(2,1)S(1)} collective-permute-done((bf16[512,1536]{1,0:T(8,128)(2,1)S(1)}, bf16[512,1536]{1,0:T(8,128)(2,1)S(1)}, u32[]{:S(2)}, u32[]{:S(2)}) %collective-permute-start.20) | collective-permute-done | bytes 1572896 | tf_op jit(solution)/shard_map/ppermute | solution.py:483
  134.2 1.6 collective-permute-start.21
  137.0 1.5 collective-permute-start.23
  138.5 2.4 %collective-permute-done.23 = f32[1,6144]{1,0:T(1,128)S(1)} collective-permute-done((f32[1,6144]{1,0:T(1,128)S(1)}, f32[1,6144]{1,0:T(1,128)S(1)}, u32[]{:S(2)}, u32[]{:S(2)}) %collective-permute-start.23) | collective-permute-done | bytes 24608 | tf_op jit(solution)/shard_map/ppermute | solution.py:483
  141.3 1.8 %collective-permute-start.25 = (f32[1,6144]{1,0:T(1,128)S(1)}, f32[1,6144]{1,0:T(1,128)S(1)}, u32[]{:S(2)}, u32[]{:S(2)}) collective-permute-start(f32[1,6144]{1,0:T(1,128)S(1)} %shard_map.97.refs_0_), channel_id=1, source_target_pairs={{0,2},{1,3},{2,0},{3,1},{4,6},{5,7},{6,4},{7,5},{8,10},{9,11},{10,... | collective-permute-start | bytes 73736 | tf_op jit(solution)/shard_map/ppermute | solution.py:483
  143.1 2.7 %collective-permute-done.21 = bf16[32,6144]{1,0:T(8,128)(2,1)S(1)} collective-permute-done((bf16[32,6144]{1,0:T(8,128)(2,1)S(1)}, bf16[32,6144]{1,0:T(8,128)(2,1)S(1)}, u32[]{:S(2)}, u32[]{:S(2)}) %collective-permute-start.21) | collective-permute-done | bytes 393248 | tf_op jit(solution)/shard_map/ppermute | solution.py:568
  145.8 1.5 collective-permute-start.26
  147.3 16.4 %shard_map.100 = (f32[8,128]{1,0:T(8,128)S(1)}, bf16[3072,1536]{1,0:T(8,128)(2,1)}, bf16[1536,3072]{1,0:T(8,128)(2,1)}) custom-call(bf16[256,3072]{1,0:T(8,128)(2,1)S(1)} %get-tuple-element.38.refs_0_.refs_6_, bf16[64,3072]{1,0:T(8,128)(2,1)S(1)} %collective-permute-done.7.refs_1_, bf16[64,3072]{1,0:T(8,128)(2,1)S(1)} %collective-permute-done.8.refs_2_, ...), custom_call_target="tpu_custom_call" | custom-call | flops 1000 | bytes 1000 | tf_op jit(solution)/shard_map/pallas_call | solution.py:55
  (61 shorter events, 12.1 us)
Async XLA Ops:
  3.2 23.8 %collective-permute-start.1 = (bf16[64,6144]{1,0:T(8,128)(2,1)}, bf16[64,6144]{1,0:T(8,128)(2,1)S(1)}, u32[]{:S(2)}, u32[]{:S(2)}) collective-permute-start(bf16[64,6144]{1,0:T(8,128)(2,1)} %get-tuple-element.32.refs_0_), channel_id=1, source_target_pairs={{0,3},{1,2},{2,1},{3,0},{4,7},{5,6},{6,5},{7,4},{8,11},{9,10},{10,... | collective-permute-start | bytes 2359304 | tf_op jit(solution)/shard_map/ppermute | solution.py:483
  8.3 36.6 %collective-permute-start = (bf16[64,6144]{1,0:T(8,128)(2,1)}, bf16[64,6144]{1,0:T(8,128)(2,1)S(1)}, u32[]{:S(2)}, u32[]{:S(2)}) collective-permute-start(bf16[64,6144]{1,0:T(8,128)(2,1)} %get-tuple-element.32.refs_0_), channel_id=1, source_target_pairs={{0,1},{1,0},{2,3},{3,2},{4,5},{5,4},{6,7},{7,6},{8,9},{9,8},{10,11... | collective-permute-start | bytes 2359304 | tf_op jit(solution)/shard_map/ppermute | solution.py:483
  8.3 10.8 %collective-permute-start.2 = (bf16[64,3072]{1,0:T(8,128)(2,1)}, bf16[64,3072]{1,0:T(8,128)(2,1)S(1)}, u32[]{:S(2)}, u32[]{:S(2)}) collective-permute-start(bf16[64,3072]{1,0:T(8,128)(2,1)} %get-tuple-element.33), channel_id=1, source_target_pairs={{0,8},{4,12},{8,0},{12,4},{1,9},{5,13},{9,1},{13,5},{2,10},{6,14},... | collective-permute-start | bytes 1179656 | tf_op jit(solution)/shard_map/ppermute | solution.py:483
  28.1 26.6 %copy-start.3 = (bf16[64,6144]{1,0:T(8,128)(2,1)S(1)}, bf16[64,6144]{1,0:T(8,128)(2,1)}, u32[]{:S(2)}) copy-start(bf16[64,6144]{1,0:T(8,128)(2,1)} %get-tuple-element.32.refs_0_) | copy-start | bytes 2359300
  28.2 24.2 %collective-permute-start.4 = (bf16[64,3072]{1,0:T(8,128)(2,1)S(1)}, bf16[64,3072]{1,0:T(8,128)(2,1)S(1)}, u32[]{:S(2)}, u32[]{:S(2)}) collective-permute-start(bf16[64,3072]{1,0:T(8,128)(2,1)S(1)} %get-tuple-element.35), channel_id=1, source_target_pairs={{0,2},{3,1},{2,3},{1,0},{4,6},{7,5},{6,7},{5,4},{8,10},{11,9},{10,... | collective-permute-start | bytes 1179656 | tf_op jit(solution)/shard_map/ppermute | solution.py:524
  45.0 9.8 %collective-permute-start.5 = (bf16[64,3072]{1,0:T(8,128)(2,1)S(1)}, bf16[64,3072]{1,0:T(8,128)(2,1)S(1)}, u32[]{:S(2)}, u32[]{:S(2)}) collective-permute-start(bf16[64,3072]{1,0:T(8,128)(2,1)S(1)} %shard_map.86), channel_id=1, source_target_pairs={{0,8},{4,12},{8,0},{12,4},{1,9},{5,13},{9,1},{13,5},{2,10},{6,14},... | collective-permute-start | bytes 1179656 | tf_op jit(solution)/shard_map/ppermute | solution.py:483
  54.9 3.5 %collective-permute-start.6 = (bf16[256,3072]{1,0:T(8,128)(2,1)S(1)}, bf16[256,3072]{1,0:T(8,128)(2,1)S(1)}, u32[]{:S(2)}, u32[]{:S(2)}) collective-permute-start(bf16[256,3072]{1,0:T(8,128)(2,1)S(1)} %get-tuple-element.36.refs_0_.refs_5_), channel_id=1, source_target_pairs={{0,4},{4,0},{8,12},{12,8},{1,5},{5,1},{9,13},{13,9},{2,6},{6,2},{1... | collective-permute-start | bytes 4718600 | tf_op jit(solution)/shard_map/ppermute | solution.py:483
  55.0 19.5 %collective-permute-start.3 = (bf16[64,3072]{1,0:T(8,128)(2,1)S(1)}, bf16[64,3072]{1,0:T(8,128)(2,1)S(1)}, u32[]{:S(2)}, u32[]{:S(2)}) collective-permute-start(bf16[64,3072]{1,0:T(8,128)(2,1)S(1)} %get-tuple-element.34), channel_id=1, source_target_pairs={{0,2},{3,1},{2,3},{1,0},{4,6},{7,5},{6,7},{5,4},{8,10},{11,9},{10,... | collective-permute-start | bytes 1179656 | tf_op jit(solution)/shard_map/ppermute | solution.py:525
  56.1 19.6 %collective-permute-start.11 = (bf16[128,3072]{1,0:T(8,128)(2,1)S(1)}, bf16[128,3072]{1,0:T(8,128)(2,1)S(1)}, u32[]{:S(2)}, u32[]{:S(2)}) collective-permute-start(bf16[128,3072]{1,0:T(8,128)(2,1)S(1)} %get-tuple-element.46), channel_id=1, source_target_pairs={{0,8},{4,12},{8,0},{12,4},{1,9},{5,13},{9,1},{13,5},{2,10},{6,14},... | collective-permute-start | bytes 2359304 | tf_op jit(solution)/shard_map/ppermute | solution.py:483
  74.7 1.8 %collective-permute-start.10 = (bf16[64,3072]{1,0:T(8,128)(2,1)S(1)}, bf16[64,3072]{1,0:T(8,128)(2,1)S(1)}, u32[]{:S(2)}, u32[]{:S(2)}) collective-permute-start(bf16[64,3072]{1,0:T(8,128)(2,1)S(1)} %get-tuple-element.42), channel_id=1, source_target_pairs={{0,4},{4,0},{8,12},{12,8},{1,5},{5,1},{9,13},{13,9},{2,6},{6,2},{1... | collective-permute-start | bytes 1179656 | tf_op jit(solution)/shard_map/ppermute | solution.py:483
  74.8 2.2 %collective-permute-start.7 = (bf16[64,3072]{1,0:T(8,128)(2,1)S(1)}, bf16[64,3072]{1,0:T(8,128)(2,1)S(1)}, u32[]{:S(2)}, u32[]{:S(2)}) collective-permute-start(bf16[64,3072]{1,0:T(8,128)(2,1)S(1)} %get-tuple-element.39), channel_id=1, source_target_pairs={{0,4},{4,0},{8,12},{12,8},{1,5},{5,1},{9,13},{13,9},{2,6},{6,2},{1... | collective-permute-start | bytes 1179656 | tf_op jit(solution)/shard_map/ppermute | solution.py:483
  75.3 2.3 %collective-permute-start.8 = (bf16[64,3072]{1,0:T(8,128)(2,1)S(1)}, bf16[64,3072]{1,0:T(8,128)(2,1)S(1)}, u32[]{:S(2)}, u32[]{:S(2)}) collective-permute-start(bf16[64,3072]{1,0:T(8,128)(2,1)S(1)} %get-tuple-element.40), channel_id=1, source_target_pairs={{0,4},{4,0},{8,12},{12,8},{1,5},{5,1},{9,13},{13,9},{2,6},{6,2},{1... | collective-permute-start | bytes 1179656 | tf_op jit(solution)/shard_map/ppermute | solution.py:483
  75.4 2.8 %collective-permute-start.9 = (bf16[64,3072]{1,0:T(8,128)(2,1)S(1)}, bf16[64,3072]{1,0:T(8,128)(2,1)S(1)}, u32[]{:S(2)}, u32[]{:S(2)}) collective-permute-start(bf16[64,3072]{1,0:T(8,128)(2,1)S(1)} %get-tuple-element.41), channel_id=1, source_target_pairs={{0,4},{4,0},{8,12},{12,8},{1,5},{5,1},{9,13},{13,9},{2,6},{6,2},{1... | collective-permute-start | bytes 1179656 | tf_op jit(solution)/shard_map/ppermute | solution.py:483
  88.5 25.7 %collective-permute-start.18 = (bf16[512,1536]{1,0:T(8,128)(2,1)S(1)}, bf16[512,1536]{1,0:T(8,128)(2,1)S(1)}, u32[]{:S(2)}, u32[]{:S(2)}) collective-permute-start(bf16[512,1536]{1,0:T(8,128)(2,1)S(1)} %shard_map.90.refs_0_.refs_7_), channel_id=1, source_target_pairs={{0,4},{4,0},{8,12},{12,8},{1,5},{5,1},{9,13},{13,9},{2,6},{6,2},{1... | collective-permute-start | bytes 4718600 | tf_op jit(solution)/shard_map/ppermute | solution.py:483
  96.2 2.4 %collective-permute-start.12 = (bf16[32,6144]{1,0:T(8,128)(2,1)S(1)}, bf16[32,6144]{1,0:T(8,128)(2,1)S(1)}, u32[]{:S(2)}, u32[]{:S(2)}) collective-permute-start(bf16[32,6144]{1,0:T(8,128)(2,1)S(1)} %get-tuple-element.48.refs_3_), channel_id=1, source_target_pairs={{0,4},{4,0},{8,12},{12,8},{1,5},{5,1},{9,13},{13,9},{2,6},{6,2},{1... | collective-permute-start | bytes 1179656 | tf_op jit(solution)/shard_map/ppermute | solution.py:483
  96.5 36.5 %collective-permute-start.20 = (bf16[512,1536]{1,0:T(8,128)(2,1)S(1)}, bf16[512,1536]{1,0:T(8,128)(2,1)S(1)}, u32[]{:S(2)}, u32[]{:S(2)}) collective-permute-start(bf16[512,1536]{1,0:T(8,128)(2,1)S(1)} %shard_map.90.refs_0_.refs_7_), channel_id=1, source_target_pairs={{0,8},{4,12},{8,0},{12,4},{1,9},{5,13},{9,1},{13,5},{2,10},{6,14},... | collective-permute-start | bytes 4718600 | tf_op jit(solution)/shard_map/ppermute | solution.py:483
  98.0 1.7 %collective-permute-start.13 = (bf16[32,6144]{1,0:T(8,128)(2,1)S(1)}, bf16[32,6144]{1,0:T(8,128)(2,1)S(1)}, u32[]{:S(2)}, u32[]{:S(2)}) collective-permute-start(bf16[32,6144]{1,0:T(8,128)(2,1)S(1)} %get-tuple-element.49), channel_id=1, source_target_pairs={{0,4},{4,0},{8,12},{12,8},{1,5},{5,1},{9,13},{13,9},{2,6},{6,2},{1... | collective-permute-start | bytes 1179656 | tf_op jit(solution)/shard_map/ppermute | solution.py:483
  98.0 2.3 %collective-permute-start.14 = (bf16[32,6144]{1,0:T(8,128)(2,1)S(1)}, bf16[32,6144]{1,0:T(8,128)(2,1)S(1)}, u32[]{:S(2)}, u32[]{:S(2)}) collective-permute-start(bf16[32,6144]{1,0:T(8,128)(2,1)S(1)} %get-tuple-element.50), channel_id=1, source_target_pairs={{0,4},{4,0},{8,12},{12,8},{1,5},{5,1},{9,13},{13,9},{2,6},{6,2},{1... | collective-permute-start | bytes 1179656 | tf_op jit(solution)/shard_map/ppermute | solution.py:483
  98.5 2.3 %collective-permute-start.15 = (bf16[32,6144]{1,0:T(8,128)(2,1)S(1)}, bf16[32,6144]{1,0:T(8,128)(2,1)S(1)}, u32[]{:S(2)}, u32[]{:S(2)}) collective-permute-start(bf16[32,6144]{1,0:T(8,128)(2,1)S(1)} %get-tuple-element.51), channel_id=1, source_target_pairs={{0,4},{4,0},{8,12},{12,8},{1,5},{5,1},{9,13},{13,9},{2,6},{6,2},{1... | collective-permute-start | bytes 1179656 | tf_op jit(solution)/shard_map/ppermute | solution.py:483
  101.8 12.4 %collective-permute-start.17 = (bf16[32,6144]{1,0:T(8,128)(2,1)S(1)}, bf16[32,6144]{1,0:T(8,128)(2,1)S(1)}, u32[]{:S(2)}, u32[]{:S(2)}) collective-permute-start(bf16[32,6144]{1,0:T(8,128)(2,1)S(1)} %get-tuple-element.55), channel_id=1, source_target_pairs={{2,0},{1,3},{3,2},{0,1},{6,4},{5,7},{7,6},{4,5},{10,8},{9,11},{11,... | collective-permute-start | bytes 1179656 | tf_op jit(solution)/shard_map/ppermute | solution.py:553
  102.3 19.8 %collective-permute-start.16 = (bf16[32,6144]{1,0:T(8,128)(2,1)S(1)}, bf16[32,6144]{1,0:T(8,128)(2,1)S(1)}, u32[]{:S(2)}, u32[]{:S(2)}) collective-permute-start(bf16[32,6144]{1,0:T(8,128)(2,1)S(1)} %get-tuple-element.53), channel_id=1, source_target_pairs={{0,1},{1,0},{2,3},{3,2},{4,5},{5,4},{6,7},{7,6},{8,9},{9,8},{10,11... | collective-permute-start | bytes 1179656 | tf_op jit(solution)/shard_map/ppermute | solution.py:483
  114.4 18.7 %collective-permute-start.19 = (bf16[32,6144]{1,0:T(8,128)(2,1)S(1)}, bf16[32,6144]{1,0:T(8,128)(2,1)S(1)}, u32[]{:S(2)}, u32[]{:S(2)}) collective-permute-start(bf16[32,6144]{1,0:T(8,128)(2,1)S(1)} %shard_map.93.refs_1_), channel_id=1, source_target_pairs={{0,3},{1,2},{2,1},{3,0},{4,7},{5,6},{6,5},{7,4},{8,11},{9,10},{10,... | collective-permute-start | bytes 1179656 | tf_op jit(solution)/shard_map/ppermute | solution.py:483
  116.2 17.0 %copy-start.4 = (bf16[1,32,6144]{2,1,0:T(8,128)(2,1)S(1)}, bf16[1,32,6144]{2,1,0:T(8,128)(2,1)}, u32[]{:S(2)}) copy-start(bf16[1,32,6144]{2,1,0:T(8,128)(2,1)} %param.5) | copy-start | bytes 1179652
  116.2 17.0 %copy-start.5 = (bf16[1,32,6144]{2,1,0:T(8,128)(2,1)S(1)}, bf16[1,32,6144]{2,1,0:T(8,128)(2,1)}, u32[]{:S(2)}) copy-start(bf16[1,32,6144]{2,1,0:T(8,128)(2,1)} %param.6) | copy-start | bytes 1179652
  116.2 31.1 %collective-permute-start.27 = (bf16[256,3072]{1,0:T(8,128)(2,1)S(1)}, bf16[256,3072]{1,0:T(8,128)(2,1)S(1)}, u32[]{:S(2)}, u32[]{:S(2)}) collective-permute-start(bf16[256,3072]{1,0:T(8,128)(2,1)S(1)} %shard_map.99.refs_5_), channel_id=1, source_target_pairs={{0,4},{4,0},{8,12},{12,8},{1,5},{5,1},{9,13},{13,9},{2,6},{6,2},{1... | collective-permute-start | bytes 4718600 | tf_op jit(solution)/shard_map/ppermute | solution.py:483
  133.1 14.2 %collective-permute-start.28 = (bf16[512,1536]{1,0:T(8,128)(2,1)S(1)}, bf16[512,1536]{1,0:T(8,128)(2,1)S(1)}, u32[]{:S(2)}, u32[]{:S(2)}) collective-permute-start(bf16[512,1536]{1,0:T(8,128)(2,1)S(1)} %shard_map.94.refs_7_.refs_9_), channel_id=1, source_target_pairs={{0,4},{4,0},{8,12},{12,8},{1,5},{5,1},{9,13},{13,9},{2,6},{6,2},{1... | collective-permute-start | bytes 4718600 | tf_op jit(solution)/shard_map/ppermute | solution.py:483
  134.2 11.6 %collective-permute-start.21 = (bf16[32,6144]{1,0:T(8,128)(2,1)S(1)}, bf16[32,6144]{1,0:T(8,128)(2,1)S(1)}, u32[]{:S(2)}, u32[]{:S(2)}) collective-permute-start(bf16[32,6144]{1,0:T(8,128)(2,1)S(1)} %shard_map.95.refs_1_.refs_11_), channel_id=1, source_target_pairs={{16,0},{0,16},{17,1},{1,17},{18,2},{2,18},{19,3},{3,19},{20,4},{4,... | collective-permute-start | bytes 1179656 | tf_op jit(solution)/shard_map/ppermute | solution.py:568
  135.8 1.2 collective-permute-start.22
  137.0 3.9 %collective-permute-start.23 = (f32[1,6144]{1,0:T(1,128)S(1)}, f32[1,6144]{1,0:T(1,128)S(1)}, u32[]{:S(2)}, u32[]{:S(2)}) collective-permute-start(f32[1,6144]{1,0:T(1,128)S(1)} %add.6), channel_id=1, source_target_pairs={{0,8},{4,12},{8,0},{12,4},{1,9},{5,13},{9,1},{13,5},{2,10},{6,14},... | collective-permute-start | bytes 73736 | tf_op jit(solution)/shard_map/ppermute | solution.py:483
  141.0 22.8 %collective-permute-start.24 = (f32[1,6144]{1,0:T(1,128)S(1)}, f32[1,6144]{1,0:T(1,128)S(1)}, u32[]{:S(2)}, u32[]{:S(2)}) collective-permute-start(f32[1,6144]{1,0:T(1,128)S(1)} %shard_map.97.refs_0_), channel_id=1, source_target_pairs={{0,1},{1,0},{2,3},{3,2},{4,5},{5,4},{6,7},{7,6},{8,9},{9,8},{10,11... | collective-permute-start | bytes 73736 | tf_op jit(solution)/shard_map/ppermute | solution.py:483
  141.3 22.5 %collective-permute-start.25 = (f32[1,6144]{1,0:T(1,128)S(1)}, f32[1,6144]{1,0:T(1,128)S(1)}, u32[]{:S(2)}, u32[]{:S(2)}) collective-permute-start(f32[1,6144]{1,0:T(1,128)S(1)} %shard_map.97.refs_0_), channel_id=1, source_target_pairs={{0,2},{1,3},{2,0},{3,1},{4,6},{5,7},{6,4},{7,5},{8,10},{9,11},{10,... | collective-permute-start | bytes 73736 | tf_op jit(solution)/shard_map/ppermute | solution.py:483
  145.8 18.0 %collective-permute-start.26 = (f32[1,6144]{1,0:T(1,128)S(1)}, f32[1,6144]{1,0:T(1,128)S(1)}, u32[]{:S(2)}, u32[]{:S(2)}) collective-permute-start(f32[1,6144]{1,0:T(1,128)S(1)} %shard_map.97.refs_0_), channel_id=1, source_target_pairs={{0,3},{1,2},{2,1},{3,0},{4,7},{5,6},{6,5},{7,4},{8,11},{9,10},{10,... | collective-permute-start | bytes 73736 | tf_op jit(solution)/shard_map/ppermute | solution.py:483
  (4 other events, 20.9 us)

commit v3 on v2

--- a/solution.py
+++ b/solution.py
@@ -159,21 +159,25 @@
     return run(body, blocks, outs, after=after)
 
 
-def regrouped(parts, after=()):
-    half = parts[0].shape[1]
-    rows = parts[0].shape[0] // 2
-    count = sum(part.shape[0] for part in parts) // (2 * rows)
-
-    def body(ins, outs, scratch):
-        blocks = [
-            part[at:at + 2 * rows, :] for part in ins for at in range(0, part.shape[0], 2 * rows)
-        ]
-        for k, block in enumerate(blocks):
-            outs[0][k * rows:(k + 1) * rows, :] = block[:rows]
-            outs[0][(count + k) * rows:(count + k + 1) * rows, :] = block[rows:]
-
-    outs = [array((2 * count * rows, half), parts[0].dtype)]
-    return run(body, parts, outs, after=after)[0]
+def regrouped(blocks, folded, after=()):
+    rows, half = blocks[0].shape
+    rows //= 2
+    count = len(blocks) + 1
+    hidden = folded.shape[1]
+    first = folded.shape[0] - half // hidden * 2 * rows
+
+    def body(ins, outs, scratch):
+        for k, block in enumerate(ins[:-1]):
+            outs[0][k * rows:(k + 1) * rows, :] = block[:rows, :]
+            outs[0][(count + k) * rows:(count + k + 1) * rows, :] = block[rows:, :]
+        for j in range(half // hidden):
+            at = first + j * 2 * rows
+            columns = slice(j * hidden, (j + 1) * hidden)
+            outs[0][(count - 1) * rows:count * rows, columns] = ins[-1][at:at + rows, :]
+            outs[0][(2 * count - 1) * rows:, columns] = ins[-1][at + rows:at + 2 * rows, :]
+
+    outs = [array((2 * count * rows, half), blocks[0].dtype)]
+    return run(body, (*blocks, folded), outs, after=after)[0]
 
 
 def held(block, after):
@@ -191,25 +195,25 @@
 
     def body(ins, outs, scratch):
         w_in_ref, w_out_ref = ins[-2:]
-        rows_all, in_weight, out_weight, sems = scratch
-
-        def coming(j, forth, near=False):
+        rows_all, in_weight, out_weight, sems, near_sem = scratch
+
+        def coming(j, forth):
             units = window(tile, pair_place() * steps + j)
-            place = window(tile, j)
-            depth = window(half, near_place() if near else far_place())
+            place, depth = window(tile, j), window(half, far_place())
             if forth:
-                source = w_in_ref.at[depth, units]
-                target = (outs[2] if near else in_weight).at[:, place]
+                source, target = w_in_ref.at[depth, units], in_weight.at[:, place]
             else:
-                source = w_out_ref.at[units, depth]
-                target = (outs[3] if near else out_weight).at[place, :]
-            return pltpu.make_async_copy(
-                source, target, sems.at[2 * int(near) + 1 - int(forth), j]
-            )
-
-        every = [(j, forth, near) for near in (False, True) for forth in (True, False) for j in range(steps)]
-        for which in every:
-            coming(*which).start()
+                source, target = w_out_ref.at[units, depth], out_weight.at[place, :]
+            return pltpu.make_async_copy(source, target, sems.at[1 - int(forth), j])
+
+        along = pltpu.make_async_copy(
+            w_in_ref.at[window(half, near_place()), window(hidden, pair_place())],
+            outs[2], near_sem,
+        )
+        for forth in (True, False):
+            for j in range(steps):
+                coming(j, forth).start()
+        along.start()
         for k in range(2):
             rows_all[k * rows:(k + 1) * rows, :] = ins[k][:rows, :]
 
@@ -228,34 +232,44 @@
             place = window(tile, j)
             outs[1][:, place] = dot(rows_all[...], out_weight[place, :], 1, 1)
 
-        for which in every[2 * steps:]:
-            coming(*which).wait()
+        along.wait()
 
     wide = array((tokens, hidden), jnp.float32)
     return run(
-        body, groups,
-        [wide, wide, array((half, hidden), kind), array((hidden, half), kind)],
-        apart=(w_in, w_out),
+        body, groups, [wide, wide, array((half, hidden), kind)], apart=(w_in, w_out),
         scratch=[
             pltpu.VMEM((tokens, half), kind),
             pltpu.VMEM((half, hidden), kind),
             pltpu.VMEM((hidden, half), kind),
-            pltpu.SemaphoreType.DMA((4, steps)),
+            pltpu.SemaphoreType.DMA((2, steps)),
+            pltpu.SemaphoreType.DMA,
         ],
         after=after, limit=24,
     )
 
 
-def finished(group, pairs, prior, after=()):
+def finished(group, pairs, prior, w_out, along=(), after=()):
     tokens, half = group.shape
     rows, hidden, kind = tokens // 2, prior[0].shape[1], group.dtype
     tile = tile_of(hidden)
+    steps = hidden // tile
     piece = pairs[0].shape[0]
     each = rows // piece
 
     def body(ins, outs, scratch):
-        pre_ref, back_act_ref, in_weight, out_weight = ins[1 + 2 * each:]
-        rows_all, slope_ref = scratch
+        pre_ref, back_act_ref, in_weight, *more, w_out_ref = ins[1 + 2 * each:]
+        rows_all, slope_ref, out_weight, sems = scratch
+
+        def coming(j):
+            units = window(tile, pair_place() * steps + j)
+            return pltpu.make_async_copy(
+                w_out_ref.at[units, window(half, near_place())],
+                out_weight.at[window(tile, j), :],
+                sems.at[j],
+            )
+
+        for j in range(steps):
+            coming(j).start()
 
         def stack(below):
             rows_all[:rows, :] = ins[0][below * rows:(below + 1) * rows, :]
@@ -263,35 +277,51 @@
                 at = rows + k * piece
                 rows_all[at:at + piece, :] = ins[1 + below * each + k][...]
 
+        for block in more:
+            for k in range(half // hidden):
+                at = tokens + k * block.shape[0]
+                outs[0][at:at + block.shape[0], :] = block[:, k * hidden:(k + 1) * hidden]
         stack(0)
 
-        @pl.loop(0, hidden // tile)
+        @pl.loop(0, steps)
         def _(j):
             place = window(tile, j)
             pre = pre_ref[:, place] + dot(rows_all[...], in_weight[:, place], 1, 0)
             normal_cdf = 0.5 * (1.0 + lax.erf(pre * SQRT_HALF))
             density = INV_ROOT_TWO_PI * jnp.exp(-0.5 * pre * pre)
-            outs[0][:tokens, place] = (pre * normal_cdf).astype(kind)
+            active = (pre * normal_cdf).astype(kind)
+            outs[0][:tokens, place] = active
+            outs[2][:tokens, place] = active
             slope_ref[:, place] = normal_cdf + pre * density
 
         stack(1)
 
-        @pl.loop(0, hidden // tile)
+        @pl.loop(0, steps)
         def _(j):
+            coming(j).wait()
             place = window(tile, j)
             back_act = back_act_ref[:, place] + dot(rows_all[...], out_weight[place, :], 1, 1)
-            outs[0][tokens:, place] = (back_act * slope_ref[:, place]).astype(kind)
-
+            pre_error = (back_act * slope_ref[:, place]).astype(kind)
+            outs[1][:, place] = pre_error
+            outs[2][tokens:, place] = pre_error
+
+    below = sum(block.size // hidden for block in along)
     return run(
-        body, (group, *pairs, *prior), [array((2 * tokens, hidden), kind)],
-        [pltpu.VMEM((tokens, half), kind), pltpu.VMEM((tokens, hidden), jnp.float32)],
-        after=after, limit=8,
-    )[0]
-
-
-def sums(both, near_weight, w_in, after=()):
-    tokens, hidden = both.shape[0] // 2, both.shape[1]
-    half, rows, kind = near_weight.shape[0], tokens // 2, both.dtype
+        body, (group, *pairs, *prior, *along),
+        [array((rows, hidden), kind) for rows in (tokens + below, tokens, 2 * tokens)],
+        [
+            pltpu.VMEM((tokens, half), kind),
+            pltpu.VMEM((tokens, hidden), jnp.float32),
+            pltpu.VMEM((hidden, half), kind),
+            pltpu.SemaphoreType.DMA((steps,)),
+        ],
+        apart=(w_out,), after=after, limit=18,
+    )
+
+
+def sums(pre_error, near_weight, w_in, after=()):
+    tokens, hidden = pre_error.shape
+    half, rows, kind = near_weight.shape[0], tokens // 2, pre_error.dtype
     tile = tile_of(half)
     piece = rows // PIECES
 
@@ -309,14 +339,14 @@
             @pl.loop(0, half // tile)
             def _(j):
                 columns = window(tile, first + j)
-                term = dot(ins[0][tokens:, :], weight[window(tile, j), :], 1, 1)
+                term = dot(ins[0][...], weight[window(tile, j), :], 1, 1)
                 outs[0][:, columns] = term[:rows]
                 for k in range(PIECES):
                     at = rows + k * piece
                     outs[1 + k][:, columns] = term[at:at + piece].astype(kind)
 
     return run(
-        body, (both, near_weight),
+        body, (pre_error, near_weight),
         [array((rows, 2 * half), jnp.float32)] + [array((piece, 2 * half), kind)] * PIECES,
         [pltpu.VMEM((half, hidden), kind), pltpu.SemaphoreType.DMA],
         apart=(w_in,), after=after, limit=16,
@@ -362,90 +392,69 @@
     return run(body, (mine, came), [array(mine.shape, mine.dtype)], after=after)[0]
 
 
-def gradients(cut, full, after=()):
-    tokens, part = full[0].shape[0] // 2, full[0].shape[1]
-    rows, width, kind = tokens // 2, cut[0][0].shape[1] // 2, full[0].dtype
+def gradient(cut, full, rows, cut_rows, after=()):
+    part, width, kind = full[0][0].shape[1], cut[0][0].shape[1] // 2, full[0][0].dtype
     tile = tile_of(2 * part)
     steps = 2 * part // tile
-    names = [entry[0] for entry in cut]
-
-    def body(ins, outs, scratch):
-        a_all, b_all, wide, tall, in_sems, sems = scratch
+    shape = (width, 2 * part) if cut_rows else (2 * part, width)
+
+    def body(ins, outs, scratch):
+        a_all, b_all, buffer, in_sems, sems = scratch
         lo = pair_place()
-        moves = [[], []]
-        for which in range(2):
-            at = 0
-            for k, (_, first, count) in enumerate(cut):
-                if first[which] is None:
-                    continue
-                source = ins[k].at[pl.ds(first[which], count), window(width, lo)]
-                moves[which].append((source, a_all.at[which, pl.ds(at, count), :]))
-                at += count
-            for k in range(4):
-                for half in range(2):
-                    at = (k // 2 * 2 + (half if k % 2 == 0 else 1 - half)) * rows
-                    place = window(part, lo if k % 2 == 0 else 1 - lo)
-                    source = ins[len(cut) + k].at[pl.ds(which * tokens + half * rows, rows), :]
-                    moves[which].append((source, b_all.at[which, pl.ds(at, rows), place]))
+        moves, at = [], 0
+        for k, (_, first, count) in enumerate(cut):
+            source = ins[k].at[pl.ds(first, count), window(width, lo)]
+            moves.append((source, a_all.at[pl.ds(at, count), :]))
+            at += count
+        for k, (_, first) in enumerate(full):
+            for half in range(2):
+                at = (k // 2 * 2 + (half if k % 2 == 0 else 1 - half)) * rows
+                place = window(part, lo if k % 2 == 0 else 1 - lo)
+                source = ins[len(cut) + k].at[pl.ds(first + half * rows, rows), :]
+                moves.append((source, b_all.at[pl.ds(at, rows), place]))
         copies = [
-            [
-                pltpu.make_async_copy(a, b, in_sems.at[which, k])
-                for k, (a, b) in enumerate(moves[which])
-            ]
-            for which in range(2)
+            pltpu.make_async_copy(a, b, in_sems.at[k]) for k, (a, b) in enumerate(moves)
         ]
-        for copy in [*copies[0], *copies[1]]:
+        for copy in copies:
             copy.start()
-
-        for which in range(2):
-            for copy in copies[which]:
-                copy.wait()
-            buffer = (tall, wide)[which]
-
-            def leaving(j):
-                place = window(tile, j)
-                target = outs[1 + which].at[place, :] if which == 0 else outs[1 + which].at[:, place]
-                return pltpu.make_async_copy(buffer.at[j % 2], target, sems.at[which, j % 2])
-
-            @pl.loop(0, steps)
-            def _(j):
-                place = window(tile, j)
-                if which == 0:
-                    result = dot(b_all[0, :, place], a_all[0], 0, 0)
-                else:
-                    result = dot(a_all[1], b_all[1, :, place], 0, 0)
-
-                @pl.when(j >= 2)
-                def _():
-                    leaving(j - 2).wait()
-
-                buffer[j % 2] = result.astype(kind)
-                leaving(j).start()
-
-            if which == 1:
-                for k in range(2):
-                    buffer = (tall, wide)[k]
-                    for j in range(max(steps - 2, 0), steps):
-                        place = window(tile, j)
-                        target = outs[1 + k].at[place, :] if k == 0 else outs[1 + k].at[:, place]
-                        pltpu.make_async_copy(
-                            buffer.at[j % 2], target, sems.at[k, j % 2]
-                        ).wait()
+        for copy in copies:
+            copy.wait()
+
+        def leaving(j):
+            place = window(tile, j)
+            target = outs[1].at[:, place] if cut_rows else outs[1].at[place, :]
+            return pltpu.make_async_copy(buffer.at[j % 2], target, sems.at[j % 2])
+
+        @pl.loop(0, steps)
+        def _(j):
+            place = window(tile, j)
+            if cut_rows:
+                result = dot(a_all[...], b_all[:, place], 0, 0)
+            else:
+                result = dot(b_all[:, place], a_all[...], 0, 0)
+
+            @pl.when(j >= 2)
+            def _():
+                leaving(j - 2).wait()
+
+            buffer[j % 2] = result.astype(kind)
+            leaving(j).start()
+
+        for j in range(max(steps - 2, 0), steps):
+            leaving(j).wait()
         outs[0][...] = jnp.zeros_like(outs[0])
 
     return run(
-        body, (), [array((8, 128), jnp.float32)],
-        out_apart=[array((2 * part, width), kind), array((width, 2 * part), kind)],
-        apart=[*names, *full],
+        body, (), [array((8, 128), jnp.float32)], out_apart=[array(shape, kind)],
+        apart=[a for a, *_ in (*cut, *full)],
         scratch=[
-            pltpu.VMEM((2, 4 * rows, width), kind),
-            pltpu.VMEM((2, 4 * rows, 2 * part), kind),
-            pltpu.VMEM((2, width, tile), kind),
-            pltpu.VMEM((2, tile, width), kind),
-            pltpu.SemaphoreType.DMA((2, len(cut) + 8)),
-            pltpu.SemaphoreType.DMA((2, 2)),
+            pltpu.VMEM((4 * rows, width), kind),
+            pltpu.VMEM((4 * rows, 2 * part), kind),
+            pltpu.VMEM((2, width, tile) if cut_rows else (2, tile, width), kind),
+            pltpu.SemaphoreType.DMA((len(cut) + 8,)),
+            pltpu.SemaphoreType.DMA((2,)),
         ],
-        after=after, limit=24,
+        after=after, limit=16,
     )
 
 
@@ -525,25 +534,23 @@
         second_near = lax.ppermute(passing_near, "shard", RELAY)
         first_across = across(far_of(first))
         blocks = [own, first, second_far, third]
-        far, rest_far = grouped(blocks, False, apart=(2, 3), after=(first_across,))
-        rest_across = across(rest_far)
+        far, second_far = grouped(blocks, False, apart=(2,), after=(first_across,))
+        second_across, along = across(second_far), (far_of(third),)
         blocks = [own, first, second_near, third]
-        tie = (rest_across,)
+        tie = (second_across,)
     else:
         blocks = gathered(own)
         (far,) = grouped(blocks, False)
         far_across = across(far)
-        tie = ()
+        tie, along = (), ()
     far_pair = pair(far)
     prior = forth_and_back((far, far_pair), w_in, w_out)
     near, *pieces = grouped(blocks, True, pieces=PIECES, after=(prior[0],))
     pairs = [pair(piece) for piece in pieces]
-    both = finished(near, pairs, prior, after=tie)
-    both_across = across(both)
+    active, pre_error, both = finished(near, pairs, prior, w_out, along, after=tie)
+    active_across, pre_error_across = across(active), across(pre_error)
     both_pair = pair(both)
-    mine, *others = sums(both, prior[2], w_in)
-    if line:
-        far_across = regrouped((own_across, first_across, rest_across), after=(others[0],))
+    mine, *others = sums(pre_error, prior[2], w_in)
     count = PIECES if line else 1
     *terms, gain_grad = joined(
         mine, [pair(other) for other in others], far, near, ln_gain, count
@@ -552,37 +559,55 @@
         own_terms, first_terms, second_terms, third_terms = terms
         second_terms = lax.ppermute(second_terms, "shard", RELAY_BACK)
         first_terms = swapped(first_terms, "shard", 1)
-        passing = added(third_terms, second_terms, after=(both_pair,))
+        passing = added(third_terms, second_terms)
         tie = (passing,)
         terms = [own_terms, first_terms, swapped(passing, "shard", 3), second_terms]
-        tie = (terms[1], terms[2])
-        far_across = held(far_across, (passing,))
-        gain_grad = held(gain_grad, (passing,))
+        tie = (passing,)
+        gain_grad = held(gain_grad, tie)
+        active_across = held(active_across, tie)
+        far_across = regrouped((own_across, first_across, second_across), active_across)
     else:
         terms = [lax.psum_scatter(terms[0], "shard", scatter_dimension=0, tiled=True)]
     far_across_pair = pair(far_across)
-    both_across = held(both_across, tie)
-    both_across_pair = pair(both_across)
-    own_error = own_error_of(x, e, ln_gain, terms, after=(both_across,))
+    active_across_pair = pair(active_across)
+
+    tokens = pre_error.shape[0]
+    rows = tokens // 2
+    piece = pairs[0].shape[0]
+
+    def cut_at(first):
+        return [
+            (near, first, rows),
+            *[(pairs[(first + at) // piece], 0, piece) for at in range(0, rows, piece)],
+            (far_across, first, rows),
+            (far_across_pair, first, rows),
+        ]
+
+    token, w_out_grad = gradient(
+        cut_at(rows),
+        [(active, 0), (both_pair, 0), (active_across, 0), (active_across_pair, 0)],
+        rows, False,
+    )
+    own_error = own_error_of(x, e, ln_gain, terms, after=(token,))
     n_section = lax.axis_size("section")
     passed = lax.ppermute(
         own_error, "section", [((i + 1) % n_section, i) for i in range(n_section)]
     )
-    gain_grad = held(summed(gain_grad, "dp"), (own_error,))
+    pre_error_across = held(pre_error_across, (own_error,))
+    pre_error_across_pair = pair(pre_error_across)
+    gain_grad = held(gain_grad, (own_error, far_across_pair))
     if line:
-        gain_parts = [gain_grad] + [swapped(gain_grad, "shard", mask) for mask in (1, 2, 3)]
+        gain_grad = total([gain_grad, *[swapped(gain_grad, "shard", mask) for mask in (1, 2, 3)]])
     else:
-        gain_parts = [summed(gain_grad, "shard")]
-
-    tokens = both.shape[0] // 2
-    rows = tokens // 2
-    piece = pairs[0].shape[0]
-    each = rows // piece
-    cut = [(near, (rows, 0), rows)]
-    cut += [(pairs[k], (None, 0) if k < each else (0, None), piece) for k in range(PIECES)]
-    cut += [(far_across, (rows, 0), rows), (far_across_pair, (rows, 0), rows)]
-    token, w_out_grad, w_in_grad = gradients(
-        cut, (both, both_pair, both_across, both_across_pair), after=(own_error,)
+        gain_grad = summed(gain_grad, "shard")
+    gain_parts = [gain_grad, *[swapped(gain_grad, "dp", mask) for mask in (1, 2, 3)]]
+    token, w_in_grad = gradient(
+        cut_at(0),
+        [
+            (pre_error, 0), (both_pair, tokens), (pre_error_across, 0),
+            (pre_error_across_pair, 0),
+        ],
+        rows, True, after=(gain_grad,),
     )
     gain_grad = total(gain_parts, after=(token,))
     return passed[None], gain_grad, w_in_grad[None], w_out_grad[None]

time: 165 us -> 152 us (0.921)
  local copies, waits for them, and re-layouts: 9.32 us -> 1.89 us
  waiting for transfers between devices: 63.8 us -> 57.1 us
  starting transfers between devices: 42.3 us -> 44.6 us
  Pallas kernels: 48.9 us -> 47 us
    unnamed x15 -> x11, local copies, waits for them, and re-layouts: 9.32 us -> 1.89 us
    ppermute x25 -> x28, waiting for transfers between devices: 45.1 us -> 39.2 us  [swapped(): lax.ppermute(block, axis, [(i, i ^ mask) for i in range(lax.axis_size(axi...]
    ppermute x1, waiting for transfers between devices: 2.65 us -> 0.23 us  [per_device(): lax.ppermute(own_error, 'section', [((i + 1) % n_section, i) for i in ran...]
    ppermute x25 -> x28, starting transfers between devices: 22.3 us -> 24.6 us  [swapped(): lax.ppermute(block, axis, [(i, i ^ mask) for i in range(lax.axis_size(axi...]
    pallas_call x18 -> x21, Pallas kernels: 48.9 us -> 47 us  [run(): pl.pallas_call(kernel, out_shape=[*outputs, *out_apart], in_specs=[near]...]
    ppermute x1, waiting for transfers between devices: 10.1 us -> 11.8 us  [per_device(): second_terms = lax.ppermute(second_terms, 'shard', RELAY_BACK)]
  transfers between devices with their start and end apart: 29 -> 32, of which waited for: 18 -> 20; matrix products, arithmetic and copies ran while one was open for 0% -> 0% of each run, Pallas kernels for 24% -> 24%
where the time goes in v3:
time: 152 us; the launch traced here: 151 us
  waiting for transfers between devices  57.1 us (38%)
  Pallas kernels  47 us (31%)
  starting transfers between devices  44.6 us (29%)
  local copies, waits for them, and re-layouts  1.89 us (1%)
    pallas_call x21, Pallas kernels, run(): pl.pallas_call(kernel, out_shape=[*outputs, *out_apart], in_specs=[near]...  47 us
    ppermute x28, waiting for transfers between devices, swapped(): lax.ppermute(block, axis, [(i, i ^ mask) for i in range(lax.axis_size(axi...  39.2 us
    ppermute x28, starting transfers between devices, swapped(): lax.ppermute(block, axis, [(i, i ^ mask) for i in range(lax.axis_size(axi...  24.6 us
    ppermute x1, starting transfers between devices, per_device(): second_far = lax.ppermute(passing_far, 'shard', RELAY)  16.7 us
    ppermute x1, waiting for transfers between devices, per_device(): second_terms = lax.ppermute(second_terms, 'shard', RELAY_BACK)  11.8 us
    ppermute x1, waiting for transfers between devices, per_device(): second_far = lax.ppermute(passing_far, 'shard', RELAY)  5.91 us
  transfers between devices with their start and end apart: 32, of which 20 were waited for; matrix products, arithmetic and copies ran while one was open for 0% of the time, Pallas kernels for 24%

profile of v3, /device:TPU:0, one launch (start us, length us, event | category | flops | bytes accessed | tf_op | source)
XLA Modules:
  0.0 151.5 jit_solution(2642342470143984324)
XLA Ops:
  0.6 2.6 %shard_map.84 = (bf16[64,6144]{1,0:T(8,128)(2,1)}, bf16[64,3072]{1,0:T(8,128)(2,1)}) custom-call(bf16[32,6144]{1,0:T(8,128)(2,1)} %bitcast.7, bf16[32,6144]{1,0:T(8,128)(2,1)} %bitcast.9, f32[1,6144]{1,0:T(1,128)} %refs_2_.3), custom_call_target="tpu_custom_call" | custom-call | flops 1000 | bytes 1000 | tf_op jit(solution)/shard_map/pallas_call | solution.py:55
  3.2 5.1 %collective-permute-start.1 = (bf16[64,6144]{1,0:T(8,128)(2,1)}, bf16[64,6144]{1,0:T(8,128)(2,1)S(1)}, u32[]{:S(2)}, u32[]{:S(2)}) collective-permute-start(bf16[64,6144]{1,0:T(8,128)(2,1)} %get-tuple-element.35.refs_0_), channel_id=1, source_target_pairs={{0,3},{1,2},{2,1},{3,0},{4,7},{5,6},{6,5},{7,4},{8,11},{9,10},{10,... | collective-permute-start | bytes 2359304 | tf_op jit(solution)/shard_map/ppermute | solution.py:492
  8.3 1.5 collective-permute-start.2
  9.8 9.3 %collective-permute-done.2.refs_2_.refs_0_ = bf16[64,3072]{1,0:T(8,128)(2,1)S(1)} collective-permute-done((bf16[64,3072]{1,0:T(8,128)(2,1)}, bf16[64,3072]{1,0:T(8,128)(2,1)S(1)}, u32[]{:S(2)}, u32[]{:S(2)}) %collective-permute-start.2) | collective-permute-done | bytes 393248 | tf_op jit(solution)/shard_map/ppermute | solution.py:492
  19.1 7.9 %collective-permute-done.1.refs_1_.refs_3_.refs_0_ = bf16[64,6144]{1,0:T(8,128)(2,1)S(1)} collective-permute-done((bf16[64,6144]{1,0:T(8,128)(2,1)}, bf16[64,6144]{1,0:T(8,128)(2,1)S(1)}, u32[]{:S(2)}, u32[]{:S(2)}) %collective-permute-start.1) | collective-permute-done | bytes 786464 | tf_op jit(solution)/shard_map/ppermute | solution.py:492
  27.0 1.1 copy-done
  28.2 16.7 %collective-permute-start.4 = (bf16[64,3072]{1,0:T(8,128)(2,1)S(1)}, bf16[64,3072]{1,0:T(8,128)(2,1)S(1)}, u32[]{:S(2)}, u32[]{:S(2)}) collective-permute-start(bf16[64,3072]{1,0:T(8,128)(2,1)S(1)} %get-tuple-element.38), channel_id=1, source_target_pairs={{0,2},{3,1},{2,3},{1,0},{4,6},{7,5},{6,7},{5,4},{8,10},{11,9},{10,... | collective-permute-start | bytes 1179656 | tf_op jit(solution)/shard_map/ppermute | solution.py:533
  45.0 1.6 %collective-permute-start.5 = (bf16[64,3072]{1,0:T(8,128)(2,1)S(1)}, bf16[64,3072]{1,0:T(8,128)(2,1)S(1)}, u32[]{:S(2)}, u32[]{:S(2)}) collective-permute-start(bf16[64,3072]{1,0:T(8,128)(2,1)S(1)} %shard_map.86), channel_id=1, source_target_pairs={{0,8},{4,12},{8,0},{12,4},{1,9},{5,13},{9,1},{13,5},{2,10},{6,14},... | collective-permute-start | bytes 1179656 | tf_op jit(solution)/shard_map/ppermute | solution.py:492
  46.5 5.9 %collective-permute-done.4.refs_2_ = bf16[64,3072]{1,0:T(8,128)(2,1)S(1)} collective-permute-done((bf16[64,3072]{1,0:T(8,128)(2,1)S(1)}, bf16[64,3072]{1,0:T(8,128)(2,1)S(1)}, u32[]{:S(2)}, u32[]{:S(2)}) %collective-permute-start.4) | collective-permute-done | bytes 393248 | tf_op jit(solution)/shard_map/ppermute | solution.py:533
  52.4 2.3 %collective-permute-done.5.refs_4_.refs_1_ = bf16[64,3072]{1,0:T(8,128)(2,1)S(1)} collective-permute-done((bf16[64,3072]{1,0:T(8,128)(2,1)S(1)}, bf16[64,3072]{1,0:T(8,128)(2,1)S(1)}, u32[]{:S(2)}, u32[]{:S(2)}) %collective-permute-start.5) | collective-permute-done | bytes 393248 | tf_op jit(solution)/shard_map/ppermute | solution.py:492
  54.9 1.1 collective-permute-start.3
  56.1 1.5 collective-permute-start.11
  58.3 9.5 %shard_map.88 = (f32[256,1536]{1,0:T(8,128)S(1)}, f32[256,1536]{1,0:T(8,128)S(1)}, bf16[3072,1536]{1,0:T(8,128)(2,1)S(1)}) custom-call(bf16[256,3072]{1,0:T(8,128)(2,1)S(1)} %get-tuple-element.39.refs_0_.refs_5_, bf16[256,3072]{1,0:T(8,128)(2,1)S(1)} %collective-permute-done.6.refs_1_, bf16[6144,3072]{1,0:T(8,128)(2,1)} %bitcast.13, bf16[3072,6144]{1,0:T(8,128)(2,1)} %bitcast.11), custom_call_target="tpu_custom_call" | custom-call | flops 1000 | bytes 1000 | tf_op jit(solution)/shard_map/pallas_call | solution.py:55
  71.5 6.7 %shard_map.91 = (bf16[384,1536]{1,0:T(8,128)(2,1)S(1)}, bf16[256,1536]{1,0:T(8,128)(2,1)S(1)}, bf16[512,1536]{1,0:T(8,128)(2,1)S(1)}) custom-call(bf16[256,3072]{1,0:T(8,128)(2,1)S(1)} %get-tuple-element.41.refs_0_.refs_6_, bf16[64,3072]{1,0:T(8,128)(2,1)S(1)} %collective-permute-done.7.refs_1_, bf16[64,3072]{1,0:T(8,128)(2,1)S(1)} %collective-permute-done.8.refs_2_, ...), custom_call_target="tpu_custom_call" | custom-call | flops 1000 | bytes 1000 | tf_op jit(solution)/shard_map/pallas_call | solution.py:55
  78.3 1.6 %collective-permute-start.19 = (bf16[384,1536]{1,0:T(8,128)(2,1)S(1)}, bf16[384,1536]{1,0:T(8,128)(2,1)S(1)}, u32[]{:S(2)}, u32[]{:S(2)}) collective-permute-start(bf16[384,1536]{1,0:T(8,128)(2,1)S(1)} %get-tuple-element.59.refs_5_), channel_id=1, source_target_pairs={{0,8},{4,12},{8,0},{12,4},{1,9},{5,13},{9,1},{13,5},{2,10},{6,14},... | collective-permute-start | bytes 3538952 | tf_op jit(solution)/shard_map/ppermute | solution.py:492
  79.8 7.4 %shard_map.92 = (f32[128,6144]{1,0:T(8,128)S(1)}, bf16[32,6144]{1,0:T(8,128)(2,1)S(1)}, bf16[32,6144]{1,0:T(8,128)(2,1)S(1)}, bf16[32,6144]{1,0:T(8,128)(2,1)S(1)}, bf16[32,6144]{1,0:T(8,128)(2,1)S(1)}) custom-call(bf16[256,1536]{1,0:T(8,128)(2,1)S(1)} %get-tuple-element.49.refs_0_.refs_5_, bf16[3072,1536]{1,0:T(8,128)(2,1)S(1)} %get-tuple-element.47.refs_7_.refs_1_, ...), custom_call_target="tpu_custom_call" | custom-call | flops 1000 | bytes 1000 | tf_op jit(solution)/shard_map/pallas_call | solution.py:55
  90.7 0.9 shard_map.93
  92.1 11.8 %collective-permute-done.17.refs_1_.refs_6_ = bf16[32,6144]{1,0:T(8,128)(2,1)S(1)} collective-permute-done((bf16[32,6144]{1,0:T(8,128)(2,1)S(1)}, bf16[32,6144]{1,0:T(8,128)(2,1)S(1)}, u32[]{:S(2)}, u32[]{:S(2)}) %collective-permute-start.17) | collective-permute-done | bytes 393248 | tf_op jit(solution)/shard_map/ppermute | solution.py:560
  104.0 2.3 %collective-permute-done.19.refs_0_ = bf16[384,1536]{1,0:T(8,128)(2,1)S(1)} collective-permute-done((bf16[384,1536]{1,0:T(8,128)(2,1)S(1)}, bf16[384,1536]{1,0:T(8,128)(2,1)S(1)}, u32[]{:S(2)}, u32[]{:S(2)}) %collective-permute-start.19) | collective-permute-done | bytes 1179680 | tf_op jit(solution)/shard_map/ppermute | solution.py:492
  107.1 1.7 %collective-permute-start.30 = (bf16[256,1536]{1,0:T(8,128)(2,1)S(1)}, bf16[256,1536]{1,0:T(8,128)(2,1)S(1)}, u32[]{:S(2)}, u32[]{:S(2)}) collective-permute-start(bf16[256,1536]{1,0:T(8,128)(2,1)S(1)} %get-tuple-element.49.refs_0_.refs_5_), channel_id=1, source_target_pairs={{0,8},{4,12},{8,0},{12,4},{1,9},{5,13},{9,1},{13,5},{2,10},{6,14},... | collective-permute-start | bytes 2359304 | tf_op jit(solution)/shard_map/ppermute | solution.py:492
  109.0 2.3 %collective-permute-start.18 = (bf16[32,6144]{1,0:T(8,128)(2,1)S(1)}, bf16[32,6144]{1,0:T(8,128)(2,1)S(1)}, u32[]{:S(2)}, u32[]{:S(2)}) collective-permute-start(bf16[32,6144]{1,0:T(8,128)(2,1)S(1)} %shard_map.94.refs_1_), channel_id=1, source_target_pairs={{0,3},{1,2},{2,1},{3,0},{4,7},{5,6},{6,5},{7,4},{8,11},{9,10},{10,... | collective-permute-start | bytes 1179656 | tf_op jit(solution)/shard_map/ppermute | solution.py:492
  111.7 8.7 %shard_map.97 = (f32[8,128]{1,0:T(8,128)S(1)}, bf16[3072,1536]{1,0:T(8,128)(2,1)}) custom-call(bf16[256,3072]{1,0:T(8,128)(2,1)S(1)} %get-tuple-element.41.refs_0_.refs_6_, bf16[64,3072]{1,0:T(8,128)(2,1)S(1)} %collective-permute-done.9.refs_3_.refs_1_, bf16[64,3072]{1,0:T(8,128)(2,1)S(1)} %collective-permute-done.10.refs_4_.refs_2_, ...), custom_call_target="tpu_custom_call" | custom-call | flops 1000 | bytes 1000 | tf_op jit(solution)/shard_map/pallas_call | solution.py:55
  120.5 8.2 %collective-permute-done.18.refs_5_ = bf16[32,6144]{1,0:T(8,128)(2,1)S(1)} collective-permute-done((bf16[32,6144]{1,0:T(8,128)(2,1)S(1)}, bf16[32,6144]{1,0:T(8,128)(2,1)S(1)}, u32[]{:S(2)}, u32[]{:S(2)}) %collective-permute-start.18) | collective-permute-done | bytes 393248 | tf_op jit(solution)/shard_map/ppermute | solution.py:492
  128.7 1.0 shard_map.98.refs_1_
  129.8 1.6 %collective-permute-start.23 = (bf16[32,6144]{1,0:T(8,128)(2,1)S(1)}, bf16[32,6144]{1,0:T(8,128)(2,1)S(1)}, u32[]{:S(2)}, u32[]{:S(2)}) collective-permute-start(bf16[32,6144]{1,0:T(8,128)(2,1)S(1)} %shard_map.98.refs_1_), channel_id=1, source_target_pairs={{16,0},{0,16},{17,1},{1,17},{18,2},{2,18},{19,3},{3,19},{20,4},{4,... | collective-permute-start | bytes 1179656 | tf_op jit(solution)/shard_map/ppermute | solution.py:593
  131.4 1.1 collective-permute-start.24
  132.5 1.0 collective-permute-start.25
  133.5 2.3 %collective-permute-start.26 = (f32[1,6144]{1,0:T(1,128)S(1)}, f32[1,6144]{1,0:T(1,128)S(1)}, u32[]{:S(2)}, u32[]{:S(2)}) collective-permute-start(f32[1,6144]{1,0:T(1,128)S(1)} %shard_map.100.refs_0_), channel_id=1, source_target_pairs={{0,3},{1,2},{2,1},{3,0},{4,7},{5,6},{6,5},{7,4},{8,11},{9,10},{10,... | collective-permute-start | bytes 73736 | tf_op jit(solution)/shard_map/ppermute | solution.py:492
  135.8 1.5 collective-permute-done.25.refs_2_
  137.2 1.9 %collective-permute-done.26.refs_3_ = f32[1,6144]{1,0:T(1,128)S(1)} collective-permute-done((f32[1,6144]{1,0:T(1,128)S(1)}, f32[1,6144]{1,0:T(1,128)S(1)}, u32[]{:S(2)}, u32[]{:S(2)}) %collective-permute-start.26) | collective-permute-done | bytes 24608 | tf_op jit(solution)/shard_map/ppermute | solution.py:492
  139.6 1.5 collective-permute-start.29
  141.3 8.8 %shard_map.103 = (f32[8,128]{1,0:T(8,128)S(1)}, bf16[1536,3072]{1,0:T(8,128)(2,1)}) custom-call(bf16[256,3072]{1,0:T(8,128)(2,1)S(1)} %get-tuple-element.41.refs_0_.refs_6_, bf16[64,3072]{1,0:T(8,128)(2,1)S(1)} %collective-permute-done.7.refs_1_, bf16[64,3072]{1,0:T(8,128)(2,1)S(1)} %collective-permute-done.8.refs_2_, ...), custom_call_target="tpu_custom_call" | custom-call | flops 1000 | bytes 1000 | tf_op jit(solution)/shard_map/pallas_call | solution.py:55
  (64 shorter events, 12.4 us)
Async XLA Ops:
  3.2 23.8 %collective-permute-start.1 = (bf16[64,6144]{1,0:T(8,128)(2,1)}, bf16[64,6144]{1,0:T(8,128)(2,1)S(1)}, u32[]{:S(2)}, u32[]{:S(2)}) collective-permute-start(bf16[64,6144]{1,0:T(8,128)(2,1)} %get-tuple-element.35.refs_0_), channel_id=1, source_target_pairs={{0,3},{1,2},{2,1},{3,0},{4,7},{5,6},{6,5},{7,4},{8,11},{9,10},{10,... | collective-permute-start | bytes 2359304 | tf_op jit(solution)/shard_map/ppermute | solution.py:492
  8.3 36.6 %collective-permute-start = (bf16[64,6144]{1,0:T(8,128)(2,1)}, bf16[64,6144]{1,0:T(8,128)(2,1)S(1)}, u32[]{:S(2)}, u32[]{:S(2)}) collective-permute-start(bf16[64,6144]{1,0:T(8,128)(2,1)} %get-tuple-element.35.refs_0_), channel_id=1, source_target_pairs={{0,1},{1,0},{2,3},{3,2},{4,5},{5,4},{6,7},{7,6},{8,9},{9,8},{10,11... | collective-permute-start | bytes 2359304 | tf_op jit(solution)/shard_map/ppermute | solution.py:492
  8.3 10.8 %collective-permute-start.2 = (bf16[64,3072]{1,0:T(8,128)(2,1)}, bf16[64,3072]{1,0:T(8,128)(2,1)S(1)}, u32[]{:S(2)}, u32[]{:S(2)}) collective-permute-start(bf16[64,3072]{1,0:T(8,128)(2,1)} %get-tuple-element.36), channel_id=1, source_target_pairs={{0,8},{4,12},{8,0},{12,4},{1,9},{5,13},{9,1},{13,5},{2,10},{6,14},... | collective-permute-start | bytes 1179656 | tf_op jit(solution)/shard_map/ppermute | solution.py:492
  28.2 24.2 %collective-permute-start.4 = (bf16[64,3072]{1,0:T(8,128)(2,1)S(1)}, bf16[64,3072]{1,0:T(8,128)(2,1)S(1)}, u32[]{:S(2)}, u32[]{:S(2)}) collective-permute-start(bf16[64,3072]{1,0:T(8,128)(2,1)S(1)} %get-tuple-element.38), channel_id=1, source_target_pairs={{0,2},{3,1},{2,3},{1,0},{4,6},{7,5},{6,7},{5,4},{8,10},{11,9},{10,... | collective-permute-start | bytes 1179656 | tf_op jit(solution)/shard_map/ppermute | solution.py:533
  45.0 9.8 %collective-permute-start.5 = (bf16[64,3072]{1,0:T(8,128)(2,1)S(1)}, bf16[64,3072]{1,0:T(8,128)(2,1)S(1)}, u32[]{:S(2)}, u32[]{:S(2)}) collective-permute-start(bf16[64,3072]{1,0:T(8,128)(2,1)S(1)} %shard_map.86), channel_id=1, source_target_pairs={{0,8},{4,12},{8,0},{12,4},{1,9},{5,13},{9,1},{13,5},{2,10},{6,14},... | collective-permute-start | bytes 1179656 | tf_op jit(solution)/shard_map/ppermute | solution.py:492
  54.9 3.5 %collective-permute-start.6 = (bf16[256,3072]{1,0:T(8,128)(2,1)S(1)}, bf16[256,3072]{1,0:T(8,128)(2,1)S(1)}, u32[]{:S(2)}, u32[]{:S(2)}) collective-permute-start(bf16[256,3072]{1,0:T(8,128)(2,1)S(1)} %get-tuple-element.39.refs_0_.refs_5_), channel_id=1, source_target_pairs={{0,4},{4,0},{8,12},{12,8},{1,5},{5,1},{9,13},{13,9},{2,6},{6,2},{1... | collective-permute-start | bytes 4718600 | tf_op jit(solution)/shard_map/ppermute | solution.py:492
  54.9 12.9 %collective-permute-start.3 = (bf16[64,3072]{1,0:T(8,128)(2,1)S(1)}, bf16[64,3072]{1,0:T(8,128)(2,1)S(1)}, u32[]{:S(2)}, u32[]{:S(2)}) collective-permute-start(bf16[64,3072]{1,0:T(8,128)(2,1)S(1)} %get-tuple-element.37), channel_id=1, source_target_pairs={{0,2},{3,1},{2,3},{1,0},{4,6},{7,5},{6,7},{5,4},{8,10},{11,9},{10,... | collective-permute-start | bytes 1179656 | tf_op jit(solution)/shard_map/ppermute | solution.py:534
  56.1 13.1 %collective-permute-start.11 = (bf16[64,3072]{1,0:T(8,128)(2,1)S(1)}, bf16[64,3072]{1,0:T(8,128)(2,1)S(1)}, u32[]{:S(2)}, u32[]{:S(2)}) collective-permute-start(bf16[64,3072]{1,0:T(8,128)(2,1)S(1)} %get-tuple-element.48), channel_id=1, source_target_pairs={{0,8},{4,12},{8,0},{12,4},{1,9},{5,13},{9,1},{13,5},{2,10},{6,14},... | collective-permute-start | bytes 1179656 | tf_op jit(solution)/shard_map/ppermute | solution.py:492
  68.0 1.8 %collective-permute-start.10 = (bf16[64,3072]{1,0:T(8,128)(2,1)S(1)}, bf16[64,3072]{1,0:T(8,128)(2,1)S(1)}, u32[]{:S(2)}, u32[]{:S(2)}) collective-permute-start(bf16[64,3072]{1,0:T(8,128)(2,1)S(1)} %get-tuple-element.45), channel_id=1, source_target_pairs={{0,4},{4,0},{8,12},{12,8},{1,5},{5,1},{9,13},{13,9},{2,6},{6,2},{1... | collective-permute-start | bytes 1179656 | tf_op jit(solution)/shard_map/ppermute | solution.py:492
  68.1 2.3 %collective-permute-start.7 = (bf16[64,3072]{1,0:T(8,128)(2,1)S(1)}, bf16[64,3072]{1,0:T(8,128)(2,1)S(1)}, u32[]{:S(2)}, u32[]{:S(2)}) collective-permute-start(bf16[64,3072]{1,0:T(8,128)(2,1)S(1)} %get-tuple-element.42), channel_id=1, source_target_pairs={{0,4},{4,0},{8,12},{12,8},{1,5},{5,1},{9,13},{13,9},{2,6},{6,2},{1... | collective-permute-start | bytes 1179656 | tf_op jit(solution)/shard_map/ppermute | solution.py:492
  68.6 2.3 %collective-permute-start.8 = (bf16[64,3072]{1,0:T(8,128)(2,1)S(1)}, bf16[64,3072]{1,0:T(8,128)(2,1)S(1)}, u32[]{:S(2)}, u32[]{:S(2)}) collective-permute-start(bf16[64,3072]{1,0:T(8,128)(2,1)S(1)} %get-tuple-element.43), channel_id=1, source_target_pairs={{0,4},{4,0},{8,12},{12,8},{1,5},{5,1},{9,13},{13,9},{2,6},{6,2},{1... | collective-permute-start | bytes 1179656 | tf_op jit(solution)/shard_map/ppermute | solution.py:492
  68.7 2.8 %collective-permute-start.9 = (bf16[64,3072]{1,0:T(8,128)(2,1)S(1)}, bf16[64,3072]{1,0:T(8,128)(2,1)S(1)}, u32[]{:S(2)}, u32[]{:S(2)}) collective-permute-start(bf16[64,3072]{1,0:T(8,128)(2,1)S(1)} %get-tuple-element.44), channel_id=1, source_target_pairs={{0,4},{4,0},{8,12},{12,8},{1,5},{5,1},{9,13},{13,9},{2,6},{6,2},{1... | collective-permute-start | bytes 1179656 | tf_op jit(solution)/shard_map/ppermute | solution.py:492
  78.3 28.1 %collective-permute-start.19 = (bf16[384,1536]{1,0:T(8,128)(2,1)S(1)}, bf16[384,1536]{1,0:T(8,128)(2,1)S(1)}, u32[]{:S(2)}, u32[]{:S(2)}) collective-permute-start(bf16[384,1536]{1,0:T(8,128)(2,1)S(1)} %get-tuple-element.59.refs_5_), channel_id=1, source_target_pairs={{0,8},{4,12},{8,0},{12,4},{1,9},{5,13},{9,1},{13,5},{2,10},{6,14},... | collective-permute-start | bytes 3538952 | tf_op jit(solution)/shard_map/ppermute | solution.py:492
  87.2 1.8 %collective-permute-start.12 = (bf16[32,6144]{1,0:T(8,128)(2,1)S(1)}, bf16[32,6144]{1,0:T(8,128)(2,1)S(1)}, u32[]{:S(2)}, u32[]{:S(2)}) collective-permute-start(bf16[32,6144]{1,0:T(8,128)(2,1)S(1)} %get-tuple-element.51), channel_id=1, source_target_pairs={{0,4},{4,0},{8,12},{12,8},{1,5},{5,1},{9,13},{13,9},{2,6},{6,2},{1... | collective-permute-start | bytes 1179656 | tf_op jit(solution)/shard_map/ppermute | solution.py:492
  87.3 2.3 %collective-permute-start.13 = (bf16[32,6144]{1,0:T(8,128)(2,1)S(1)}, bf16[32,6144]{1,0:T(8,128)(2,1)S(1)}, u32[]{:S(2)}, u32[]{:S(2)}) collective-permute-start(bf16[32,6144]{1,0:T(8,128)(2,1)S(1)} %get-tuple-element.52), channel_id=1, source_target_pairs={{0,4},{4,0},{8,12},{12,8},{1,5},{5,1},{9,13},{13,9},{2,6},{6,2},{1... | collective-permute-start | bytes 1179656 | tf_op jit(solution)/shard_map/ppermute | solution.py:492
  87.8 2.3 %collective-permute-start.14 = (bf16[32,6144]{1,0:T(8,128)(2,1)S(1)}, bf16[32,6144]{1,0:T(8,128)(2,1)S(1)}, u32[]{:S(2)}, u32[]{:S(2)}) collective-permute-start(bf16[32,6144]{1,0:T(8,128)(2,1)S(1)} %get-tuple-element.53), channel_id=1, source_target_pairs={{0,4},{4,0},{8,12},{12,8},{1,5},{5,1},{9,13},{13,9},{2,6},{6,2},{1... | collective-permute-start | bytes 1179656 | tf_op jit(solution)/shard_map/ppermute | solution.py:492
  87.9 2.8 %collective-permute-start.15 = (bf16[32,6144]{1,0:T(8,128)(2,1)S(1)}, bf16[32,6144]{1,0:T(8,128)(2,1)S(1)}, u32[]{:S(2)}, u32[]{:S(2)}) collective-permute-start(bf16[32,6144]{1,0:T(8,128)(2,1)S(1)} %get-tuple-element.54), channel_id=1, source_target_pairs={{0,4},{4,0},{8,12},{12,8},{1,5},{5,1},{9,13},{13,9},{2,6},{6,2},{1... | collective-permute-start | bytes 1179656 | tf_op jit(solution)/shard_map/ppermute | solution.py:492
  91.6 12.3 %collective-permute-start.17 = (bf16[32,6144]{1,0:T(8,128)(2,1)S(1)}, bf16[32,6144]{1,0:T(8,128)(2,1)S(1)}, u32[]{:S(2)}, u32[]{:S(2)}) collective-permute-start(bf16[32,6144]{1,0:T(8,128)(2,1)S(1)} %get-tuple-element.58), channel_id=1, source_target_pairs={{2,0},{1,3},{3,2},{0,1},{6,4},{5,7},{7,6},{4,5},{10,8},{9,11},{11,... | collective-permute-start | bytes 1179656 | tf_op jit(solution)/shard_map/ppermute | solution.py:560
  92.1 16.9 %collective-permute-start.21 = (bf16[512,1536]{1,0:T(8,128)(2,1)S(1)}, bf16[512,1536]{1,0:T(8,128)(2,1)S(1)}, u32[]{:S(2)}, u32[]{:S(2)}) collective-permute-start(bf16[512,1536]{1,0:T(8,128)(2,1)S(1)} %get-tuple-element.60), channel_id=1, source_target_pairs={{0,4},{4,0},{8,12},{12,8},{1,5},{5,1},{9,13},{13,9},{2,6},{6,2},{1... | collective-permute-start | bytes 4718600 | tf_op jit(solution)/shard_map/ppermute | solution.py:492
  106.5 5.2 %collective-permute-start.20 = (bf16[256,3072]{1,0:T(8,128)(2,1)S(1)}, bf16[256,3072]{1,0:T(8,128)(2,1)S(1)}, u32[]{:S(2)}, u32[]{:S(2)}) collective-permute-start(bf16[256,3072]{1,0:T(8,128)(2,1)S(1)} %shard_map.96.refs_3_), channel_id=1, source_target_pairs={{0,4},{4,0},{8,12},{12,8},{1,5},{5,1},{9,13},{13,9},{2,6},{6,2},{1... | collective-permute-start | bytes 4718600 | tf_op jit(solution)/shard_map/ppermute | solution.py:492
  106.6 5.1 %collective-permute-start.22 = (bf16[384,1536]{1,0:T(8,128)(2,1)S(1)}, bf16[384,1536]{1,0:T(8,128)(2,1)S(1)}, u32[]{:S(2)}, u32[]{:S(2)}) collective-permute-start(bf16[384,1536]{1,0:T(8,128)(2,1)S(1)} %shard_map.95.refs_3_.refs_7_), channel_id=1, source_target_pairs={{0,4},{4,0},{8,12},{12,8},{1,5},{5,1},{9,13},{13,9},{2,6},{6,2},{1... | collective-permute-start | bytes 3538952 | tf_op jit(solution)/shard_map/ppermute | solution.py:492
  107.1 22.5 %collective-permute-start.30 = (bf16[256,1536]{1,0:T(8,128)(2,1)S(1)}, bf16[256,1536]{1,0:T(8,128)(2,1)S(1)}, u32[]{:S(2)}, u32[]{:S(2)}) collective-permute-start(bf16[256,1536]{1,0:T(8,128)(2,1)S(1)} %get-tuple-element.49.refs_0_.refs_5_), channel_id=1, source_target_pairs={{0,8},{4,12},{8,0},{12,4},{1,9},{5,13},{9,1},{13,5},{2,10},{6,14},... | collective-permute-start | bytes 2359304 | tf_op jit(solution)/shard_map/ppermute | solution.py:492
  108.8 11.7 %collective-permute-start.16 = (bf16[32,6144]{1,0:T(8,128)(2,1)S(1)}, bf16[32,6144]{1,0:T(8,128)(2,1)S(1)}, u32[]{:S(2)}, u32[]{:S(2)}) collective-permute-start(bf16[32,6144]{1,0:T(8,128)(2,1)S(1)} %get-tuple-element.56), channel_id=1, source_target_pairs={{0,1},{1,0},{2,3},{3,2},{4,5},{5,4},{6,7},{7,6},{8,9},{9,8},{10,11... | collective-permute-start | bytes 1179656 | tf_op jit(solution)/shard_map/ppermute | solution.py:492
  109.0 19.6 %collective-permute-start.18 = (bf16[32,6144]{1,0:T(8,128)(2,1)S(1)}, bf16[32,6144]{1,0:T(8,128)(2,1)S(1)}, u32[]{:S(2)}, u32[]{:S(2)}) collective-permute-start(bf16[32,6144]{1,0:T(8,128)(2,1)S(1)} %shard_map.94.refs_1_), channel_id=1, source_target_pairs={{0,3},{1,2},{2,1},{3,0},{4,7},{5,6},{6,5},{7,4},{8,11},{9,10},{10,... | collective-permute-start | bytes 1179656 | tf_op jit(solution)/shard_map/ppermute | solution.py:492
  129.7 11.6 %collective-permute-start.31 = (bf16[256,1536]{1,0:T(8,128)(2,1)S(1)}, bf16[256,1536]{1,0:T(8,128)(2,1)S(1)}, u32[]{:S(2)}, u32[]{:S(2)}) collective-permute-start(bf16[256,1536]{1,0:T(8,128)(2,1)S(1)} %shard_map.102.refs_7_), channel_id=1, source_target_pairs={{0,4},{4,0},{8,12},{12,8},{1,5},{5,1},{9,13},{13,9},{2,6},{6,2},{1... | collective-permute-start | bytes 2359304 | tf_op jit(solution)/shard_map/ppermute | solution.py:492
  129.8 11.5 %collective-permute-start.23 = (bf16[32,6144]{1,0:T(8,128)(2,1)S(1)}, bf16[32,6144]{1,0:T(8,128)(2,1)S(1)}, u32[]{:S(2)}, u32[]{:S(2)}) collective-permute-start(bf16[32,6144]{1,0:T(8,128)(2,1)S(1)} %shard_map.98.refs_1_), channel_id=1, source_target_pairs={{16,0},{0,16},{17,1},{1,17},{18,2},{2,18},{19,3},{3,19},{20,4},{4,... | collective-permute-start | bytes 1179656 | tf_op jit(solution)/shard_map/ppermute | solution.py:593
  131.4 4.4 %collective-permute-start.24 = (f32[1,6144]{1,0:T(1,128)S(1)}, f32[1,6144]{1,0:T(1,128)S(1)}, u32[]{:S(2)}, u32[]{:S(2)}) collective-permute-start(f32[1,6144]{1,0:T(1,128)S(1)} %shard_map.100.refs_0_), channel_id=1, source_target_pairs={{0,1},{1,0},{2,3},{3,2},{4,5},{5,4},{6,7},{7,6},{8,9},{9,8},{10,11... | collective-permute-start | bytes 73736 | tf_op jit(solution)/shard_map/ppermute | solution.py:492
  132.5 4.7 %collective-permute-start.25 = (f32[1,6144]{1,0:T(1,128)S(1)}, f32[1,6144]{1,0:T(1,128)S(1)}, u32[]{:S(2)}, u32[]{:S(2)}) collective-permute-start(f32[1,6144]{1,0:T(1,128)S(1)} %shard_map.100.refs_0_), channel_id=1, source_target_pairs={{0,2},{1,3},{2,0},{3,1},{4,6},{5,7},{6,4},{7,5},{8,10},{9,11},{10,... | collective-permute-start | bytes 73736 | tf_op jit(solution)/shard_map/ppermute | solution.py:492
  133.5 5.6 %collective-permute-start.26 = (f32[1,6144]{1,0:T(1,128)S(1)}, f32[1,6144]{1,0:T(1,128)S(1)}, u32[]{:S(2)}, u32[]{:S(2)}) collective-permute-start(f32[1,6144]{1,0:T(1,128)S(1)} %shard_map.100.refs_0_), channel_id=1, source_target_pairs={{0,3},{1,2},{2,1},{3,0},{4,7},{5,6},{6,5},{7,4},{8,11},{9,10},{10,... | collective-permute-start | bytes 73736 | tf_op jit(solution)/shard_map/ppermute | solution.py:492
  139.1 11.0 %collective-permute-start.27 = (f32[1,6144]{1,0:T(1,128)S(1)}, f32[1,6144]{1,0:T(1,128)S(1)}, u32[]{:S(2)}, u32[]{:S(2)}) collective-permute-start(f32[1,6144]{1,0:T(1,128)S(1)} %shard_map.101.refs_9_.refs_0_), channel_id=1, source_target_pairs={{0,4},{4,0},{8,12},{12,8},{1,5},{5,1},{9,13},{13,9},{2,6},{6,2},{1... | collective-permute-start | bytes 73736 | tf_op jit(solution)/shard_map/ppermute | solution.py:492
  139.2 10.9 %collective-permute-start.28 = (f32[1,6144]{1,0:T(1,128)S(1)}, f32[1,6144]{1,0:T(1,128)S(1)}, u32[]{:S(2)}, u32[]{:S(2)}) collective-permute-start(f32[1,6144]{1,0:T(1,128)S(1)} %shard_map.101.refs_9_.refs_0_), channel_id=1, source_target_pairs={{0,8},{4,12},{8,0},{12,4},{1,9},{5,13},{9,1},{13,5},{2,10},{6,14},... | collective-permute-start | bytes 73736 | tf_op jit(solution)/shard_map/ppermute | solution.py:492
  139.6 10.5 %collective-permute-start.29 = (f32[1,6144]{1,0:T(1,128)S(1)}, f32[1,6144]{1,0:T(1,128)S(1)}, u32[]{:S(2)}, u32[]{:S(2)}) collective-permute-start(f32[1,6144]{1,0:T(1,128)S(1)} %shard_map.101.refs_9_.refs_0_), channel_id=1, source_target_pairs={{0,12},{4,8},{8,4},{12,0},{1,13},{5,9},{9,5},{13,1},{2,14},{6,10},... | collective-permute-start | bytes 73736 | tf_op jit(solution)/shard_map/ppermute | solution.py:492
  (5 other events, 78.4 us)

commit v4 on v3

--- a/solution.py
+++ b/solution.py
@@ -529,7 +529,8 @@
     if line:
         first, third = swapped(own, "shard", 1), swapped(own, "shard", 3)
         own_across = across(own_far)
-        passing_far, passing_near = passed_on(own, third, after=(own_across,))
+        own = held(own, (own_across,))
+        passing_far, passing_near = passed_on(own, third)
         second_far = lax.ppermute(passing_far, "shard", RELAY)
         second_near = lax.ppermute(passing_near, "shard", RELAY)
         first_across = across(far_of(first))
@@ -588,18 +589,19 @@
         [(active, 0), (both_pair, 0), (active_across, 0), (active_across_pair, 0)],
         rows, False,
     )
-    own_error = own_error_of(x, e, ln_gain, terms, after=(token,))
-    n_section = lax.axis_size("section")
-    passed = lax.ppermute(
-        own_error, "section", [((i + 1) % n_section, i) for i in range(n_section)]
-    )
-    pre_error_across = held(pre_error_across, (own_error,))
-    pre_error_across_pair = pair(pre_error_across)
-    gain_grad = held(gain_grad, (own_error, far_across_pair))
+    gain_grad = held(gain_grad, (token,))
     if line:
         gain_grad = total([gain_grad, *[swapped(gain_grad, "shard", mask) for mask in (1, 2, 3)]])
     else:
         gain_grad = summed(gain_grad, "shard")
+    own_error = own_error_of(x, e, ln_gain, terms, after=(gain_grad,))
+    n_section = lax.axis_size("section")
+    passed = lax.ppermute(
+        own_error, "section", [((i + 1) % n_section, i) for i in range(n_section)]
+    )
+    pre_error_across = held(pre_error_across, (own_error,))
+    pre_error_across_pair = pair(pre_error_across)
+    gain_grad = held(gain_grad, (own_error,))
     gain_parts = [gain_grad, *[swapped(gain_grad, "dp", mask) for mask in (1, 2, 3)]]
     token, w_in_grad = gradient(
         cut_at(0),
@@ -610,6 +612,7 @@
         rows, True, after=(gain_grad,),
     )
     gain_grad = total(gain_parts, after=(token,))
+    passed = held(passed, (token,))
     return passed[None], gain_grad, w_in_grad[None], w_out_grad[None]
 
 

time: 152 us -> 149 us (0.980)
  waiting for transfers between devices: 57.1 us -> 54.4 us
    ppermute x28, waiting for transfers between devices: 39.2 us -> 36.9 us  [swapped(): lax.ppermute(block, axis, [(i, i ^ mask) for i in range(lax.axis_size(axi...]
    pallas_call x21 -> x24, Pallas kernels: 47 us -> 47.9 us  [run(): pl.pallas_call(kernel, out_shape=[*outputs, *out_apart], in_specs=[near]...]
  transfers between devices with their start and end apart: 32 -> 32, of which waited for: 20 -> 18; matrix products, arithmetic and copies ran while one was open for 0% -> 0% of each run, Pallas kernels for 24% -> 25%
where the time goes in v4:
time: 149 us
  waiting for transfers between devices  54.4 us (37%)
  Pallas kernels  47.9 us (32%)
  starting transfers between devices  44.4 us (30%)
    pallas_call x24, Pallas kernels, run(): pl.pallas_call(kernel, out_shape=[*outputs, *out_apart], in_specs=[near]...  47.9 us
    ppermute x28, waiting for transfers between devices, swapped(): lax.ppermute(block, axis, [(i, i ^ mask) for i in range(lax.axis_size(axi...  36.9 us
    ppermute x28, starting transfers between devices, swapped(): lax.ppermute(block, axis, [(i, i ^ mask) for i in range(lax.axis_size(axi...  24.6 us
    ppermute x1, starting transfers between devices, per_device(): second_far = lax.ppermute(passing_far, 'shard', RELAY)  16.7 us
    ppermute x1, waiting for transfers between devices, per_device(): second_terms = lax.ppermute(second_terms, 'shard', RELAY_BACK)  11.4 us
    ppermute x1, waiting for transfers between devices, per_device(): second_far = lax.ppermute(passing_far, 'shard', RELAY)  6.07 us
  transfers between devices with their start and end apart: 32, of which 18 were waited for; matrix products, arithmetic and copies ran while one was open for 0% of the time, Pallas kernels for 25%

profile of v4, /device:TPU:0, one launch (start us, length us, event | category | flops | bytes accessed | tf_op | source)
XLA Modules:
  0.0 148.7 jit_solution(15045276324195293449)
XLA Ops:
  0.6 2.6 %shard_map.84 = (bf16[64,6144]{1,0:T(8,128)(2,1)}, bf16[64,3072]{1,0:T(8,128)(2,1)}) custom-call(bf16[32,6144]{1,0:T(8,128)(2,1)} %bitcast.7, bf16[32,6144]{1,0:T(8,128)(2,1)} %bitcast.9, f32[1,6144]{1,0:T(1,128)} %refs_2_.3), custom_call_target="tpu_custom_call" | custom-call | flops 1000 | bytes 1000 | tf_op jit(solution)/shard_map/pallas_call | solution.py:55
  3.2 5.1 %collective-permute-start.2 = (bf16[64,6144]{1,0:T(8,128)(2,1)}, bf16[64,6144]{1,0:T(8,128)(2,1)S(1)}, u32[]{:S(2)}, u32[]{:S(2)}) collective-permute-start(bf16[64,6144]{1,0:T(8,128)(2,1)} %get-tuple-element.35.refs_0_), channel_id=1, source_target_pairs={{0,3},{1,2},{2,1},{3,0},{4,7},{5,6},{6,5},{7,4},{8,11},{9,10},{10,... | collective-permute-start | bytes 2359304 | tf_op jit(solution)/shard_map/ppermute | solution.py:492
  8.3 1.5 %collective-permute-start = (bf16[64,3072]{1,0:T(8,128)(2,1)}, bf16[64,3072]{1,0:T(8,128)(2,1)S(1)}, u32[]{:S(2)}, u32[]{:S(2)}) collective-permute-start(bf16[64,3072]{1,0:T(8,128)(2,1)} %get-tuple-element.36), channel_id=1, source_target_pairs={{0,8},{4,12},{8,0},{12,4},{1,9},{5,13},{9,1},{13,5},{2,10},{6,14},... | collective-permute-start | bytes 1179656 | tf_op jit(solution)/shard_map/ppermute | solution.py:492
  9.8 9.3 %collective-permute-done.refs_1_.refs_0_ = bf16[64,3072]{1,0:T(8,128)(2,1)S(1)} collective-permute-done((bf16[64,3072]{1,0:T(8,128)(2,1)}, bf16[64,3072]{1,0:T(8,128)(2,1)S(1)}, u32[]{:S(2)}, u32[]{:S(2)}) %collective-permute-start) | collective-permute-done | bytes 393248 | tf_op jit(solution)/shard_map/ppermute | solution.py:492
  19.1 1.1 copy-done.2
  20.3 6.7 %collective-permute-done.2.refs_1_.refs_3_.refs_0_ = bf16[64,6144]{1,0:T(8,128)(2,1)S(1)} collective-permute-done((bf16[64,6144]{1,0:T(8,128)(2,1)}, bf16[64,6144]{1,0:T(8,128)(2,1)S(1)}, u32[]{:S(2)}, u32[]{:S(2)}) %collective-permute-start.2) | collective-permute-done | bytes 786464 | tf_op jit(solution)/shard_map/ppermute | solution.py:492
  27.1 16.7 %collective-permute-start.4 = (bf16[64,3072]{1,0:T(8,128)(2,1)S(1)}, bf16[64,3072]{1,0:T(8,128)(2,1)S(1)}, u32[]{:S(2)}, u32[]{:S(2)}) collective-permute-start(bf16[64,3072]{1,0:T(8,128)(2,1)S(1)} %get-tuple-element.38), channel_id=1, source_target_pairs={{0,2},{3,1},{2,3},{1,0},{4,6},{7,5},{6,7},{5,4},{8,10},{11,9},{10,... | collective-permute-start | bytes 1179656 | tf_op jit(solution)/shard_map/ppermute | solution.py:534
  43.8 1.6 %collective-permute-start.5 = (bf16[64,3072]{1,0:T(8,128)(2,1)S(1)}, bf16[64,3072]{1,0:T(8,128)(2,1)S(1)}, u32[]{:S(2)}, u32[]{:S(2)}) collective-permute-start(bf16[64,3072]{1,0:T(8,128)(2,1)S(1)} %shard_map.87), channel_id=1, source_target_pairs={{0,8},{4,12},{8,0},{12,4},{1,9},{5,13},{9,1},{13,5},{2,10},{6,14},... | collective-permute-start | bytes 1179656 | tf_op jit(solution)/shard_map/ppermute | solution.py:492
  45.4 6.1 %collective-permute-done.4.refs_2_ = bf16[64,3072]{1,0:T(8,128)(2,1)S(1)} collective-permute-done((bf16[64,3072]{1,0:T(8,128)(2,1)S(1)}, bf16[64,3072]{1,0:T(8,128)(2,1)S(1)}, u32[]{:S(2)}, u32[]{:S(2)}) %collective-permute-start.4) | collective-permute-done | bytes 393248 | tf_op jit(solution)/shard_map/ppermute | solution.py:534
  51.4 2.7 %collective-permute-done.5.refs_4_.refs_1_ = bf16[64,3072]{1,0:T(8,128)(2,1)S(1)} collective-permute-done((bf16[64,3072]{1,0:T(8,128)(2,1)S(1)}, bf16[64,3072]{1,0:T(8,128)(2,1)S(1)}, u32[]{:S(2)}, u32[]{:S(2)}) %collective-permute-start.5) | collective-permute-done | bytes 393248 | tf_op jit(solution)/shard_map/ppermute | solution.py:492
  54.9 1.5 %collective-permute-start.11 = (bf16[64,3072]{1,0:T(8,128)(2,1)S(1)}, bf16[64,3072]{1,0:T(8,128)(2,1)S(1)}, u32[]{:S(2)}, u32[]{:S(2)}) collective-permute-start(bf16[64,3072]{1,0:T(8,128)(2,1)S(1)} %get-tuple-element.48), channel_id=1, source_target_pairs={{0,8},{4,12},{8,0},{12,4},{1,9},{5,13},{9,1},{13,5},{2,10},{6,14},... | collective-permute-start | bytes 1179656 | tf_op jit(solution)/shard_map/ppermute | solution.py:492
  56.4 1.3 collective-permute-done.6.refs_1_
  57.8 9.5 %shard_map.89 = (f32[256,1536]{1,0:T(8,128)S(1)}, f32[256,1536]{1,0:T(8,128)S(1)}, bf16[3072,1536]{1,0:T(8,128)(2,1)S(1)}) custom-call(bf16[256,3072]{1,0:T(8,128)(2,1)S(1)} %get-tuple-element.39.refs_0_.refs_5_, bf16[256,3072]{1,0:T(8,128)(2,1)S(1)} %collective-permute-done.6.refs_1_, bf16[6144,3072]{1,0:T(8,128)(2,1)} %bitcast.13, bf16[3072,6144]{1,0:T(8,128)(2,1)} %bitcast.11), custom_call_target="tpu_custom_call" | custom-call | flops 1000 | bytes 1000 | tf_op jit(solution)/shard_map/pallas_call | solution.py:55
  70.9 6.7 %shard_map.92 = (bf16[384,1536]{1,0:T(8,128)(2,1)S(1)}, bf16[256,1536]{1,0:T(8,128)(2,1)S(1)}, bf16[512,1536]{1,0:T(8,128)(2,1)S(1)}) custom-call(bf16[256,3072]{1,0:T(8,128)(2,1)S(1)} %get-tuple-element.41.refs_0_.refs_6_, bf16[64,3072]{1,0:T(8,128)(2,1)S(1)} %collective-permute-done.7.refs_1_, bf16[64,3072]{1,0:T(8,128)(2,1)S(1)} %collective-permute-done.8.refs_2_, ...), custom_call_target="tpu_custom_call" | custom-call | flops 1000 | bytes 1000 | tf_op jit(solution)/shard_map/pallas_call | solution.py:55
  77.7 1.6 %collective-permute-start.19 = (bf16[384,1536]{1,0:T(8,128)(2,1)S(1)}, bf16[384,1536]{1,0:T(8,128)(2,1)S(1)}, u32[]{:S(2)}, u32[]{:S(2)}) collective-permute-start(bf16[384,1536]{1,0:T(8,128)(2,1)S(1)} %get-tuple-element.60.refs_5_), channel_id=1, source_target_pairs={{0,8},{4,12},{8,0},{12,4},{1,9},{5,13},{9,1},{13,5},{2,10},{6,14},... | collective-permute-start | bytes 3538952 | tf_op jit(solution)/shard_map/ppermute | solution.py:492
  79.2 7.4 %shard_map.93 = (f32[128,6144]{1,0:T(8,128)S(1)}, bf16[32,6144]{1,0:T(8,128)(2,1)S(1)}, bf16[32,6144]{1,0:T(8,128)(2,1)S(1)}, bf16[32,6144]{1,0:T(8,128)(2,1)S(1)}, bf16[32,6144]{1,0:T(8,128)(2,1)S(1)}) custom-call(bf16[256,1536]{1,0:T(8,128)(2,1)S(1)} %get-tuple-element.49.refs_0_.refs_5_, bf16[3072,1536]{1,0:T(8,128)(2,1)S(1)} %get-tuple-element.47.refs_7_.refs_1_, ...), custom_call_target="tpu_custom_call" | custom-call | flops 1000 | bytes 1000 | tf_op jit(solution)/shard_map/pallas_call | solution.py:55
  90.1 0.9 shard_map.94
  91.0 0.9 collective-permute-start.17
  92.0 11.4 %collective-permute-done.17.refs_1_.refs_6_ = bf16[32,6144]{1,0:T(8,128)(2,1)S(1)} collective-permute-done((bf16[32,6144]{1,0:T(8,128)(2,1)S(1)}, bf16[32,6144]{1,0:T(8,128)(2,1)S(1)}, u32[]{:S(2)}, u32[]{:S(2)}) %collective-permute-start.17) | collective-permute-done | bytes 393248 | tf_op jit(solution)/shard_map/ppermute | solution.py:561
  103.5 2.3 %collective-permute-done.19.refs_0_ = bf16[384,1536]{1,0:T(8,128)(2,1)S(1)} collective-permute-done((bf16[384,1536]{1,0:T(8,128)(2,1)S(1)}, bf16[384,1536]{1,0:T(8,128)(2,1)S(1)}, u32[]{:S(2)}, u32[]{:S(2)}) %collective-permute-start.19) | collective-permute-done | bytes 1179680 | tf_op jit(solution)/shard_map/ppermute | solution.py:492
  106.5 1.7 %collective-permute-start.27 = (bf16[256,1536]{1,0:T(8,128)(2,1)S(1)}, bf16[256,1536]{1,0:T(8,128)(2,1)S(1)}, u32[]{:S(2)}, u32[]{:S(2)}) collective-permute-start(bf16[256,1536]{1,0:T(8,128)(2,1)S(1)} %get-tuple-element.49.refs_0_.refs_5_), channel_id=1, source_target_pairs={{0,8},{4,12},{8,0},{12,4},{1,9},{5,13},{9,1},{13,5},{2,10},{6,14},... | collective-permute-start | bytes 2359304 | tf_op jit(solution)/shard_map/ppermute | solution.py:492
  108.9 1.3 collective-permute-start.18
  110.2 0.9 collective-permute-done.22.refs_8_
  111.1 8.7 %shard_map.99 = (f32[8,128]{1,0:T(8,128)S(1)}, bf16[3072,1536]{1,0:T(8,128)(2,1)}) custom-call(bf16[256,3072]{1,0:T(8,128)(2,1)S(1)} %get-tuple-element.41.refs_0_.refs_6_, bf16[64,3072]{1,0:T(8,128)(2,1)S(1)} %collective-permute-done.9.refs_3_.refs_1_, bf16[64,3072]{1,0:T(8,128)(2,1)S(1)} %collective-permute-done.10.refs_4_.refs_2_, ...), custom_call_target="tpu_custom_call" | custom-call | flops 1000 | bytes 1000 | tf_op jit(solution)/shard_map/pallas_call | solution.py:55
  120.6 1.5 %collective-permute-start.24 = (f32[1,6144]{1,0:T(1,128)S(1)}, f32[1,6144]{1,0:T(1,128)S(1)}, u32[]{:S(2)}, u32[]{:S(2)}) collective-permute-start(f32[1,6144]{1,0:T(1,128)S(1)} %shard_map.100.refs_0_), channel_id=1, source_target_pairs={{0,2},{1,3},{2,0},{3,1},{4,6},{5,7},{6,4},{7,5},{8,10},{9,11},{10,... | collective-permute-start | bytes 73736 | tf_op jit(solution)/shard_map/ppermute | solution.py:492
  122.2 6.1 %collective-permute-done.23.refs_1_ = f32[1,6144]{1,0:T(1,128)S(1)} collective-permute-done((f32[1,6144]{1,0:T(1,128)S(1)}, f32[1,6144]{1,0:T(1,128)S(1)}, u32[]{:S(2)}, u32[]{:S(2)}) %collective-permute-start.23) | collective-permute-done | bytes 24608 | tf_op jit(solution)/shard_map/ppermute | solution.py:492
  128.2 2.7 %collective-permute-start.25 = (f32[1,6144]{1,0:T(1,128)S(1)}, f32[1,6144]{1,0:T(1,128)S(1)}, u32[]{:S(2)}, u32[]{:S(2)}) collective-permute-start(f32[1,6144]{1,0:T(1,128)S(1)} %shard_map.100.refs_0_), channel_id=1, source_target_pairs={{0,3},{1,2},{2,1},{3,0},{4,7},{5,6},{6,5},{7,4},{8,11},{9,10},{10,... | collective-permute-start | bytes 73736 | tf_op jit(solution)/shard_map/ppermute | solution.py:492
  131.0 2.9 %collective-permute-done.25.refs_3_ = f32[1,6144]{1,0:T(1,128)S(1)} collective-permute-done((f32[1,6144]{1,0:T(1,128)S(1)}, f32[1,6144]{1,0:T(1,128)S(1)}, u32[]{:S(2)}, u32[]{:S(2)}) %collective-permute-start.25) | collective-permute-done | bytes 24608 | tf_op jit(solution)/shard_map/ppermute | solution.py:492
  133.9 1.0 shard_map.102.refs_1_
  135.0 1.6 %collective-permute-start.26 = (bf16[32,6144]{1,0:T(8,128)(2,1)S(1)}, bf16[32,6144]{1,0:T(8,128)(2,1)S(1)}, u32[]{:S(2)}, u32[]{:S(2)}) collective-permute-start(bf16[32,6144]{1,0:T(8,128)(2,1)S(1)} %shard_map.102.refs_1_), channel_id=1, source_target_pairs={{16,0},{0,16},{17,1},{1,17},{18,2},{2,18},{19,3},{3,19},{20,4},{4,... | collective-permute-start | bytes 1179656 | tf_op jit(solution)/shard_map/ppermute | solution.py:599
  137.1 1.4 collective-permute-start.31
  138.5 8.8 %shard_map.105 = (f32[8,128]{1,0:T(8,128)S(1)}, bf16[1536,3072]{1,0:T(8,128)(2,1)}) custom-call(bf16[256,3072]{1,0:T(8,128)(2,1)S(1)} %get-tuple-element.41.refs_0_.refs_6_, bf16[64,3072]{1,0:T(8,128)(2,1)S(1)} %collective-permute-done.7.refs_1_, bf16[64,3072]{1,0:T(8,128)(2,1)S(1)} %collective-permute-done.8.refs_2_, ...), custom_call_target="tpu_custom_call" | custom-call | flops 1000 | bytes 1000 | tf_op jit(solution)/shard_map/pallas_call | solution.py:55
  (64 shorter events, 12.4 us)
Async XLA Ops:
  3.2 23.8 %collective-permute-start.2 = (bf16[64,6144]{1,0:T(8,128)(2,1)}, bf16[64,6144]{1,0:T(8,128)(2,1)S(1)}, u32[]{:S(2)}, u32[]{:S(2)}) collective-permute-start(bf16[64,6144]{1,0:T(8,128)(2,1)} %get-tuple-element.35.refs_0_), channel_id=1, source_target_pairs={{0,3},{1,2},{2,1},{3,0},{4,7},{5,6},{6,5},{7,4},{8,11},{9,10},{10,... | collective-permute-start | bytes 2359304 | tf_op jit(solution)/shard_map/ppermute | solution.py:492
  8.3 35.5 %collective-permute-start.1 = (bf16[64,6144]{1,0:T(8,128)(2,1)}, bf16[64,6144]{1,0:T(8,128)(2,1)S(1)}, u32[]{:S(2)}, u32[]{:S(2)}) collective-permute-start(bf16[64,6144]{1,0:T(8,128)(2,1)} %get-tuple-element.35.refs_0_), channel_id=1, source_target_pairs={{0,1},{1,0},{2,3},{3,2},{4,5},{5,4},{6,7},{7,6},{8,9},{9,8},{10,11... | collective-permute-start | bytes 2359304 | tf_op jit(solution)/shard_map/ppermute | solution.py:492
  8.3 10.8 %collective-permute-start = (bf16[64,3072]{1,0:T(8,128)(2,1)}, bf16[64,3072]{1,0:T(8,128)(2,1)S(1)}, u32[]{:S(2)}, u32[]{:S(2)}) collective-permute-start(bf16[64,3072]{1,0:T(8,128)(2,1)} %get-tuple-element.36), channel_id=1, source_target_pairs={{0,8},{4,12},{8,0},{12,4},{1,9},{5,13},{9,1},{13,5},{2,10},{6,14},... | collective-permute-start | bytes 1179656 | tf_op jit(solution)/shard_map/ppermute | solution.py:492
  27.1 24.4 %collective-permute-start.4 = (bf16[64,3072]{1,0:T(8,128)(2,1)S(1)}, bf16[64,3072]{1,0:T(8,128)(2,1)S(1)}, u32[]{:S(2)}, u32[]{:S(2)}) collective-permute-start(bf16[64,3072]{1,0:T(8,128)(2,1)S(1)} %get-tuple-element.38), channel_id=1, source_target_pairs={{0,2},{3,1},{2,3},{1,0},{4,6},{7,5},{6,7},{5,4},{8,10},{11,9},{10,... | collective-permute-start | bytes 1179656 | tf_op jit(solution)/shard_map/ppermute | solution.py:534
  43.8 10.3 %collective-permute-start.5 = (bf16[64,3072]{1,0:T(8,128)(2,1)S(1)}, bf16[64,3072]{1,0:T(8,128)(2,1)S(1)}, u32[]{:S(2)}, u32[]{:S(2)}) collective-permute-start(bf16[64,3072]{1,0:T(8,128)(2,1)S(1)} %shard_map.87), channel_id=1, source_target_pairs={{0,8},{4,12},{8,0},{12,4},{1,9},{5,13},{9,1},{13,5},{2,10},{6,14},... | collective-permute-start | bytes 1179656 | tf_op jit(solution)/shard_map/ppermute | solution.py:492
  54.3 3.5 %collective-permute-start.6 = (bf16[256,3072]{1,0:T(8,128)(2,1)S(1)}, bf16[256,3072]{1,0:T(8,128)(2,1)S(1)}, u32[]{:S(2)}, u32[]{:S(2)}) collective-permute-start(bf16[256,3072]{1,0:T(8,128)(2,1)S(1)} %get-tuple-element.39.refs_0_.refs_5_), channel_id=1, source_target_pairs={{0,4},{4,0},{8,12},{12,8},{1,5},{5,1},{9,13},{13,9},{2,6},{6,2},{1... | collective-permute-start | bytes 4718600 | tf_op jit(solution)/shard_map/ppermute | solution.py:492
  54.4 12.9 %collective-permute-start.3 = (bf16[64,3072]{1,0:T(8,128)(2,1)S(1)}, bf16[64,3072]{1,0:T(8,128)(2,1)S(1)}, u32[]{:S(2)}, u32[]{:S(2)}) collective-permute-start(bf16[64,3072]{1,0:T(8,128)(2,1)S(1)} %get-tuple-element.37), channel_id=1, source_target_pairs={{0,2},{3,1},{2,3},{1,0},{4,6},{7,5},{6,7},{5,4},{8,10},{11,9},{10,... | collective-permute-start | bytes 1179656 | tf_op jit(solution)/shard_map/ppermute | solution.py:535
  54.9 13.6 %collective-permute-start.11 = (bf16[64,3072]{1,0:T(8,128)(2,1)S(1)}, bf16[64,3072]{1,0:T(8,128)(2,1)S(1)}, u32[]{:S(2)}, u32[]{:S(2)}) collective-permute-start(bf16[64,3072]{1,0:T(8,128)(2,1)S(1)} %get-tuple-element.48), channel_id=1, source_target_pairs={{0,8},{4,12},{8,0},{12,4},{1,9},{5,13},{9,1},{13,5},{2,10},{6,14},... | collective-permute-start | bytes 1179656 | tf_op jit(solution)/shard_map/ppermute | solution.py:492
  67.5 1.8 %collective-permute-start.10 = (bf16[64,3072]{1,0:T(8,128)(2,1)S(1)}, bf16[64,3072]{1,0:T(8,128)(2,1)S(1)}, u32[]{:S(2)}, u32[]{:S(2)}) collective-permute-start(bf16[64,3072]{1,0:T(8,128)(2,1)S(1)} %get-tuple-element.45), channel_id=1, source_target_pairs={{0,4},{4,0},{8,12},{12,8},{1,5},{5,1},{9,13},{13,9},{2,6},{6,2},{1... | collective-permute-start | bytes 1179656 | tf_op jit(solution)/shard_map/ppermute | solution.py:492
  67.5 2.3 %collective-permute-start.7 = (bf16[64,3072]{1,0:T(8,128)(2,1)S(1)}, bf16[64,3072]{1,0:T(8,128)(2,1)S(1)}, u32[]{:S(2)}, u32[]{:S(2)}) collective-permute-start(bf16[64,3072]{1,0:T(8,128)(2,1)S(1)} %get-tuple-element.42), channel_id=1, source_target_pairs={{0,4},{4,0},{8,12},{12,8},{1,5},{5,1},{9,13},{13,9},{2,6},{6,2},{1... | collective-permute-start | bytes 1179656 | tf_op jit(solution)/shard_map/ppermute | solution.py:492
  68.0 2.3 %collective-permute-start.8 = (bf16[64,3072]{1,0:T(8,128)(2,1)S(1)}, bf16[64,3072]{1,0:T(8,128)(2,1)S(1)}, u32[]{:S(2)}, u32[]{:S(2)}) collective-permute-start(bf16[64,3072]{1,0:T(8,128)(2,1)S(1)} %get-tuple-element.43), channel_id=1, source_target_pairs={{0,4},{4,0},{8,12},{12,8},{1,5},{5,1},{9,13},{13,9},{2,6},{6,2},{1... | collective-permute-start | bytes 1179656 | tf_op jit(solution)/shard_map/ppermute | solution.py:492
  68.1 2.8 %collective-permute-start.9 = (bf16[64,3072]{1,0:T(8,128)(2,1)S(1)}, bf16[64,3072]{1,0:T(8,128)(2,1)S(1)}, u32[]{:S(2)}, u32[]{:S(2)}) collective-permute-start(bf16[64,3072]{1,0:T(8,128)(2,1)S(1)} %get-tuple-element.44), channel_id=1, source_target_pairs={{0,4},{4,0},{8,12},{12,8},{1,5},{5,1},{9,13},{13,9},{2,6},{6,2},{1... | collective-permute-start | bytes 1179656 | tf_op jit(solution)/shard_map/ppermute | solution.py:492
  77.7 28.1 %collective-permute-start.19 = (bf16[384,1536]{1,0:T(8,128)(2,1)S(1)}, bf16[384,1536]{1,0:T(8,128)(2,1)S(1)}, u32[]{:S(2)}, u32[]{:S(2)}) collective-permute-start(bf16[384,1536]{1,0:T(8,128)(2,1)S(1)} %get-tuple-element.60.refs_5_), channel_id=1, source_target_pairs={{0,8},{4,12},{8,0},{12,4},{1,9},{5,13},{9,1},{13,5},{2,10},{6,14},... | collective-permute-start | bytes 3538952 | tf_op jit(solution)/shard_map/ppermute | solution.py:492
  86.6 1.8 %collective-permute-start.12 = (bf16[32,6144]{1,0:T(8,128)(2,1)S(1)}, bf16[32,6144]{1,0:T(8,128)(2,1)S(1)}, u32[]{:S(2)}, u32[]{:S(2)}) collective-permute-start(bf16[32,6144]{1,0:T(8,128)(2,1)S(1)} %get-tuple-element.51), channel_id=1, source_target_pairs={{0,4},{4,0},{8,12},{12,8},{1,5},{5,1},{9,13},{13,9},{2,6},{6,2},{1... | collective-permute-start | bytes 1179656 | tf_op jit(solution)/shard_map/ppermute | solution.py:492
  86.7 2.3 %collective-permute-start.13 = (bf16[32,6144]{1,0:T(8,128)(2,1)S(1)}, bf16[32,6144]{1,0:T(8,128)(2,1)S(1)}, u32[]{:S(2)}, u32[]{:S(2)}) collective-permute-start(bf16[32,6144]{1,0:T(8,128)(2,1)S(1)} %get-tuple-element.52), channel_id=1, source_target_pairs={{0,4},{4,0},{8,12},{12,8},{1,5},{5,1},{9,13},{13,9},{2,6},{6,2},{1... | collective-permute-start | bytes 1179656 | tf_op jit(solution)/shard_map/ppermute | solution.py:492
  87.2 2.3 %collective-permute-start.14 = (bf16[32,6144]{1,0:T(8,128)(2,1)S(1)}, bf16[32,6144]{1,0:T(8,128)(2,1)S(1)}, u32[]{:S(2)}, u32[]{:S(2)}) collective-permute-start(bf16[32,6144]{1,0:T(8,128)(2,1)S(1)} %get-tuple-element.53), channel_id=1, source_target_pairs={{0,4},{4,0},{8,12},{12,8},{1,5},{5,1},{9,13},{13,9},{2,6},{6,2},{1... | collective-permute-start | bytes 1179656 | tf_op jit(solution)/shard_map/ppermute | solution.py:492
  87.3 2.8 %collective-permute-start.15 = (bf16[32,6144]{1,0:T(8,128)(2,1)S(1)}, bf16[32,6144]{1,0:T(8,128)(2,1)S(1)}, u32[]{:S(2)}, u32[]{:S(2)}) collective-permute-start(bf16[32,6144]{1,0:T(8,128)(2,1)S(1)} %get-tuple-element.54), channel_id=1, source_target_pairs={{0,4},{4,0},{8,12},{12,8},{1,5},{5,1},{9,13},{13,9},{2,6},{6,2},{1... | collective-permute-start | bytes 1179656 | tf_op jit(solution)/shard_map/ppermute | solution.py:492
  91.0 12.3 %collective-permute-start.17 = (bf16[32,6144]{1,0:T(8,128)(2,1)S(1)}, bf16[32,6144]{1,0:T(8,128)(2,1)S(1)}, u32[]{:S(2)}, u32[]{:S(2)}) collective-permute-start(bf16[32,6144]{1,0:T(8,128)(2,1)S(1)} %get-tuple-element.58), channel_id=1, source_target_pairs={{2,0},{1,3},{3,2},{0,1},{6,4},{5,7},{7,6},{4,5},{10,8},{9,11},{11,... | collective-permute-start | bytes 1179656 | tf_op jit(solution)/shard_map/ppermute | solution.py:561
  92.0 16.9 %collective-permute-start.21 = (bf16[512,1536]{1,0:T(8,128)(2,1)S(1)}, bf16[512,1536]{1,0:T(8,128)(2,1)S(1)}, u32[]{:S(2)}, u32[]{:S(2)}) collective-permute-start(bf16[512,1536]{1,0:T(8,128)(2,1)S(1)} %get-tuple-element.61), channel_id=1, source_target_pairs={{0,4},{4,0},{8,12},{12,8},{1,5},{5,1},{9,13},{13,9},{2,6},{6,2},{1... | collective-permute-start | bytes 4718600 | tf_op jit(solution)/shard_map/ppermute | solution.py:492
  105.9 5.2 %collective-permute-start.20 = (bf16[256,3072]{1,0:T(8,128)(2,1)S(1)}, bf16[256,3072]{1,0:T(8,128)(2,1)S(1)}, u32[]{:S(2)}, u32[]{:S(2)}) collective-permute-start(bf16[256,3072]{1,0:T(8,128)(2,1)S(1)} %shard_map.98.refs_3_), channel_id=1, source_target_pairs={{0,4},{4,0},{8,12},{12,8},{1,5},{5,1},{9,13},{13,9},{2,6},{6,2},{1... | collective-permute-start | bytes 4718600 | tf_op jit(solution)/shard_map/ppermute | solution.py:492
  106.0 5.1 %collective-permute-start.22 = (bf16[384,1536]{1,0:T(8,128)(2,1)S(1)}, bf16[384,1536]{1,0:T(8,128)(2,1)S(1)}, u32[]{:S(2)}, u32[]{:S(2)}) collective-permute-start(bf16[384,1536]{1,0:T(8,128)(2,1)S(1)} %shard_map.97.refs_3_.refs_7_), channel_id=1, source_target_pairs={{0,4},{4,0},{8,12},{12,8},{1,5},{5,1},{9,13},{13,9},{2,6},{6,2},{1... | collective-permute-start | bytes 3538952 | tf_op jit(solution)/shard_map/ppermute | solution.py:492
  106.5 28.4 %collective-permute-start.27 = (bf16[256,1536]{1,0:T(8,128)(2,1)S(1)}, bf16[256,1536]{1,0:T(8,128)(2,1)S(1)}, u32[]{:S(2)}, u32[]{:S(2)}) collective-permute-start(bf16[256,1536]{1,0:T(8,128)(2,1)S(1)} %get-tuple-element.49.refs_0_.refs_5_), channel_id=1, source_target_pairs={{0,8},{4,12},{8,0},{12,4},{1,9},{5,13},{9,1},{13,5},{2,10},{6,14},... | collective-permute-start | bytes 2359304 | tf_op jit(solution)/shard_map/ppermute | solution.py:492
  108.2 25.7 %collective-permute-start.16 = (bf16[32,6144]{1,0:T(8,128)(2,1)S(1)}, bf16[32,6144]{1,0:T(8,128)(2,1)S(1)}, u32[]{:S(2)}, u32[]{:S(2)}) collective-permute-start(bf16[32,6144]{1,0:T(8,128)(2,1)S(1)} %get-tuple-element.56), channel_id=1, source_target_pairs={{0,1},{1,0},{2,3},{3,2},{4,5},{5,4},{6,7},{7,6},{8,9},{9,8},{10,11... | collective-permute-start | bytes 1179656 | tf_op jit(solution)/shard_map/ppermute | solution.py:492
  108.9 25.0 %collective-permute-start.18 = (bf16[32,6144]{1,0:T(8,128)(2,1)S(1)}, bf16[32,6144]{1,0:T(8,128)(2,1)S(1)}, u32[]{:S(2)}, u32[]{:S(2)}) collective-permute-start(bf16[32,6144]{1,0:T(8,128)(2,1)S(1)} %shard_map.95.refs_1_), channel_id=1, source_target_pairs={{0,3},{1,2},{2,1},{3,0},{4,7},{5,6},{6,5},{7,4},{8,11},{9,10},{10,... | collective-permute-start | bytes 1179656 | tf_op jit(solution)/shard_map/ppermute | solution.py:492
  119.9 8.4 %collective-permute-start.23 = (f32[1,6144]{1,0:T(1,128)S(1)}, f32[1,6144]{1,0:T(1,128)S(1)}, u32[]{:S(2)}, u32[]{:S(2)}) collective-permute-start(f32[1,6144]{1,0:T(1,128)S(1)} %shard_map.100.refs_0_), channel_id=1, source_target_pairs={{0,1},{1,0},{2,3},{3,2},{4,5},{5,4},{6,7},{7,6},{8,9},{9,8},{10,11... | collective-permute-start | bytes 73736 | tf_op jit(solution)/shard_map/ppermute | solution.py:492
  120.6 10.4 %collective-permute-start.24 = (f32[1,6144]{1,0:T(1,128)S(1)}, f32[1,6144]{1,0:T(1,128)S(1)}, u32[]{:S(2)}, u32[]{:S(2)}) collective-permute-start(f32[1,6144]{1,0:T(1,128)S(1)} %shard_map.100.refs_0_), channel_id=1, source_target_pairs={{0,2},{1,3},{2,0},{3,1},{4,6},{5,7},{6,4},{7,5},{8,10},{9,11},{10,... | collective-permute-start | bytes 73736 | tf_op jit(solution)/shard_map/ppermute | solution.py:492
  128.2 5.6 %collective-permute-start.25 = (f32[1,6144]{1,0:T(1,128)S(1)}, f32[1,6144]{1,0:T(1,128)S(1)}, u32[]{:S(2)}, u32[]{:S(2)}) collective-permute-start(f32[1,6144]{1,0:T(1,128)S(1)} %shard_map.100.refs_0_), channel_id=1, source_target_pairs={{0,3},{1,2},{2,1},{3,0},{4,7},{5,6},{6,5},{7,4},{8,11},{9,10},{10,... | collective-permute-start | bytes 73736 | tf_op jit(solution)/shard_map/ppermute | solution.py:492
  135.0 3.5 %collective-permute-start.28 = (bf16[256,1536]{1,0:T(8,128)(2,1)S(1)}, bf16[256,1536]{1,0:T(8,128)(2,1)S(1)}, u32[]{:S(2)}, u32[]{:S(2)}) collective-permute-start(bf16[256,1536]{1,0:T(8,128)(2,1)S(1)} %shard_map.103.refs_7_), channel_id=1, source_target_pairs={{0,4},{4,0},{8,12},{12,8},{1,5},{5,1},{9,13},{13,9},{2,6},{6,2},{1... | collective-permute-start | bytes 2359304 | tf_op jit(solution)/shard_map/ppermute | solution.py:492
  135.0 12.2 %collective-permute-start.26 = (bf16[32,6144]{1,0:T(8,128)(2,1)S(1)}, bf16[32,6144]{1,0:T(8,128)(2,1)S(1)}, u32[]{:S(2)}, u32[]{:S(2)}) collective-permute-start(bf16[32,6144]{1,0:T(8,128)(2,1)S(1)} %shard_map.102.refs_1_), channel_id=1, source_target_pairs={{16,0},{0,16},{17,1},{1,17},{18,2},{2,18},{19,3},{3,19},{20,4},{4,... | collective-permute-start | bytes 1179656 | tf_op jit(solution)/shard_map/ppermute | solution.py:599
  136.6 11.4 %collective-permute-start.29 = (f32[1,6144]{1,0:T(1,128)S(1)}, f32[1,6144]{1,0:T(1,128)S(1)}, u32[]{:S(2)}, u32[]{:S(2)}) collective-permute-start(f32[1,6144]{1,0:T(1,128)S(1)} %shard_map.104.refs_9_.refs_0_), channel_id=1, source_target_pairs={{0,4},{4,0},{8,12},{12,8},{1,5},{5,1},{9,13},{13,9},{2,6},{6,2},{1... | collective-permute-start | bytes 73736 | tf_op jit(solution)/shard_map/ppermute | solution.py:492
  136.8 11.3 %collective-permute-start.30 = (f32[1,6144]{1,0:T(1,128)S(1)}, f32[1,6144]{1,0:T(1,128)S(1)}, u32[]{:S(2)}, u32[]{:S(2)}) collective-permute-start(f32[1,6144]{1,0:T(1,128)S(1)} %shard_map.104.refs_9_.refs_0_), channel_id=1, source_target_pairs={{0,8},{4,12},{8,0},{12,4},{1,9},{5,13},{9,1},{13,5},{2,10},{6,14},... | collective-permute-start | bytes 73736 | tf_op jit(solution)/shard_map/ppermute | solution.py:492
  137.1 10.9 %collective-permute-start.31 = (f32[1,6144]{1,0:T(1,128)S(1)}, f32[1,6144]{1,0:T(1,128)S(1)}, u32[]{:S(2)}, u32[]{:S(2)}) collective-permute-start(f32[1,6144]{1,0:T(1,128)S(1)} %shard_map.104.refs_9_.refs_0_), channel_id=1, source_target_pairs={{0,12},{4,8},{8,4},{12,0},{1,13},{5,9},{9,5},{13,1},{2,14},{6,10},... | collective-permute-start | bytes 73736 | tf_op jit(solution)/shard_map/ppermute | solution.py:492
  (4 other events, 59.4 us)
